TPU v7x, 512 devices: a whole 4x4x16 slice. The times are simulated.
512 devices in a mesh: dp: 64 (over z_hi, y, x, core), tensor: 8 (over z_lo).
Axes of the slice: x: 4, y: 4, z: 16 (z_hi: 2, z_lo: 8; z = z_hi * 8 + z_lo), core: 2. Of those that a mesh axis runs over, the one named last changes fastest.
Arguments:
- queries: bfloat16 [8192, 8192], P('dp', 'tensor'), may hold values from -32 to 32
- key_value_store: bfloat16 [128, 1600, 2048], P('dp', 'tensor'), may hold values from -24 to 24
- output_gradient: bfloat16 [8192, 8192], P('dp', 'tensor'), may hold values from -6 to 6
- image_ids: int32 [64, 4], replicated, may hold values from 0 to 127, as said below
- image_counts: int32 [64], replicated, may hold values from 0 to 4, as said below
- image_start: int32 [64, 4], replicated, may hold values from 0 to 128, as said below
Outputs:
- attended: bfloat16 [8192, 8192], P('dp', 'tensor')
- grad_queries: bfloat16 [8192, 8192], P('dp', 'tensor')
- grad_kv: bfloat16 [128, 1600, 2048], P('dp', 'tensor')
Inputs may be any that keep to these rules, and one draw needn't show every extreme that they name: `image_ids`: slot m of sample s names an image for m < image_counts[s]; every image is named by exactly one such slot. Device d of dp owns images d * 2 to (d + 1) * 2 - 1, and an image named by sample s is owned by device s or device (s + 1) modulo 64. Entries at or past a sample's count name some image and are unused. `image_counts`: the counts sum to 128; some sample has 4 images and some has none. `image_start`: within a sample the starts rise strictly with the slot; entries at or past the count are 128.
All inputs are finite; a program needn't handle non-finite values.
Results may differ from a plain program's by a relative error of at most 0.012.
Values may be sent and summed in bfloat16 or wider, within the bound.
No kernel may reach another device: no remote copies, remote signals or barrier semaphores. Data moves between devices by JAX's collectives and lax.ppermute only.
A program may use at most 64 MiB of HBM per device.

v0:
```python
import jax
import jax.numpy as jnp
from jax import lax
from jax.sharding import PartitionSpec as P

HEAD_DIM_SIZE = 128
IMG_DEV = 2


NEG_FILL = -1e30


def from_behind(value, axis, steps):
    count = lax.axis_size(axis)
    pairs = [(source, (source + steps) % count) for source in range(count)]
    return lax.ppermute(value, axis, pairs)


def split_pair(stored, group_index, head_size):
    base_col = group_index * 2 * head_size
    return (
        stored[:, base_col : base_col + head_size],
        stored[:, base_col + head_size : base_col + 2 * head_size],
    )


def score_block(query_blk, key_matrix_rows, score_scale):
    return (
        jnp.einsum("thd,vd->thv", query_blk, key_matrix_rows, preferred_element_type=jnp.float32)
        * score_scale
    )


def block_stats(scores, visible):
    row_top = jnp.max(jnp.where(visible, scores, NEG_FILL), axis=2)
    row_total = jnp.sum(jnp.where(visible, jnp.exp(scores - row_top[..., None]), 0.0), axis=2)
    return (row_top, row_total)


def merge_stats(top_first, total_first, top_second, total_second):
    row_top = jnp.maximum(top_first, top_second)
    return (
        row_top,
        total_first * jnp.exp(top_first - row_top) + total_second * jnp.exp(top_second - row_top),
    )


def finish_stats(row_top, row_total):
    return jnp.where(row_total > 0.0, row_top + jnp.log(jnp.maximum(row_total, 1.0)), 0.0)


def out_block(query_blk, key_matrix_rows, value_matrix_rows, visible, log_total, score_scale):
    scores = score_block(query_blk, key_matrix_rows, score_scale)
    weights_half = jnp.where(visible, jnp.exp(scores - log_total[..., None]), 0.0).astype(
        jnp.bfloat16
    )
    return jnp.einsum(
        "thv,vd->thd", weights_half, value_matrix_rows, preferred_element_type=jnp.float32
    )


def grad_block(
    query_blk,
    cot_blk,
    key_matrix_rows,
    value_matrix_rows,
    visible,
    log_total,
    delta_row,
    score_scale,
):
    scores = score_block(query_blk, key_matrix_rows, score_scale)
    weights = jnp.where(visible, jnp.exp(scores - log_total[..., None]), 0.0)
    weights_half = weights.astype(jnp.bfloat16)
    dweights = jnp.einsum(
        "thd,vd->thv", cot_blk, value_matrix_rows, preferred_element_type=jnp.float32
    )
    dscores = (weights * (dweights - delta_row[..., None])).astype(jnp.bfloat16)
    dquery = (
        jnp.einsum("thv,vd->thd", dscores, key_matrix_rows, preferred_element_type=jnp.float32)
        * score_scale
    )
    dkey_rows = (
        jnp.einsum("thv,thd->vd", dscores, query_blk, preferred_element_type=jnp.float32)
        * score_scale
    )
    dvalue_rows = jnp.einsum(
        "thv,thd->vd", weights_half, cot_blk, preferred_element_type=jnp.float32
    )
    return (dquery, jnp.concatenate([dkey_rows, dvalue_rows], axis=1))


def local(queries, key_value_store, output_gradient, image_ids, image_counts, image_start):
    score_scale = HEAD_DIM_SIZE ** (-0.5)
    kv_heads = lax.all_to_all(key_value_store, "tensor", split_axis=2, concat_axis=1, tiled=True)
    tok_rows = queries.shape[0]
    heads_dev = queries.shape[1] // HEAD_DIM_SIZE
    kv_dev = kv_heads.shape[2] // (2 * HEAD_DIM_SIZE)
    vis_rows = kv_heads.shape[1]
    group_width = heads_dev // kv_dev
    head_block = min(group_width, max(1, 512 // tok_rows))
    unit_list = [
        (group_index, group_index * group_width + block_index * head_block)
        for group_index in range(kv_dev)
        for block_index in range(group_width // head_block)
    ]
    query3 = queries.reshape(tok_rows, heads_dev, HEAD_DIM_SIZE)
    cot3 = output_gradient.reshape(tok_rows, heads_dev, HEAD_DIM_SIZE)
    positions = jnp.arange(tok_rows, dtype=jnp.int32)
    sample_index = lax.axis_index("dp")
    dp_count = lax.axis_size("dp")
    neighbour = from_behind(kv_heads, "dp", -1)
    pooled = jnp.concatenate([kv_heads, neighbour], axis=0)
    slot_count = image_counts[sample_index]
    row_ids = image_ids[sample_index]
    row_starts = image_start[sample_index]

    def fetch_slot(slot_num):
        image_index = row_ids[slot_num]
        pool_slot = (
            image_index // IMG_DEV - sample_index
        ) % dp_count * IMG_DEV + image_index % IMG_DEV
        visible = (positions >= row_starts[slot_num])[:, None, None]
        return (pool_slot, lax.dynamic_index_in_dim(pooled, pool_slot, 0, keepdims=False), visible)

    log_parts = []
    out_parts = []
    for group_index, head_lo in unit_list:
        query_blk = query3[:, head_lo : head_lo + head_block]

        def stat_step(slot_num, state):
            _, stored, visible = fetch_slot(slot_num)
            key_matrix_rows, _ = split_pair(stored, group_index, HEAD_DIM_SIZE)
            row_top, row_total = block_stats(
                score_block(query_blk, key_matrix_rows, score_scale), visible
            )
            return merge_stats(state[0], state[1], row_top, row_total)

        initial_state = (
            jnp.full((tok_rows, head_block), NEG_FILL, jnp.float32),
            jnp.zeros((tok_rows, head_block), jnp.float32),
        )
        row_top, row_total = lax.fori_loop(0, slot_count, stat_step, initial_state)
        log_total = finish_stats(row_top, row_total)

        def out_step(slot_num, accum):
            _, stored, visible = fetch_slot(slot_num)
            key_matrix_rows, value_matrix_rows = split_pair(stored, group_index, HEAD_DIM_SIZE)
            return accum + out_block(
                query_blk, key_matrix_rows, value_matrix_rows, visible, log_total, score_scale
            )

        out_parts.append(
            lax.fori_loop(
                0,
                slot_count,
                out_step,
                jnp.zeros((tok_rows, head_block, HEAD_DIM_SIZE), jnp.float32),
            )
        )
        log_parts.append(log_total)
    attended3 = jnp.concatenate(out_parts, axis=1).astype(jnp.bfloat16)
    delta_all = jnp.sum(cot3.astype(jnp.float32) * attended3.astype(jnp.float32), axis=2)
    grad_pool = jnp.zeros((2 * IMG_DEV, vis_rows, kv_dev * 2 * HEAD_DIM_SIZE), jnp.float32)
    dq_parts = []
    for unit_num, (group_index, head_lo) in enumerate(unit_list):
        query_blk = query3[:, head_lo : head_lo + head_block]
        cot_blk = cot3[:, head_lo : head_lo + head_block]
        log_total = log_parts[unit_num]
        delta_row = delta_all[:, head_lo : head_lo + head_block]

        def back_step(slot_num, state):
            dq_accum, pool_accum = state
            pool_slot, stored, visible = fetch_slot(slot_num)
            key_matrix_rows, value_matrix_rows = split_pair(stored, group_index, HEAD_DIM_SIZE)
            dquery, dkv_rows = grad_block(
                query_blk,
                cot_blk,
                key_matrix_rows,
                value_matrix_rows,
                visible,
                log_total,
                delta_row,
                score_scale,
            )
            corner = (pool_slot, 0, group_index * 2 * HEAD_DIM_SIZE)
            current = lax.dynamic_slice(pool_accum, corner, (1, vis_rows, 2 * HEAD_DIM_SIZE))
            pool_accum = lax.dynamic_update_slice(pool_accum, current + dkv_rows[None], corner)
            return (dq_accum + dquery, pool_accum)

        dq_blk, grad_pool = lax.fori_loop(
            0,
            slot_count,
            back_step,
            (jnp.zeros((tok_rows, head_block, HEAD_DIM_SIZE), jnp.float32), grad_pool),
        )
        dq_parts.append(dq_blk)
    dq_whole = jnp.concatenate(dq_parts, axis=1)
    grad_half = grad_pool.astype(jnp.bfloat16)
    returned = from_behind(grad_half[IMG_DEV:], "dp", 1)
    grad_own = grad_half[:IMG_DEV] + returned
    attended = attended3.reshape(tok_rows, heads_dev * HEAD_DIM_SIZE)
    grad_queries = dq_whole.reshape(tok_rows, heads_dev * HEAD_DIM_SIZE).astype(jnp.bfloat16)
    grad_kv = lax.all_to_all(grad_own, "tensor", split_axis=1, concat_axis=2, tiled=True)
    return (attended, grad_queries, grad_kv)


def solution(mesh):
    return jax.shard_map(
        local,
        mesh=mesh,
        in_specs=(P("dp", "tensor"), P("dp", "tensor", None), P("dp", "tensor"), P(), P(), P()),
        out_specs=(P("dp", "tensor"), P("dp", "tensor"), P("dp", "tensor", None)),
        check_vma=False,
    )
```

profile of v0, /device:TPU:1, one launch (start us, length us, event | category | flops | bytes accessed | tf_op | source)
XLA Modules:
  0.0 532.8 jit_solution(5319841438199330682)
XLA Ops:
  0.6 6.1 %copy.31 = bf16[2,200,2048]{1,0,2:T(2,128)(2,1)} copy(bf16[2,200,2048]{2,1,0:T(8,128)(2,1)} %param.19) | data formatting | bytes 3276800 | tf_op args[1]
  6.7 0.0 copy-start.9
  6.7 0.0 copy-start.10
  6.7 108.5 %all_to_all.36 = bf16[2,200,2048]{1,0,2:T(2,128)(2,1)S(1)} all-to-all(bf16[2,200,2048]{1,0,2:T(2,128)(2,1)} %copy.31), channel_id=1, replica_groups=mesh['dp'=64,'tensor'=8] {'tensor'}, dimensions={2} | all-to-all | bytes 3276800 | tf_op jit(solution)/shard_map/all_to_all | solution.py:95
  115.2 0.0 copy-start.14
  115.2 0.0 copy-start.11
  115.2 0.0 copy-start.12
  115.2 3.6 copy.32
  118.8 3.7 collective-permute-start
  122.6 0.0 copy-done.9
  122.6 0.2 copy.40
  122.7 0.0 copy-done.10
  122.8 0.0 copy-start.8
  122.8 0.2 copy.33
  123.0 0.8 copy.35
  123.7 0.1 copy.37
  123.9 0.0 copy-done.8
  123.9 0.1 copy.44
  124.0 0.8 copy.42
  124.8 0.0 copy-done.14
  124.8 0.6 dynamic_slice.150
  125.4 0.0 copy-done.11
  125.4 0.0 copy-done.12
  125.4 0.8 dynamic-slice_reduce_fusion
  126.1 16.6 %collective-permute-done = bf16[2,1600,256]{2,1,0:T(8,128)(2,1)} collective-permute-done((bf16[2,1600,256]{2,1,0:T(8,128)(2,1)}, bf16[2,1600,256]{2,1,0:T(8,128)(2,1)}, u32[]{:S(2)}, u32[]{:S(2)}) %collective-permute-start) | collective-permute-done | bytes 1638432 | tf_op jit(solution)/shard_map/ppermute | solution.py:16
  142.8 2.2 pad_maximum_fusion
  145.0 0.6 while.92
  145.6 0.0 copy-start.13
  145.6 0.6 copy-done.13
  146.1 0.7 broadcast.200.clone.1
  146.9 0.6 while.93
  147.4 1.7 copy.38
  149.1 0.6 while.94
  149.7 0.7 broadcast.200.clone
  150.4 0.6 while.95
  151.0 1.7 copy.39
  152.7 1.8 multiply_reduce_fusion
  154.5 0.7 broadcast.200.clone.2
  155.2 3.3 broadcast_in_dim.160
  158.5 0.6 while.96
  159.1 0.7 broadcast.200
  159.8 0.7 while.97
  160.5 11.8 %copy.52 = bf16[4,1600,256]{2,0,1:T(4,128)(2,1)S(1)} copy(f32[4,1600,256]{2,1,0:T(8,128)} %get-tuple-element.1102) | data formatting | bytes 9830400 | tf_op jit(solution)/shard_map/while | solution.py:191
  172.4 1.8 slice.129
  174.2 0.0 copy-start.4
  174.2 257.9 %collective-permute-start.1 = (bf16[2,1600,256]{2,0,1:T(2,128)(2,1)S(1)}, bf16[2,1600,256]{2,0,1:T(2,128)(2,1)S(1)}, u32[]{:S(2)}, u32[]{:S(2)}) collective-permute-start(bf16[2,1600,256]{2,0,1:T(2,128)(2,1)S(1)} %slice.129), channel_id=1, source_target_pairs={{0,8},{8,16},{16,24},{24,32},{32,40},{40,48},{48,56},{56,64},{64,7... | collective-permute-start | bytes 4915208 | tf_op jit(solution)/shard_map/ppermute | solution.py:16
  432.1 18.0 %collective-permute-done.1 = bf16[2,1600,256]{2,0,1:T(2,128)(2,1)S(1)} collective-permute-done((bf16[2,1600,256]{2,0,1:T(2,128)(2,1)S(1)}, bf16[2,1600,256]{2,0,1:T(2,128)(2,1)S(1)}, u32[]{:S(2)}, u32[]{:S(2)}) %collective-permute-start.1) | collective-permute-done | bytes 1638432 | tf_op jit(solution)/shard_map/ppermute | solution.py:16
  450.1 2.8 slice_add_fusion
  452.9 0.0 copy-start.7
  452.9 4.1 all-to-all-start.1
  457.1 1.8 copy.48
  458.8 0.0 copy-done.4
  458.9 0.0 copy-done.7
  458.9 0.7 copy_bitcast_fusion
  459.7 70.9 %all-to-all-done.1 = bf16[2,1600,256]{2,0,1:T(2,128)(2,1)S(1)} async-done(((bf16[2,1600,256]{2,0,1:T(2,128)(2,1)}), bf16[2,1600,256]{2,0,1:T(2,128)(2,1)S(1)}, u32[]{:S(2)}, u32[]{:S(2)}) %all-to-all-start.1) | async-done | bytes 1638432 | tf_op jit(solution)/shard_map/all_to_all | solution.py:204
  530.6 0.5 copy.47
  531.1 1.7 all_to_all.33
  (11 shorter events, 0.1 us)
Async XLA Ops:
  6.7 115.9 %copy-start.9 = (bf16[128,1024]{1,0:T(8,128)(2,1)S(1)}, bf16[128,1024]{1,0:T(8,128)(2,1)}, u32[]{:S(2)}) copy-start(bf16[128,1024]{1,0:T(8,128)(2,1)} %param.20) | copy-start | bytes 786436
  6.7 116.0 %copy-start.10 = (bf16[128,1024]{1,0:T(8,128)(2,1)S(1)}, bf16[128,1024]{1,0:T(8,128)(2,1)}, u32[]{:S(2)}) copy-start(bf16[128,1024]{1,0:T(8,128)(2,1)} %param.18) | copy-start | bytes 786436
  115.2 9.6 %copy-start.14 = (s32[64]{0:T(128)S(1)}, s32[64]{0:T(128)}, u32[]{:S(2)}) copy-start(s32[64]{0:T(128)} %param.22) | copy-start | bytes 772
  115.2 10.1 %copy-start.11 = (s32[64,4]{0,1:T(4,128)S(1)}, s32[64,4]{0,1:T(4,128)}, u32[]{:S(2)}) copy-start(s32[64,4]{0,1:T(4,128)} %param.21) | copy-start | bytes 3076
  115.2 10.1 %copy-start.12 = (s32[64,4]{0,1:T(4,128)S(1)}, s32[64,4]{0,1:T(4,128)}, u32[]{:S(2)}) copy-start(s32[64,4]{0,1:T(4,128)} %param.23) | copy-start | bytes 3076
  118.8 23.9 %collective-permute-start = (bf16[2,1600,256]{2,1,0:T(8,128)(2,1)}, bf16[2,1600,256]{2,1,0:T(8,128)(2,1)}, u32[]{:S(2)}, u32[]{:S(2)}) collective-permute-start(bf16[2,1600,256]{2,1,0:T(8,128)(2,1)} %bitcast.260), channel_id=1, source_target_pairs={{0,504},{8,0},{16,8},{24,16},{32,24},{40,32},{48,40},{56,48},{64,5... | collective-permute-start | bytes 4915208 | tf_op jit(solution)/shard_map/ppermute | solution.py:16
  122.8 1.1 copy-start.8
  145.6 0.6 copy-start.13
  174.2 284.7 %copy-start.4 = (f32[128,4,128]{2,0,1:T(8,128)S(1)}, f32[128,4,128]{2,0,1:T(8,128)}, u32[]{:S(2)}) copy-start(f32[128,4,128]{2,0,1:T(8,128)} %get-tuple-element.1101) | copy-start | bytes 786436
  174.2 275.9 %collective-permute-start.1 = (bf16[2,1600,256]{2,0,1:T(2,128)(2,1)S(1)}, bf16[2,1600,256]{2,0,1:T(2,128)(2,1)S(1)}, u32[]{:S(2)}, u32[]{:S(2)}) collective-permute-start(bf16[2,1600,256]{2,0,1:T(2,128)(2,1)S(1)} %slice.129), channel_id=1, source_target_pairs={{0,8},{8,16},{16,24},{24,32},{32,40},{40,48},{48,56},{56,64},{64,7... | collective-permute-start | bytes 4915208 | tf_op jit(solution)/shard_map/ppermute | solution.py:16
  452.9 6.0 %copy-start.7 = (f32[128,4,128]{2,0,1:T(8,128)S(1)}, f32[128,4,128]{2,0,1:T(8,128)}, u32[]{:S(2)}) copy-start(f32[128,4,128]{2,0,1:T(8,128)} %get-tuple-element.1099) | copy-start | bytes 786436
  452.9 77.7 %all-to-all-start.1 = ((bf16[2,1600,256]{2,0,1:T(2,128)(2,1)}), bf16[2,1600,256]{2,0,1:T(2,128)(2,1)S(1)}, u32[]{:S(2)}, u32[]{:S(2)}) async-start(bf16[2,1600,256]{2,0,1:T(2,128)(2,1)} %slice_add_fusion), calls=%async_computation.1 | async-start | bytes 3276800 | tf_op jit(solution)/shard_map/all_to_all | solution.py:204
where the time goes:
time: 536 us; the launch traced here: 533 us
  starting transfers between devices  266 us (50%)
  blocking collectives  108 us (20%)
  waiting for transfers between devices  106 us (20%)
  local copies, waits for them, and re-layouts  41 us (8%)
  other arithmetic  7.58 us (1%)
    ppermute x2, starting transfers between devices, from_behind(): return lax.ppermute(value, axis, pairs)  262 us
    all_to_all x1, blocking collectives, local(): lax.all_to_all(key_value_store, 'tensor', split_axis=2, concat_axis=1, ti...  108 us
    all_to_all x1, waiting for transfers between devices, local(): lax.all_to_all(grad_own, 'tensor', split_axis=1, concat_axis=2, tiled=True)  70.9 us
    ppermute x2, waiting for transfers between devices, from_behind(): return lax.ppermute(value, axis, pairs)  34.7 us
    while x1, local copies, waits for them, and re-layouts, local(): lax.fori_loop(0, slot_count, back_step, (jnp.zeros((tok_rows, head_block,...  11.8 us
  transfers between devices with their start and end apart: 3, of which 3 were waited for; matrix products, arithmetic and copies ran while one was open for 1% of the time, Pallas kernels for 0%

commit v1 on v0

v1 whole, which is shorter than its diff:
```python
import functools
import math

import jax
import jax.numpy as jnp
from jax import lax
from jax.experimental import pallas as pl
from jax.experimental.pallas import tpu as pltpu
from jax.sharding import PartitionSpec as P

HEAD = 128
IMG_DEV = 2
NEG_FILL = -1e30
BIG = 1e30
LOG2E = 1.4426950408889634
SCALE = HEAD ** (-0.5)
SCALE2 = SCALE * LOG2E

NT = (((1,), (1,)), ((), ()))
TN = (((0,), (0,)), ((), ()))
NN = (((1,), (0,)), ((), ()))


def dot(a, b, dims):
    return lax.dot_general(a, b, dims, preferred_element_type=jnp.float32)


def shift(value, axis, steps):
    count = lax.axis_size(axis)
    pairs = [(source, (source + steps) % count) for source in range(count)]
    return lax.ppermute(value, axis, pairs)


def stack_heads(src_ref, dst_ref, slot):
    rows, cols = src_ref.shape
    for h in range(cols // HEAD):
        dst_ref[slot, h * rows : (h + 1) * rows, :] = src_ref[:, h * HEAD : (h + 1) * HEAD]


def visible_rows(start, rows, width):
    pos = lax.broadcasted_iota(jnp.int32, (1, width), 1) % rows
    return pos >= start


def fwd_kernel(meta, q_own, q_back, g_own, g_back, kv, o_own, o_back, stats, qr, gr, score, wts, acc):
    tok, cols = q_own.shape
    width = tok * cols // HEAD
    keys = kv.shape[1]
    tile = score.shape[0] // 4
    stack_heads(q_own, qr, 0)
    stack_heads(q_back, qr, 1)
    stack_heads(g_own, gr, 0)
    stack_heads(g_back, gr, 1)
    acc[...] = jnp.zeros_like(acc)
    stats[...] = jnp.zeros_like(stats)
    for slot in range(2):
        stats[slot, 0:1, :] = jnp.full((1, width), NEG_FILL, jnp.float32)
    for img in range(IMG_DEV):
        slot = meta[img, 0]
        seen = visible_rows(meta[img, 1], tok, width)
        top = jnp.full((1, width), NEG_FILL, jnp.float32)
        for step in range(keys // tile):
            rows = slice(step * tile, (step + 1) * tile)
            part = dot(kv[img, rows, :HEAD], qr[slot], NT)
            score[rows, :] = part
            top = jnp.maximum(top, jnp.max(part, axis=0, keepdims=True))
        total = jnp.zeros((1, width), jnp.float32)
        out = jnp.zeros((HEAD, width), jnp.float32)
        for step in range(keys // tile):
            rows = slice(step * tile, (step + 1) * tile)
            part = jnp.exp2((score[rows, :] - top) * SCALE2)
            total = total + jnp.sum(part, axis=0, keepdims=True)
            out = out + dot(kv[img, rows, HEAD:], part.astype(jnp.bfloat16), TN)
        old_top = stats[slot, 0:1, :]
        top = jnp.where(seen, top, NEG_FILL)
        new_top = jnp.maximum(old_top, top)
        old_w = jnp.exp2((old_top - new_top) * SCALE2)
        new_w = jnp.where(seen, jnp.exp2((top - new_top) * SCALE2), 0.0)
        stats[slot, 0:1, :] = new_top
        stats[slot, 1:2, :] = stats[slot, 1:2, :] * old_w + total * new_w
        acc[slot] = acc[slot] * old_w + out * new_w
    eye = (
        lax.broadcasted_iota(jnp.int32, (HEAD, HEAD), 0)
        == lax.broadcasted_iota(jnp.int32, (HEAD, HEAD), 1)
    ).astype(jnp.bfloat16)
    for slot in range(2):
        total = stats[slot, 1:2, :]
        mean = acc[slot] * jnp.where(total > 0.0, 1.0 / jnp.maximum(total, 1e-30), 0.0)
        cot = dot(eye, gr[slot], NT)
        stats[slot, 2:3, :] = jnp.sum(cot * mean, axis=0, keepdims=True)
        if slot == 0:
            o_own[...] = mean
        else:
            o_back[...] = mean.astype(jnp.bfloat16)


def merge(first, second):
    top = jnp.maximum(first[0:1], second[0:1])
    w_first = first[1:2] * jnp.exp2((first[0:1] - top) * SCALE2)
    w_second = second[1:2] * jnp.exp2((second[0:1] - top) * SCALE2)
    total = w_first + w_second
    inv = jnp.where(total > 0.0, 1.0 / jnp.maximum(total, 1e-30), 0.0)
    return top, total, w_first * inv, w_second * inv


def bwd_kernel(meta, q_own, q_back, g_own, g_back, kv, stats, far_own, far_back,
               dq_own, dq_back, dkv, qr, gr, acc):
    tok, cols = q_own.shape
    width = tok * cols // HEAD
    keys = kv.shape[1]
    tile = 400 if keys % 400 == 0 else keys
    stack_heads(q_own, qr, 0)
    stack_heads(q_back, qr, 1)
    stack_heads(g_own, gr, 0)
    stack_heads(g_back, gr, 1)
    acc[...] = jnp.zeros_like(acc)
    logs, deltas = [], []
    for slot, far in ((0, far_own), (1, far_back)):
        near_v = stats[slot]
        far_v = far[...]
        top, total, w_near, w_far = merge(near_v, far_v)
        logs.append(jnp.where(total > 0.0, top * SCALE2 + jnp.log(jnp.maximum(total, 1e-30)) * LOG2E, 0.0))
        deltas.append(w_near * near_v[2:3] + w_far * far_v[2:3])
    for img in range(IMG_DEV):
        slot = meta[img, 0]
        seen = visible_rows(meta[img, 1], tok, width)
        log_total = jnp.where(slot == 0, logs[0], logs[1])
        log_total = jnp.where(seen, log_total, BIG)
        delta = jnp.where(slot == 0, deltas[0], deltas[1])
        for step in range(keys // tile):
            rows = slice(step * tile, (step + 1) * tile)
            key = kv[img, rows, :HEAD]
            part = jnp.exp2(dot(key, qr[slot], NT) * SCALE2 - log_total)
            dweight = dot(kv[img, rows, HEAD:], gr[slot], NT)
            ds = (part * (dweight - delta)).astype(jnp.bfloat16)
            dkv[img, rows, HEAD:] = dot(part.astype(jnp.bfloat16), gr[slot], NN).astype(jnp.bfloat16)
            dkv[img, rows, :HEAD] = (dot(ds, qr[slot], NN) * SCALE).astype(jnp.bfloat16)
            acc[slot] = acc[slot] + dot(key, ds, TN)
    for slot, out in ((0, dq_own), (1, dq_back)):
        for h in range(cols // HEAD):
            block = acc[slot, :, h * tok : (h + 1) * tok] * SCALE
            out[:, h * HEAD : (h + 1) * HEAD] = block.T.astype(out.dtype)


def finish_kernel(o_own, o_far, stats, far, out):
    tok, cols = out.shape
    _, _, w_near, w_far = merge(stats[0], far[...])
    whole = o_own[...] * w_near + o_far[...].astype(jnp.float32) * w_far
    for h in range(cols // HEAD):
        out[:, h * HEAD : (h + 1) * HEAD] = whole[:, h * tok : (h + 1) * tok].T.astype(out.dtype)


VMEM = pl.BlockSpec(memory_space=pltpu.VMEM)
SMEM = pl.BlockSpec(memory_space=pltpu.SMEM)
PARAMS = dict(compiler_params=pltpu.CompilerParams(vmem_limit_bytes=48 * 1024 * 1024))


def local(queries, key_value_store, output_gradient, image_ids, image_counts, image_start):
    bf16, f32 = jnp.bfloat16, jnp.float32
    tok, cols = queries.shape
    width = tok * cols // HEAD
    n_tensor = lax.axis_size("tensor")
    n_dp = lax.axis_size("dp")
    me_t = lax.axis_index("tensor")
    me_d = lax.axis_index("dp")
    n_img, part_keys, store_cols = key_value_store.shape
    pair = store_cols // n_tensor
    keys = part_keys * n_tensor

    q_back = shift(queries, "dp", 1)
    g_back = shift(output_gradient, "dp", 1)

    pieces = []
    for k in range(n_tensor):
        piece = lax.dynamic_slice_in_dim(key_value_store, ((me_t + k) % n_tensor) * pair, pair, axis=2)
        pieces.append(piece if k == 0 else shift(piece, "tensor", k))
    kv = jnp.concatenate(pieces, axis=1)

    mine = me_d * IMG_DEV + jnp.arange(IMG_DEV, dtype=jnp.int32)
    rows = []
    for slot in range(2):
        sample = (me_d - slot) % n_dp
        ids, starts = image_ids[sample], image_start[sample]
        live = jnp.arange(ids.shape[0], dtype=jnp.int32) < image_counts[sample]
        hit = (ids[None, :] == mine[:, None]) & live[None, :]
        rows.append((jnp.any(hit, axis=1), jnp.sum(jnp.where(hit, starts[None, :], 0), axis=1)))
    slot_of = jnp.where(rows[0][0], 0, 1)
    start_of = jnp.where(rows[0][0], rows[0][1], rows[1][1])
    meta = jnp.stack([slot_of, start_of], axis=1).astype(jnp.int32)

    stat_shape = (2, 8, width)
    row_scratch = [pltpu.VMEM((2, width, HEAD), bf16), pltpu.VMEM((2, width, HEAD), bf16)]
    o_own, o_back, stats = pl.pallas_call(
        fwd_kernel,
        out_shape=(
            jax.ShapeDtypeStruct((HEAD, width), f32),
            jax.ShapeDtypeStruct((HEAD, width), bf16),
            jax.ShapeDtypeStruct(stat_shape, f32),
        ),
        in_specs=[SMEM] + [VMEM] * 5,
        out_specs=(VMEM, VMEM, VMEM),
        scratch_shapes=row_scratch + [
            pltpu.VMEM((keys, width), f32),
            pltpu.VMEM((8, 128), bf16),
            pltpu.VMEM((2, HEAD, width), f32),
        ],
        name="attend",
        **PARAMS,
    )(meta, queries, q_back, output_gradient, g_back, kv)

    far_own = shift(stats[1], "dp", -1)
    far_back = shift(stats[0], "dp", 1)
    o_far = shift(o_back, "dp", -1)

    dq_own, dq_back, dkv = pl.pallas_call(
        bwd_kernel,
        out_shape=(
            jax.ShapeDtypeStruct((tok, cols), f32),
            jax.ShapeDtypeStruct((tok, cols), bf16),
            jax.ShapeDtypeStruct((n_img, keys, pair), bf16),
        ),
        in_specs=[SMEM] + [VMEM] * 8,
        out_specs=(VMEM, VMEM, VMEM),
        scratch_shapes=row_scratch + [pltpu.VMEM((2, HEAD, width), f32)],
        name="backward",
        **PARAMS,
    )(meta, queries, q_back, output_gradient, g_back, kv, stats, far_own, far_back)

    dq_far = shift(dq_back, "dp", -1)
    returned = []
    for k in range(n_tensor):
        piece = dkv[:, k * part_keys : (k + 1) * part_keys, :]
        returned.append(piece if k == 0 else shift(piece, "tensor", -k))

    attended = pl.pallas_call(
        finish_kernel,
        out_shape=jax.ShapeDtypeStruct((tok, cols), bf16),
        in_specs=[VMEM] * 4,
        out_specs=VMEM,
        name="finish",
        **PARAMS,
    )(o_own, o_far, stats, far_own)
    grad_queries = (dq_own + dq_far.astype(f32)).astype(bf16)
    wide = jnp.stack(returned, axis=0)
    order = (jnp.arange(n_tensor) - me_t) % n_tensor
    grad_kv = jnp.concatenate(
        [lax.dynamic_index_in_dim(wide, order[h], 0, keepdims=False) for h in range(n_tensor)], axis=2
    )
    return attended, grad_queries, grad_kv


def solution(mesh):
    return jax.shard_map(
        local,
        mesh=mesh,
        in_specs=(P("dp", "tensor"), P("dp", "tensor", None), P("dp", "tensor"), P(), P(), P()),
        out_specs=(P("dp", "tensor"), P("dp", "tensor"), P("dp", "tensor", None)),
        check_vma=False,
    )
```

time: 536 us -> 270 us (0.50)
  starting transfers between devices: 266 us -> 156 us
  blocking collectives: 108 us -> 0 us
  waiting for transfers between devices: 106 us -> 69.6 us
  local copies, waits for them, and re-layouts: 41 us -> 8.19 us
  Pallas kernels: 0 us -> 16.3 us
  between operations: 0.87 us -> 16.4 us
    all_to_all x1 -> x0, blocking collectives: 108 us -> none  [local(): lax.all_to_all(key_value_store, 'tensor', split_axis=2, concat_axis=1, ti...]
    ppermute x2 -> x20, starting transfers between devices: 262 us -> 156 us  [shift(): return lax.ppermute(value, axis, pairs)]
    all_to_all x1 -> x0, waiting for transfers between devices: 70.9 us -> none  [local(): lax.all_to_all(grad_own, 'tensor', split_axis=1, concat_axis=2, tiled=True)]
    ppermute x2 -> x20, waiting for transfers between devices: 34.7 us -> 69.6 us  [shift(): return lax.ppermute(value, axis, pairs)]
    pallas_call x0 -> x3, Pallas kernels: none -> 16.3 us  [the longest x1 9.16 us: local(): pl.pallas_call(bwd_kernel, out_shape=(jax.ShapeDtypeStruct((tok, cols), f...]
    while x3 -> x0, local copies, waits for them, and re-layouts: 15.2 us -> none  [the longest x1 11.8 us: local(): lax.fori_loop(0, slot_count, back_step, (jnp.zeros((tok_rows, head_block,...]
    unnamed x26 -> x34, local copies, waits for them, and re-layouts: 10.6 us -> 3.89 us
    all_to_all x3 -> x0, local copies, waits for them, and re-layouts: 5.84 us -> none  [the longest x1 3.63 us: local(): lax.all_to_all(key_value_store, 'tensor', split_axis=2, concat_axis=1, ti...]
  transfers between devices with their start and end apart: 3 -> 20, of which waited for: 3 -> 8; matrix products, arithmetic and copies ran while one was open for 1% -> 3% of each run, Pallas kernels for 0% -> 4%
where the time goes in v1:
time: 270 us; the launch traced here: 269 us
  starting transfers between devices  156 us (58%)
  waiting for transfers between devices  69.6 us (26%)
  between operations  16.4 us (6%)
  Pallas kernels  16.3 us (6%)
  local copies, waits for them, and re-layouts  8.19 us (3%)
    ppermute x20, starting transfers between devices, shift(): return lax.ppermute(value, axis, pairs)  156 us
    ppermute x20, waiting for transfers between devices, shift(): return lax.ppermute(value, axis, pairs)  69.6 us
    pallas_call x1, Pallas kernels, local(): pl.pallas_call(bwd_kernel, out_shape=(jax.ShapeDtypeStruct((tok, cols), f...  9.16 us
    pallas_call x1, Pallas kernels, local(): pl.pallas_call(fwd_kernel, out_shape=(jax.ShapeDtypeStruct((HEAD, width),...  6.09 us
  transfers between devices with their start and end apart: 20, of which 8 were waited for; matrix products, arithmetic and copies ran while one was open for 3% of the time, Pallas kernels for 4%

profile of v1, /device:TPU:1, one launch (start us, length us, event | category | flops | bytes accessed | tf_op | source)
XLA Modules:
  0.0 268.7 jit_solution(13551153824178252855)
XLA Ops:
  0.6 4.5 %collective-permute-start = (bf16[128,1024]{1,0:T(8,128)(2,1)}, bf16[128,1024]{1,0:T(8,128)(2,1)S(1)}, u32[]{:S(2)}, u32[]{:S(2)}) collective-permute-start(bf16[128,1024]{1,0:T(8,128)(2,1)} %q_own.3), channel_id=1, source_target_pairs={{0,8},{8,16},{16,24},{24,32},{32,40},{40,48},{48,56},{56,64},{64,7... | collective-permute-start | bytes 786440 | tf_op jit(solution)/shard_map/ppermute | solution.py:31
  5.1 1.9 collective-permute-start.1
  7.2 0.0 copy-start.6
  7.2 0.0 copy-start.4
  7.2 0.0 copy-start.5
  7.2 2.4 constant_dynamic-slice_fusion
  9.6 3.7 %collective-permute-start.2 = (bf16[2,200,256]{2,1,0:T(8,128)(2,1)}, bf16[2,200,256]{2,1,0:T(8,128)(2,1)}, u32[]{:S(2)}, u32[]{:S(2)}) collective-permute-start(bf16[2,200,256]{2,1,0:T(8,128)(2,1)} %get-tuple-element.33), channel_id=1, source_target_pairs={{0,1},{1,2},{2,3},{3,4},{4,5},{5,6},{6,7},{7,0},{8,9},{9,10},{10,1... | collective-permute-start | bytes 614408 | tf_op jit(solution)/shard_map/ppermute | solution.py:31
  13.3 4.9 %collective-permute-start.3 = (bf16[2,200,256]{2,1,0:T(8,128)(2,1)}, bf16[2,200,256]{2,1,0:T(8,128)(2,1)}, u32[]{:S(2)}, u32[]{:S(2)}) collective-permute-start(bf16[2,200,256]{2,1,0:T(8,128)(2,1)} %get-tuple-element.32), channel_id=1, source_target_pairs={{0,2},{1,3},{2,4},{3,5},{4,6},{5,7},{6,0},{7,1},{8,10},{9,11},{10,... | collective-permute-start | bytes 614408 | tf_op jit(solution)/shard_map/ppermute | solution.py:31
  18.2 7.5 %collective-permute-start.4 = (bf16[2,200,256]{2,1,0:T(8,128)(2,1)}, bf16[2,200,256]{2,1,0:T(8,128)(2,1)}, u32[]{:S(2)}, u32[]{:S(2)}) collective-permute-start(bf16[2,200,256]{2,1,0:T(8,128)(2,1)} %get-tuple-element.31), channel_id=1, source_target_pairs={{0,3},{1,4},{2,5},{3,6},{4,7},{5,0},{6,1},{7,2},{8,11},{9,12},{10,... | collective-permute-start | bytes 614408 | tf_op jit(solution)/shard_map/ppermute | solution.py:31
  25.8 0.7 fusion.11
  26.4 1.3 iota_compare_fusion
  27.7 0.2 fusion.2
  28.0 0.2 fusion.5
  28.1 0.2 fusion.7
  28.3 0.1 copy.12
  28.4 0.1 copy.11
  28.5 0.1 pad_add_fusion.meta
  28.6 0.0 collective-permute-done.2
  28.6 3.3 %collective-permute-start.5 = (bf16[2,200,256]{2,1,0:T(8,128)(2,1)S(1)}, bf16[2,200,256]{2,1,0:T(8,128)(2,1)S(1)}, u32[]{:S(2)}, u32[]{:S(2)}) collective-permute-start(bf16[2,200,256]{2,1,0:T(8,128)(2,1)S(1)} %get-tuple-element.30), channel_id=1, source_target_pairs={{0,4},{1,5},{2,6},{3,7},{4,0},{5,1},{6,2},{7,3},{8,12},{9,13},{10,... | collective-permute-start | bytes 614408 | tf_op jit(solution)/shard_map/ppermute | solution.py:31
  31.9 0.9 constant_dynamic-update-slice_fusion.6
  32.9 13.3 %collective-permute-done.3 = bf16[2,200,256]{2,1,0:T(8,128)(2,1)} collective-permute-done((bf16[2,200,256]{2,1,0:T(8,128)(2,1)}, bf16[2,200,256]{2,1,0:T(8,128)(2,1)}, u32[]{:S(2)}, u32[]{:S(2)}) %collective-permute-start.3) | collective-permute-done | bytes 204832 | tf_op jit(solution)/shard_map/ppermute | solution.py:31
  46.1 1.9 collective-permute-start.6
  48.0 0.9 constant_dynamic-update-slice_fusion.5
  49.0 19.1 %collective-permute-done.4 = bf16[2,200,256]{2,1,0:T(8,128)(2,1)} collective-permute-done((bf16[2,200,256]{2,1,0:T(8,128)(2,1)}, bf16[2,200,256]{2,1,0:T(8,128)(2,1)}, u32[]{:S(2)}, u32[]{:S(2)}) %collective-permute-start.4) | collective-permute-done | bytes 204832 | tf_op jit(solution)/shard_map/ppermute | solution.py:31
  68.1 1.9 collective-permute-start.7
  70.0 0.9 constant_dynamic-update-slice_fusion.4
  71.0 0.0 collective-permute-done.5
  71.0 22.3 %collective-permute-start.8 = (bf16[2,200,256]{2,1,0:T(8,128)(2,1)S(1)}, bf16[2,200,256]{2,1,0:T(8,128)(2,1)S(1)}, u32[]{:S(2)}, u32[]{:S(2)}) collective-permute-start(bf16[2,200,256]{2,1,0:T(8,128)(2,1)S(1)} %get-tuple-element.28), channel_id=1, source_target_pairs={{0,7},{1,0},{2,1},{3,2},{4,3},{5,4},{6,5},{7,6},{8,15},{9,8},{10,9... | collective-permute-start | bytes 614408 | tf_op jit(solution)/shard_map/ppermute | solution.py:31
  93.3 0.0 collective-permute-done.6
  93.3 0.0 collective-permute-done.7
  93.4 3.9 %collective-permute-done.8 = bf16[2,200,256]{2,1,0:T(8,128)(2,1)S(1)} collective-permute-done((bf16[2,200,256]{2,1,0:T(8,128)(2,1)S(1)}, bf16[2,200,256]{2,1,0:T(8,128)(2,1)S(1)}, u32[]{:S(2)}, u32[]{:S(2)}) %collective-permute-start.8) | collective-permute-done | bytes 204832 | tf_op jit(solution)/shard_map/ppermute | solution.py:31
  97.3 0.0 collective-permute-done.q_back
  97.3 0.0 collective-permute-done.1.g_back
  97.4 6.1 %attend.1 = (f32[128,1024]{1,0:T(8,128)S(1)}, bf16[128,1024]{1,0:T(8,128)(2,1)S(1)}, f32[2,8,1024]{2,1,0:T(8,128)S(1)}) custom-call(s32[2,2]{1,0:T(2,128)S(1)} %pad_add_fusion.meta, bf16[128,1024]{1,0:T(8,128)(2,1)S(1)} %copy-done, bf16[128,1024]{1,0:T(8,128)(2,1)S(1)} %collective-permute-done.q_back, bf16[128,1024]{1,0:T(8,128)(2,1)S(1)} %copy-done.1, ...), custom_call_target="tpu_custom_call" | custom-call | tf_op jit(solution)/shard_map/attend/pallas_call | solution.py:193
  103.5 0.0 copy-start.2
  103.5 0.7 copy-done.2
  104.2 3.1 %collective-permute-start.10 = (f32[8,1024]{1,0:T(8,128)S(1)}, f32[8,1024]{1,0:T(8,128)S(1)}, u32[]{:S(2)}, u32[]{:S(2)}) collective-permute-start(f32[8,1024]{1,0:T(8,128)S(1)} %get-tuple-element.37), channel_id=1, source_target_pairs={{0,504},{8,0},{16,8},{24,16},{32,24},{40,32},{48,40},{56,48},{64,5... | collective-permute-start | bytes 98312 | tf_op jit(solution)/shard_map/ppermute | solution.py:31
  107.3 3.0 %collective-permute-start.11 = (f32[8,1024]{1,0:T(8,128)S(1)}, f32[8,1024]{1,0:T(8,128)S(1)}, u32[]{:S(2)}, u32[]{:S(2)}) collective-permute-start(f32[8,1024]{1,0:T(8,128)S(1)} %get-tuple-element.36), channel_id=1, source_target_pairs={{0,8},{8,16},{16,24},{24,32},{32,40},{40,48},{48,56},{56,64},{64,7... | collective-permute-start | bytes 98312 | tf_op jit(solution)/shard_map/ppermute | solution.py:31
  110.3 0.7 fusion.10
  126.1 24.9 %collective-permute-start.9 = (bf16[128,1024]{1,0:T(8,128)(2,1)}, bf16[128,1024]{1,0:T(8,128)(2,1)S(1)}, u32[]{:S(2)}, u32[]{:S(2)}) collective-permute-start(bf16[128,1024]{1,0:T(8,128)(2,1)} %copy-done.2), channel_id=1, source_target_pairs={{0,504},{8,0},{16,8},{24,16},{32,24},{40,32},{48,40},{56,48},{64,5... | collective-permute-start | bytes 786440 | tf_op jit(solution)/shard_map/ppermute | solution.py:31
  151.0 0.0 collective-permute-done.10.far.far_own
  151.1 0.0 collective-permute-done.11.far_back
  151.1 9.2 %backward.1 = (f32[128,1024]{1,0:T(8,128)S(1)}, bf16[128,1024]{1,0:T(8,128)(2,1)S(1)}, bf16[2,1600,256]{2,1,0:T(8,128)(2,1)S(1)}) custom-call(s32[2,2]{1,0:T(2,128)S(1)} %pad_add_fusion.meta, bf16[128,1024]{1,0:T(8,128)(2,1)S(1)} %copy-done, bf16[128,1024]{1,0:T(8,128)(2,1)S(1)} %collective-permute-done.q_back, bf16[128,1024]{1,0:T(8,128)(2,1)S(1)} %copy-done.1, ...), custom_call_target="tpu_custom_call" | custom-call | tf_op jit(solution)/shard_map/backward/pallas_call | solution.py:215
  160.2 16.6 %collective-permute-start.12 = (bf16[128,1024]{1,0:T(8,128)(2,1)S(1)}, bf16[128,1024]{1,0:T(8,128)(2,1)S(1)}, u32[]{:S(2)}, u32[]{:S(2)}) collective-permute-start(bf16[128,1024]{1,0:T(8,128)(2,1)S(1)} %get-tuple-element.13), channel_id=1, source_target_pairs={{0,504},{8,0},{16,8},{24,16},{32,24},{40,32},{48,40},{56,48},{64,5... | collective-permute-start | bytes 786440 | tf_op jit(solution)/shard_map/ppermute | solution.py:31
  176.8 0.1 fusion.9
  176.9 10.7 %collective-permute-start.13 = (bf16[2,200,256]{2,1,0:T(8,128)(2,1)S(1)}, bf16[2,200,256]{2,1,0:T(8,128)(2,1)S(1)}, u32[]{:S(2)}, u32[]{:S(2)}) collective-permute-start(bf16[2,200,256]{2,1,0:T(8,128)(2,1)S(1)} %get-tuple-element.27), channel_id=1, source_target_pairs={{0,7},{1,0},{2,1},{3,2},{4,3},{5,4},{6,5},{7,6},{8,15},{9,8},{10,9... | collective-permute-start | bytes 614408 | tf_op jit(solution)/shard_map/ppermute | solution.py:31
  187.6 1.9 collective-permute-start.14
  189.6 1.9 collective-permute-start.15
  191.5 0.6 collective-permute-done.13
  192.2 8.6 %collective-permute-start.16 = (bf16[2,200,256]{2,1,0:T(8,128)(2,1)S(1)}, bf16[2,200,256]{2,1,0:T(8,128)(2,1)S(1)}, u32[]{:S(2)}, u32[]{:S(2)}) collective-permute-start(bf16[2,200,256]{2,1,0:T(8,128)(2,1)S(1)} %get-tuple-element.24), channel_id=1, source_target_pairs={{0,4},{1,5},{2,6},{3,7},{4,0},{5,1},{6,2},{7,3},{8,12},{9,13},{10,... | collective-permute-start | bytes 614408 | tf_op jit(solution)/shard_map/ppermute | solution.py:31
  200.8 3.7 %collective-permute-done.14 = bf16[2,200,256]{2,1,0:T(8,128)(2,1)S(1)} collective-permute-done((bf16[2,200,256]{2,1,0:T(8,128)(2,1)S(1)}, bf16[2,200,256]{2,1,0:T(8,128)(2,1)S(1)}, u32[]{:S(2)}, u32[]{:S(2)}) %collective-permute-start.14) | collective-permute-done | bytes 204832 | tf_op jit(solution)/shard_map/ppermute | solution.py:31
  204.4 3.2 %collective-permute-start.17 = (bf16[2,200,256]{2,1,0:T(8,128)(2,1)S(1)}, bf16[2,200,256]{2,1,0:T(8,128)(2,1)S(1)}, u32[]{:S(2)}, u32[]{:S(2)}) collective-permute-start(bf16[2,200,256]{2,1,0:T(8,128)(2,1)S(1)} %get-tuple-element.23), channel_id=1, source_target_pairs={{0,3},{1,4},{2,5},{3,6},{4,7},{5,0},{6,1},{7,2},{8,11},{9,12},{10,... | collective-permute-start | bytes 614408 | tf_op jit(solution)/shard_map/ppermute | solution.py:31
  207.7 1.3 collective-permute-done.15
  209.0 28.0 %collective-permute-start.18 = (bf16[2,200,256]{2,1,0:T(8,128)(2,1)S(1)}, bf16[2,200,256]{2,1,0:T(8,128)(2,1)S(1)}, u32[]{:S(2)}, u32[]{:S(2)}) collective-permute-start(bf16[2,200,256]{2,1,0:T(8,128)(2,1)S(1)} %get-tuple-element.22), channel_id=1, source_target_pairs={{0,2},{1,3},{2,4},{3,5},{4,6},{5,7},{6,0},{7,1},{8,10},{9,11},{10,... | collective-permute-start | bytes 614408 | tf_op jit(solution)/shard_map/ppermute | solution.py:31
  237.1 15.3 %collective-permute-done.16 = bf16[2,200,256]{2,1,0:T(8,128)(2,1)S(1)} collective-permute-done((bf16[2,200,256]{2,1,0:T(8,128)(2,1)S(1)}, bf16[2,200,256]{2,1,0:T(8,128)(2,1)S(1)}, u32[]{:S(2)}, u32[]{:S(2)}) %collective-permute-start.16) | collective-permute-done | bytes 204832 | tf_op jit(solution)/shard_map/ppermute | solution.py:31
  252.3 1.9 collective-permute-start.19
  254.3 0.0 collective-permute-done.17
  254.3 0.0 collective-permute-done.18
  254.3 12.3 %collective-permute-done.19 = bf16[2,200,256]{2,1,0:T(8,128)(2,1)S(1)} collective-permute-done((bf16[2,200,256]{2,1,0:T(8,128)(2,1)S(1)}, bf16[2,200,256]{2,1,0:T(8,128)(2,1)S(1)}, u32[]{:S(2)}, u32[]{:S(2)}) %collective-permute-start.19) | collective-permute-done | bytes 204832 | tf_op jit(solution)/shard_map/ppermute | solution.py:31
  266.9 0.0 copy-start.3
  266.9 0.0 collective-permute-done.9.o_far
  266.9 1.1 finish.1
  268.0 0.0 collective-permute-done.12
  268.0 0.8 add_convert_fusion
  (32 shorter events, 0.4 us)
Async XLA Ops:
  0.6 96.7 %collective-permute-start = (bf16[128,1024]{1,0:T(8,128)(2,1)}, bf16[128,1024]{1,0:T(8,128)(2,1)S(1)}, u32[]{:S(2)}, u32[]{:S(2)}) collective-permute-start(bf16[128,1024]{1,0:T(8,128)(2,1)} %q_own.3), channel_id=1, source_target_pairs={{0,8},{8,16},{16,24},{24,32},{32,40},{40,48},{48,56},{56,64},{64,7... | collective-permute-start | bytes 786440 | tf_op jit(solution)/shard_map/ppermute | solution.py:31
  5.1 92.2 %collective-permute-start.1 = (bf16[128,1024]{1,0:T(8,128)(2,1)}, bf16[128,1024]{1,0:T(8,128)(2,1)S(1)}, u32[]{:S(2)}, u32[]{:S(2)}) collective-permute-start(bf16[128,1024]{1,0:T(8,128)(2,1)} %g_own.3), channel_id=1, source_target_pairs={{0,8},{8,16},{16,24},{24,32},{32,40},{40,48},{48,56},{56,64},{64,7... | collective-permute-start | bytes 786440 | tf_op jit(solution)/shard_map/ppermute | solution.py:31
  7.2 18.6 %copy-start.6 = (s32[64]{0:T(128)S(1)}, s32[64]{0:T(128)}, u32[]{:S(2)}) copy-start(s32[64]{0:T(128)} %param.10) | copy-start | bytes 772
  7.2 20.5 %copy-start.4 = (s32[64,4]{0,1:T(4,128)S(1)}, s32[64,4]{0,1:T(4,128)}, u32[]{:S(2)}) copy-start(s32[64,4]{0,1:T(4,128)} %param.9) | copy-start | bytes 3076
  7.2 20.5 %copy-start.5 = (s32[64,4]{0,1:T(4,128)S(1)}, s32[64,4]{0,1:T(4,128)}, u32[]{:S(2)}) copy-start(s32[64,4]{0,1:T(4,128)} %param.11) | copy-start | bytes 3076
  9.6 87.7 %copy-start = (bf16[128,1024]{1,0:T(8,128)(2,1)S(1)}, bf16[128,1024]{1,0:T(8,128)(2,1)}, u32[]{:S(2)}) copy-start(bf16[128,1024]{1,0:T(8,128)(2,1)} %q_own.3) | copy-start | bytes 786436
  9.6 87.7 %copy-start.1 = (bf16[128,1024]{1,0:T(8,128)(2,1)S(1)}, bf16[128,1024]{1,0:T(8,128)(2,1)}, u32[]{:S(2)}) copy-start(bf16[128,1024]{1,0:T(8,128)(2,1)} %g_own.3) | copy-start | bytes 786436
  9.6 19.0 %collective-permute-start.2 = (bf16[2,200,256]{2,1,0:T(8,128)(2,1)}, bf16[2,200,256]{2,1,0:T(8,128)(2,1)}, u32[]{:S(2)}, u32[]{:S(2)}) collective-permute-start(bf16[2,200,256]{2,1,0:T(8,128)(2,1)} %get-tuple-element.33), channel_id=1, source_target_pairs={{0,1},{1,2},{2,3},{3,4},{4,5},{5,6},{6,7},{7,0},{8,9},{9,10},{10,1... | collective-permute-start | bytes 614408 | tf_op jit(solution)/shard_map/ppermute | solution.py:31
  13.3 32.8 %collective-permute-start.3 = (bf16[2,200,256]{2,1,0:T(8,128)(2,1)}, bf16[2,200,256]{2,1,0:T(8,128)(2,1)}, u32[]{:S(2)}, u32[]{:S(2)}) collective-permute-start(bf16[2,200,256]{2,1,0:T(8,128)(2,1)} %get-tuple-element.32), channel_id=1, source_target_pairs={{0,2},{1,3},{2,4},{3,5},{4,6},{5,7},{6,0},{7,1},{8,10},{9,11},{10,... | collective-permute-start | bytes 614408 | tf_op jit(solution)/shard_map/ppermute | solution.py:31
  18.2 49.9 %collective-permute-start.4 = (bf16[2,200,256]{2,1,0:T(8,128)(2,1)}, bf16[2,200,256]{2,1,0:T(8,128)(2,1)}, u32[]{:S(2)}, u32[]{:S(2)}) collective-permute-start(bf16[2,200,256]{2,1,0:T(8,128)(2,1)} %get-tuple-element.31), channel_id=1, source_target_pairs={{0,3},{1,4},{2,5},{3,6},{4,7},{5,0},{6,1},{7,2},{8,11},{9,12},{10,... | collective-permute-start | bytes 614408 | tf_op jit(solution)/shard_map/ppermute | solution.py:31
  28.6 42.4 %collective-permute-start.5 = (bf16[2,200,256]{2,1,0:T(8,128)(2,1)S(1)}, bf16[2,200,256]{2,1,0:T(8,128)(2,1)S(1)}, u32[]{:S(2)}, u32[]{:S(2)}) collective-permute-start(bf16[2,200,256]{2,1,0:T(8,128)(2,1)S(1)} %get-tuple-element.30), channel_id=1, source_target_pairs={{0,4},{1,5},{2,6},{3,7},{4,0},{5,1},{6,2},{7,3},{8,12},{9,13},{10,... | collective-permute-start | bytes 614408 | tf_op jit(solution)/shard_map/ppermute | solution.py:31
  46.1 47.2 %collective-permute-start.6 = (bf16[2,200,256]{2,1,0:T(8,128)(2,1)S(1)}, bf16[2,200,256]{2,1,0:T(8,128)(2,1)S(1)}, u32[]{:S(2)}, u32[]{:S(2)}) collective-permute-start(bf16[2,200,256]{2,1,0:T(8,128)(2,1)S(1)} %get-tuple-element.29), channel_id=1, source_target_pairs={{0,5},{1,6},{2,7},{3,0},{4,1},{5,2},{6,3},{7,4},{8,13},{9,14},{10,... | collective-permute-start | bytes 614408 | tf_op jit(solution)/shard_map/ppermute | solution.py:31
  68.1 25.2 %collective-permute-start.7 = (bf16[2,200,256]{2,1,0:T(8,128)(2,1)S(1)}, bf16[2,200,256]{2,1,0:T(8,128)(2,1)S(1)}, u32[]{:S(2)}, u32[]{:S(2)}) collective-permute-start(bf16[2,200,256]{2,1,0:T(8,128)(2,1)S(1)} %get-tuple-element.35), channel_id=1, source_target_pairs={{0,6},{1,7},{2,0},{3,1},{4,2},{5,3},{6,4},{7,5},{8,14},{9,15},{10,... | collective-permute-start | bytes 614408 | tf_op jit(solution)/shard_map/ppermute | solution.py:31
  71.0 26.3 %collective-permute-start.8 = (bf16[2,200,256]{2,1,0:T(8,128)(2,1)S(1)}, bf16[2,200,256]{2,1,0:T(8,128)(2,1)S(1)}, u32[]{:S(2)}, u32[]{:S(2)}) collective-permute-start(bf16[2,200,256]{2,1,0:T(8,128)(2,1)S(1)} %get-tuple-element.28), channel_id=1, source_target_pairs={{0,7},{1,0},{2,1},{3,2},{4,3},{5,4},{6,5},{7,6},{8,15},{9,8},{10,9... | collective-permute-start | bytes 614408 | tf_op jit(solution)/shard_map/ppermute | solution.py:31
  103.5 0.7 copy-start.2
  104.2 46.9 %collective-permute-start.10 = (f32[8,1024]{1,0:T(8,128)S(1)}, f32[8,1024]{1,0:T(8,128)S(1)}, u32[]{:S(2)}, u32[]{:S(2)}) collective-permute-start(f32[8,1024]{1,0:T(8,128)S(1)} %get-tuple-element.37), channel_id=1, source_target_pairs={{0,504},{8,0},{16,8},{24,16},{32,24},{40,32},{48,40},{56,48},{64,5... | collective-permute-start | bytes 98312 | tf_op jit(solution)/shard_map/ppermute | solution.py:31
  107.3 43.7 %collective-permute-start.11 = (f32[8,1024]{1,0:T(8,128)S(1)}, f32[8,1024]{1,0:T(8,128)S(1)}, u32[]{:S(2)}, u32[]{:S(2)}) collective-permute-start(f32[8,1024]{1,0:T(8,128)S(1)} %get-tuple-element.36), channel_id=1, source_target_pairs={{0,8},{8,16},{16,24},{24,32},{32,40},{40,48},{48,56},{56,64},{64,7... | collective-permute-start | bytes 98312 | tf_op jit(solution)/shard_map/ppermute | solution.py:31
  126.1 140.8 %collective-permute-start.9 = (bf16[128,1024]{1,0:T(8,128)(2,1)}, bf16[128,1024]{1,0:T(8,128)(2,1)S(1)}, u32[]{:S(2)}, u32[]{:S(2)}) collective-permute-start(bf16[128,1024]{1,0:T(8,128)(2,1)} %copy-done.2), channel_id=1, source_target_pairs={{0,504},{8,0},{16,8},{24,16},{32,24},{40,32},{48,40},{56,48},{64,5... | collective-permute-start | bytes 786440 | tf_op jit(solution)/shard_map/ppermute | solution.py:31
  160.2 107.7 %collective-permute-start.12 = (bf16[128,1024]{1,0:T(8,128)(2,1)S(1)}, bf16[128,1024]{1,0:T(8,128)(2,1)S(1)}, u32[]{:S(2)}, u32[]{:S(2)}) collective-permute-start(bf16[128,1024]{1,0:T(8,128)(2,1)S(1)} %get-tuple-element.13), channel_id=1, source_target_pairs={{0,504},{8,0},{16,8},{24,16},{32,24},{40,32},{48,40},{56,48},{64,5... | collective-permute-start | bytes 786440 | tf_op jit(solution)/shard_map/ppermute | solution.py:31
  176.9 15.2 %collective-permute-start.13 = (bf16[2,200,256]{2,1,0:T(8,128)(2,1)S(1)}, bf16[2,200,256]{2,1,0:T(8,128)(2,1)S(1)}, u32[]{:S(2)}, u32[]{:S(2)}) collective-permute-start(bf16[2,200,256]{2,1,0:T(8,128)(2,1)S(1)} %get-tuple-element.27), channel_id=1, source_target_pairs={{0,7},{1,0},{2,1},{3,2},{4,3},{5,4},{6,5},{7,6},{8,15},{9,8},{10,9... | collective-permute-start | bytes 614408 | tf_op jit(solution)/shard_map/ppermute | solution.py:31
  187.6 16.8 %collective-permute-start.14 = (bf16[2,200,256]{2,1,0:T(8,128)(2,1)S(1)}, bf16[2,200,256]{2,1,0:T(8,128)(2,1)S(1)}, u32[]{:S(2)}, u32[]{:S(2)}) collective-permute-start(bf16[2,200,256]{2,1,0:T(8,128)(2,1)S(1)} %get-tuple-element.26), channel_id=1, source_target_pairs={{0,6},{1,7},{2,0},{3,1},{4,2},{5,3},{6,4},{7,5},{8,14},{9,15},{10,... | collective-permute-start | bytes 614408 | tf_op jit(solution)/shard_map/ppermute | solution.py:31
  189.6 19.5 %collective-permute-start.15 = (bf16[2,200,256]{2,1,0:T(8,128)(2,1)S(1)}, bf16[2,200,256]{2,1,0:T(8,128)(2,1)S(1)}, u32[]{:S(2)}, u32[]{:S(2)}) collective-permute-start(bf16[2,200,256]{2,1,0:T(8,128)(2,1)S(1)} %get-tuple-element.25), channel_id=1, source_target_pairs={{0,5},{1,6},{2,7},{3,0},{4,1},{5,2},{6,3},{7,4},{8,13},{9,14},{10,... | collective-permute-start | bytes 614408 | tf_op jit(solution)/shard_map/ppermute | solution.py:31
  192.2 60.2 %collective-permute-start.16 = (bf16[2,200,256]{2,1,0:T(8,128)(2,1)S(1)}, bf16[2,200,256]{2,1,0:T(8,128)(2,1)S(1)}, u32[]{:S(2)}, u32[]{:S(2)}) collective-permute-start(bf16[2,200,256]{2,1,0:T(8,128)(2,1)S(1)} %get-tuple-element.24), channel_id=1, source_target_pairs={{0,4},{1,5},{2,6},{3,7},{4,0},{5,1},{6,2},{7,3},{8,12},{9,13},{10,... | collective-permute-start | bytes 614408 | tf_op jit(solution)/shard_map/ppermute | solution.py:31
  204.4 49.8 %collective-permute-start.17 = (bf16[2,200,256]{2,1,0:T(8,128)(2,1)S(1)}, bf16[2,200,256]{2,1,0:T(8,128)(2,1)S(1)}, u32[]{:S(2)}, u32[]{:S(2)}) collective-permute-start(bf16[2,200,256]{2,1,0:T(8,128)(2,1)S(1)} %get-tuple-element.23), channel_id=1, source_target_pairs={{0,3},{1,4},{2,5},{3,6},{4,7},{5,0},{6,1},{7,2},{8,11},{9,12},{10,... | collective-permute-start | bytes 614408 | tf_op jit(solution)/shard_map/ppermute | solution.py:31
  209.0 45.3 %collective-permute-start.18 = (bf16[2,200,256]{2,1,0:T(8,128)(2,1)S(1)}, bf16[2,200,256]{2,1,0:T(8,128)(2,1)S(1)}, u32[]{:S(2)}, u32[]{:S(2)}) collective-permute-start(bf16[2,200,256]{2,1,0:T(8,128)(2,1)S(1)} %get-tuple-element.22), channel_id=1, source_target_pairs={{0,2},{1,3},{2,4},{3,5},{4,6},{5,7},{6,0},{7,1},{8,10},{9,11},{10,... | collective-permute-start | bytes 614408 | tf_op jit(solution)/shard_map/ppermute | solution.py:31
  252.3 14.3 %collective-permute-start.19 = (bf16[2,200,256]{2,1,0:T(8,128)(2,1)S(1)}, bf16[2,200,256]{2,1,0:T(8,128)(2,1)S(1)}, u32[]{:S(2)}, u32[]{:S(2)}) collective-permute-start(bf16[2,200,256]{2,1,0:T(8,128)(2,1)S(1)} %get-tuple-element.21), channel_id=1, source_target_pairs={{0,1},{1,2},{2,3},{3,4},{4,5},{5,6},{6,7},{7,0},{8,9},{9,10},{10,1... | collective-permute-start | bytes 614408 | tf_op jit(solution)/shard_map/ppermute | solution.py:31
  266.9 1.9 copy-start.3

commit v2 on v1

v2 whole, which is shorter than its diff:
```python
import functools
import math

import jax
import jax.numpy as jnp
from jax import lax
from jax.experimental import pallas as pl
from jax.experimental.pallas import tpu as pltpu
from jax.sharding import PartitionSpec as P

HEAD = 128
IMG_DEV = 2
NEG_FILL = -1e30
BIG = 1e30
LOG2E = 1.4426950408889634
SCALE = HEAD ** (-0.5)
SCALE2 = SCALE * LOG2E

NT = (((1,), (1,)), ((), ()))
TN = (((0,), (0,)), ((), ()))
NN = (((1,), (0,)), ((), ()))


def dot(a, b, dims):
    return lax.dot_general(a, b, dims, preferred_element_type=jnp.float32)


def shift(value, axis, steps):
    count = lax.axis_size(axis)
    pairs = [(source, (source + steps) % count) for source in range(count)]
    return lax.ppermute(value, axis, pairs)


def stack_heads(src_ref, dst_ref, slot):
    rows, cols = src_ref.shape
    for h in range(cols // HEAD):
        dst_ref[slot, h * rows : (h + 1) * rows, :] = src_ref[:, h * HEAD : (h + 1) * HEAD]


def visible_rows(start, rows, width):
    pos = lax.broadcasted_iota(jnp.int32, (1, width), 1) % rows
    return pos >= start


def load_rows(refs, dst_ref):
    for slot, ref in enumerate(refs):
        stack_heads(ref, dst_ref, slot)


def split_kernel(axis, store, *pieces):
    n, width = len(pieces), pieces[0].shape[-1]
    for k, piece in enumerate(pieces):
        col = lax.rem(lax.axis_index(axis) + k, n) * width
        piece[...] = store[:, :, pl.ds(pl.multiple_of(col, width), width)]


def join_kernel(axis, *refs):
    pieces, out = refs[:-1], refs[-1]
    n, width = len(pieces), pieces[0].shape[-1]
    for k, piece in enumerate(pieces):
        col = lax.rem(lax.axis_index(axis) + k, n) * width
        out[:, :, pl.ds(pl.multiple_of(col, width), width)] = piece[...]


def fwd_kernel(first, last, blocks, *refs):
    refs = list(refs)
    meta, q_own, q_back = refs[:3]
    del refs[:3]
    if last:
        g_own, g_back = refs[:2]
        del refs[:2]
    kvs = refs[:blocks]
    del refs[:blocks]
    if not first:
        acc_in, stats_in = refs[:2]
        del refs[:2]
    if last:
        o_own, o_back, stats, qr, gr, acc = refs
    else:
        acc, stats, qr = refs
    tok, cols = q_own.shape
    width = tok * cols // HEAD
    load_rows((q_own, q_back), qr)
    if first:
        acc[...] = jnp.zeros_like(acc)
        stats[...] = jnp.zeros_like(stats)
        for slot in range(2):
            stats[slot, 0:1, :] = jnp.full((1, width), NEG_FILL, jnp.float32)
    else:
        acc[...] = acc_in[...]
        stats[...] = stats_in[...]
    for img in range(IMG_DEV):
        slot = meta[img, 0]
        seen = visible_rows(meta[img, 1], tok, width)
        scores = [dot(kv[img, :, :HEAD], qr[slot], NT) for kv in kvs]
        top = functools.reduce(jnp.maximum, [jnp.max(s, axis=0, keepdims=True) for s in scores])
        total = jnp.zeros((1, width), jnp.float32)
        out = jnp.zeros((HEAD, width), jnp.float32)
        for kv, s in zip(kvs, scores):
            part = jnp.exp2((s - top) * SCALE2)
            total = total + jnp.sum(part, axis=0, keepdims=True)
            out = out + dot(kv[img, :, HEAD:], part.astype(jnp.bfloat16), TN)
        old_top = stats[slot, 0:1, :]
        top = jnp.where(seen, top, NEG_FILL)
        new_top = jnp.maximum(old_top, top)
        old_w = jnp.exp2((old_top - new_top) * SCALE2)
        new_w = jnp.where(seen, jnp.exp2((top - new_top) * SCALE2), 0.0)
        stats[slot, 0:1, :] = new_top
        stats[slot, 1:2, :] = stats[slot, 1:2, :] * old_w + total * new_w
        acc[slot] = acc[slot] * old_w + out * new_w
    if last:
        load_rows((g_own, g_back), gr)
        eye = (
            lax.broadcasted_iota(jnp.int32, (HEAD, HEAD), 0)
            == lax.broadcasted_iota(jnp.int32, (HEAD, HEAD), 1)
        ).astype(jnp.bfloat16)
        for slot in range(2):
            total = stats[slot, 1:2, :]
            mean = acc[slot] * jnp.where(total > 0.0, 1.0 / jnp.maximum(total, 1e-30), 0.0)
            cot = dot(eye, gr[slot], NT)
            stats[slot, 2:3, :] = jnp.sum(cot * mean, axis=0, keepdims=True)
            if slot == 0:
                o_own[...] = mean
            else:
                o_back[...] = mean.astype(jnp.bfloat16)


def merge(first, second):
    top = jnp.maximum(first[0:1], second[0:1])
    w_first = first[1:2] * jnp.exp2((first[0:1] - top) * SCALE2)
    w_second = second[1:2] * jnp.exp2((second[0:1] - top) * SCALE2)
    total = w_first + w_second
    inv = jnp.where(total > 0.0, 1.0 / jnp.maximum(total, 1e-30), 0.0)
    return top, total, w_first * inv, w_second * inv


def bwd_kernel(first, last, blocks, *refs):
    refs = list(refs)
    meta, q_own, q_back, g_own, g_back, stats, far_own, far_back = refs[:8]
    del refs[:8]
    kvs = refs[:blocks]
    del refs[:blocks]
    if not first:
        acc_in = refs.pop(0)
    if last:
        dq_own, dq_back = refs[:2]
        del refs[:2]
    else:
        acc = refs.pop(0)
    dkvs = refs[:blocks]
    del refs[:blocks]
    if last:
        qr, gr, acc = refs
    else:
        qr, gr = refs
    tok, cols = q_own.shape
    width = tok * cols // HEAD
    load_rows((q_own, q_back), qr)
    load_rows((g_own, g_back), gr)
    acc[...] = jnp.zeros_like(acc) if first else acc_in[...]
    logs, deltas = [], []
    for slot, far in ((0, far_own), (1, far_back)):
        near_v = stats[slot]
        far_v = far[...]
        top, total, w_near, w_far = merge(near_v, far_v)
        logs.append(jnp.where(total > 0.0, top * SCALE2 + jnp.log(jnp.maximum(total, 1e-30)) * LOG2E, 0.0))
        deltas.append(w_near * near_v[2:3] + w_far * far_v[2:3])
    for img in range(IMG_DEV):
        slot = meta[img, 0]
        seen = visible_rows(meta[img, 1], tok, width)
        log_total = jnp.where(slot == 0, logs[0], logs[1])
        log_total = jnp.where(seen, log_total, BIG)
        delta = jnp.where(slot == 0, deltas[0], deltas[1])
        for kv, dkv in zip(kvs, dkvs):
            key = kv[img, :, :HEAD]
            part = jnp.exp2(dot(key, qr[slot], NT) * SCALE2 - log_total)
            dweight = dot(kv[img, :, HEAD:], gr[slot], NT)
            ds = (part * (dweight - delta)).astype(jnp.bfloat16)
            dkv[img, :, HEAD:] = dot(part.astype(jnp.bfloat16), gr[slot], NN).astype(jnp.bfloat16)
            dkv[img, :, :HEAD] = (dot(ds, qr[slot], NN) * SCALE).astype(jnp.bfloat16)
            acc[slot] = acc[slot] + dot(key, ds, TN)
    if last:
        for slot, out in ((0, dq_own), (1, dq_back)):
            for h in range(cols // HEAD):
                block = acc[slot, :, h * tok : (h + 1) * tok] * SCALE
                out[:, h * HEAD : (h + 1) * HEAD] = block.T.astype(out.dtype)


def finish_kernel(o_own, o_far, stats, far, dq_own, dq_far, out, dq):
    tok, cols = out.shape
    _, _, w_near, w_far = merge(stats[0], far[...])
    whole = o_own[...] * w_near + o_far[...].astype(jnp.float32) * w_far
    for h in range(cols // HEAD):
        out[:, h * HEAD : (h + 1) * HEAD] = whole[:, h * tok : (h + 1) * tok].T.astype(out.dtype)
    dq[...] = (dq_own[...] + dq_far[...].astype(jnp.float32)).astype(dq.dtype)


VMEM = pl.BlockSpec(memory_space=pltpu.VMEM)
SMEM = pl.BlockSpec(memory_space=pltpu.SMEM)


def call(kernel, name, outs, operands, scratch=(), smem=0, flops=0):
    return pl.pallas_call(
        kernel,
        out_shape=[jax.ShapeDtypeStruct(*o) for o in outs],
        in_specs=[SMEM] * smem + [VMEM] * (len(operands) - smem),
        out_specs=[VMEM] * len(outs),
        scratch_shapes=list(scratch),
        compiler_params=pltpu.CompilerParams(vmem_limit_bytes=32 * 1024 * 1024),
        cost_estimate=pl.CostEstimate(flops=flops, bytes_accessed=1 << 20, transcendentals=0),
        name=name,
    )(*operands)


def hop(value, steps):
    count = lax.axis_size("dp")
    half = count // 2
    pairs = [(s, (s + steps) % count) for s in range(count) if s // half == (s + steps) % count // half]
    return lax.ppermute(value, "dp", pairs)


def over_seam(value, steps):
    count = lax.axis_size("dp")
    half = count // 2
    groups = [list(range(half)), list(range(half, count))]
    source = half - 1 if steps > 0 else 0
    spread = lax.all_to_all(value, "dp", 0, 0, axis_index_groups=groups, tiled=True)
    rows = value.shape[0] // half
    part = spread[source * rows : (source + 1) * rows]
    part = lax.ppermute(part, "dp", [(s, (s + half) % count) for s in range(count)])
    return lax.all_gather(part, "dp", axis_index_groups=groups, tiled=True)


def local(queries, key_value_store, output_gradient, image_ids, image_counts, image_start):
    bf16, f32 = jnp.bfloat16, jnp.float32
    tok, cols = queries.shape
    width = tok * cols // HEAD
    n = lax.axis_size("tensor")
    n_dp = lax.axis_size("dp")
    me_d = lax.axis_index("dp")
    n_img, part_keys, store_cols = key_value_store.shape
    pair = store_cols // n
    piece_shape = ((n_img, part_keys, pair), bf16)
    after = lambda value, *others: lax.optimization_barrier((value, *others))[0]
    block_flops = n_img * part_keys * width * HEAD * 2

    sends = call(functools.partial(split_kernel, "tensor"), "split", [piece_shape] * n, (key_value_store,))
    half = n // 2
    waves = [[half], [half - 1, half + 1], [k for d in range(half - 2, 0, -1) for k in (d, n - d)]]
    kv = {0: sends[0]}
    for i, wave in enumerate(waves):
        for k in wave:
            kv[k] = shift(after(sends[k], kv[half]) if i == 2 else sends[k], "tensor", k)

    both = after(jnp.concatenate([queries, output_gradient], axis=0), kv[half])
    on_seam = me_d % (n_dp // 2) == 0
    both_back = jnp.where(on_seam, over_seam(both, 1), hop(both, 1))
    q_back, g_back = both_back[:tok], both_back[tok:]

    mine = me_d * IMG_DEV + jnp.arange(IMG_DEV, dtype=jnp.int32)
    rows = []
    for slot in range(2):
        sample = (me_d - slot) % n_dp
        ids, starts = image_ids[sample], image_start[sample]
        live = jnp.arange(ids.shape[0], dtype=jnp.int32) < image_counts[sample]
        hit = (ids[None, :] == mine[:, None]) & live[None, :]
        rows.append((jnp.any(hit, axis=1), jnp.sum(jnp.where(hit, starts[None, :], 0), axis=1)))
    slot_of = jnp.where(rows[0][0], 0, 1)
    start_of = jnp.where(rows[0][0], rows[0][1], rows[1][1])
    meta = jnp.stack([slot_of, start_of], axis=1).astype(jnp.int32)

    stat_shape = ((2, 8, width), f32)
    acc_shape = ((2, HEAD, width), f32)
    rows_scratch = pltpu.VMEM((2, width, HEAD), bf16)
    state = ()
    stages = [[0] + waves[0] + waves[1], waves[2][:-2], waves[2][-2:]]
    for i, stage in enumerate(stages):
        first, last = i == 0, i == len(stages) - 1
        operands = (meta, queries, q_back) + ((output_gradient, g_back) if last else ())
        operands += tuple(kv[k] for k in stage) + tuple(state)
        outs = [((HEAD, width), f32), ((HEAD, width), bf16), stat_shape] if last else [acc_shape, stat_shape]
        scratch = [rows_scratch] + ([rows_scratch, pltpu.VMEM(*acc_shape)] if last else [])
        state = call(
            functools.partial(fwd_kernel, first, last, len(stage)), "attend", outs, operands, scratch, 1,
            2 * len(stage) * block_flops,
        )
    o_own, o_back, stats = state

    far_own = shift(stats[1], "dp", -1)
    far_back = shift(stats[0], "dp", 1)

    back = {}
    acc = ()
    parts = [waves[0] + waves[1], waves[2] + [0]]
    for i, stage in enumerate(parts):
        first, last = i == 0, i == len(parts) - 1
        operands = (meta, queries, q_back, output_gradient, g_back, stats, far_own, far_back)
        if not first:
            acc = (after(acc[0], back[half]),)
        operands += tuple(kv[k] for k in stage) + tuple(acc)
        outs = [((tok, cols), f32), ((tok, cols), bf16)] if last else [acc_shape]
        scratch = [rows_scratch] * 2 + ([pltpu.VMEM(*acc_shape)] if last else [])
        got = call(
            functools.partial(bwd_kernel, first, last, len(stage)), "backward", outs + [piece_shape] * len(stage),
            operands, scratch, 1, 5 * len(stage) * block_flops,
        )
        for k, piece in zip(stage, got[len(outs) :]):
            back[k] = shift(piece, "tensor", -k) if k else piece
        acc = got[: len(outs)]
    dq_own, dq_back = acc

    both = jnp.concatenate([o_back.reshape(tok, cols), dq_back], axis=0)
    on_seam = me_d % (n_dp // 2) == n_dp // 2 - 1
    both_far = jnp.where(on_seam, over_seam(both, -1), hop(both, -1))
    o_far, dq_far = both_far[:tok].reshape(HEAD, width), both_far[tok:]

    attended, grad_queries = call(
        finish_kernel, "finish", [((tok, cols), bf16)] * 2, (o_own, o_far, stats, far_own, dq_own, dq_far)
    )
    (grad_kv,) = call(
        functools.partial(join_kernel, "tensor"), "join", [((n_img, part_keys, store_cols), bf16)],
        [after(back[0], attended)] + [back[k] for k in range(1, n)],
    )
    return attended, grad_queries, grad_kv


def solution(mesh):
    return jax.shard_map(
        local,
        mesh=mesh,
        in_specs=(P("dp", "tensor"), P("dp", "tensor", None), P("dp", "tensor"), P(), P(), P()),
        out_specs=(P("dp", "tensor"), P("dp", "tensor"), P("dp", "tensor", None)),
        check_vma=False,
    )
```

time: 270 us -> 286 us (1.059)
  blocking collectives: 0 us -> 47.5 us
  waiting for transfers between devices: 69.6 us -> 50.8 us
  between operations: 16.4 us -> 1.1 us
  Pallas kernels: 16.3 us -> 21.7 us
  local copies, waits for them, and re-layouts: 8.19 us -> 4.01 us
    ppermute x20 -> x16, starting transfers between devices: 156 us -> 78.5 us  [shift(): return lax.ppermute(value, axis, pairs)]
    all_to_all x0 -> x2, starting transfers between devices: none -> 52.1 us  [over_seam(): lax.all_to_all(value, 'dp', 0, 0, axis_index_groups=groups, tiled=True)]
    all_gather x0 -> x2, blocking collectives: none -> 47.5 us  [over_seam(): return lax.all_gather(part, 'dp', axis_index_groups=groups, tiled=True)]
    ppermute x20 -> x16, waiting for transfers between devices: 69.6 us -> 34.1 us  [shift(): return lax.ppermute(value, axis, pairs)]
    ppermute x0 -> x4, starting transfers between devices: none -> 24.4 us  [the longest x2 18.7 us: over_seam(): lax.ppermute(part, 'dp', [(s, (s + half) % count) for s in range(count)])]
    all_to_all x0 -> x2, waiting for transfers between devices: none -> 16.7 us  [over_seam(): lax.all_to_all(value, 'dp', 0, 0, axis_index_groups=groups, tiled=True)]
    pallas_call x3 -> x8, Pallas kernels: 16.3 us -> 21.7 us  [call(): pl.pallas_call(kernel, out_shape=[jax.ShapeDtypeStruct(*o) for o in outs]...]
  transfers between devices with their start and end apart: 20 -> 22, of which waited for: 8 -> 6; matrix products, arithmetic and copies ran while one was open for 3% -> 2% of each run, Pallas kernels for 4% -> 2%
where the time goes in v2:
time: 286 us; the launch traced here: 285 us
  starting transfers between devices  155 us (54%)
  waiting for transfers between devices  50.8 us (18%)
  blocking collectives  47.5 us (17%)
  Pallas kernels  21.7 us (8%)
  other arithmetic  4.8 us (2%)
  local copies, waits for them, and re-layouts  4.01 us (1%)
    ppermute x16, starting transfers between devices, shift(): return lax.ppermute(value, axis, pairs)  78.5 us
    all_to_all x2, starting transfers between devices, over_seam(): lax.all_to_all(value, 'dp', 0, 0, axis_index_groups=groups, tiled=True)  52.1 us
    all_gather x2, blocking collectives, over_seam(): return lax.all_gather(part, 'dp', axis_index_groups=groups, tiled=True)  47.5 us
    ppermute x16, waiting for transfers between devices, shift(): return lax.ppermute(value, axis, pairs)  34.1 us
    pallas_call x8, Pallas kernels, call(): pl.pallas_call(kernel, out_shape=[jax.ShapeDtypeStruct(*o) for o in outs]...  21.7 us
    ppermute x2, starting transfers between devices, over_seam(): lax.ppermute(part, 'dp', [(s, (s + half) % count) for s in range(count)])  18.7 us
    all_to_all x2, waiting for transfers between devices, over_seam(): lax.all_to_all(value, 'dp', 0, 0, axis_index_groups=groups, tiled=True)  16.7 us
  transfers between devices with their start and end apart: 22, of which 6 were waited for; matrix products, arithmetic and copies ran while one was open for 2% of the time, Pallas kernels for 2%

profile of v2, /device:TPU:1, one launch (start us, length us, event | category | flops | bytes accessed | tf_op | source)
XLA Modules:
  0.0 285.0 jit_solution(14855710945892162668)
XLA Ops:
  0.7 1.5 copy-done.1
  2.1 0.2 split.1
  2.4 9.6 %collective-permute-start = (bf16[2,200,256]{2,1,0:T(8,128)(2,1)S(1)}, bf16[2,200,256]{2,1,0:T(8,128)(2,1)S(1)}, u32[]{:S(2)}, u32[]{:S(2)}) collective-permute-start(bf16[2,200,256]{2,1,0:T(8,128)(2,1)S(1)} %get-tuple-element.38), channel_id=1, source_target_pairs={{0,4},{1,5},{2,6},{3,7},{4,0},{5,1},{6,2},{7,3},{8,12},{9,13},{10,... | collective-permute-start | bytes 614408 | tf_op jit(solution)/shard_map/ppermute | solution.py:31
  12.0 6.3 %collective-permute-start.7 = (bf16[2,200,256]{2,1,0:T(8,128)(2,1)S(1)}, bf16[2,200,256]{2,1,0:T(8,128)(2,1)S(1)}, u32[]{:S(2)}, u32[]{:S(2)}) collective-permute-start(bf16[2,200,256]{2,1,0:T(8,128)(2,1)S(1)} %get-tuple-element.49), channel_id=1, source_target_pairs={{0,3},{1,4},{2,5},{3,6},{4,7},{5,0},{6,1},{7,2},{8,11},{9,12},{10,... | collective-permute-start | bytes 614408 | tf_op jit(solution)/shard_map/ppermute | solution.py:31
  18.3 3.8 %collective-permute-start.8 = (bf16[2,200,256]{2,1,0:T(8,128)(2,1)S(1)}, bf16[2,200,256]{2,1,0:T(8,128)(2,1)S(1)}, u32[]{:S(2)}, u32[]{:S(2)}) collective-permute-start(bf16[2,200,256]{2,1,0:T(8,128)(2,1)S(1)} %get-tuple-element.50), channel_id=1, source_target_pairs={{0,5},{1,6},{2,7},{3,0},{4,1},{5,2},{6,3},{7,4},{8,13},{9,14},{10,... | collective-permute-start | bytes 614408 | tf_op jit(solution)/shard_map/ppermute | solution.py:31
  22.2 0.6 fusion.6
  22.8 1.3 iota_compare_fusion
  24.1 0.8 pad_maximum_fusion
  24.9 5.3 %collective-permute-done.refs_4_.refs_8_ = bf16[2,200,256]{2,1,0:T(8,128)(2,1)S(1)} collective-permute-done((bf16[2,200,256]{2,1,0:T(8,128)(2,1)S(1)}, bf16[2,200,256]{2,1,0:T(8,128)(2,1)S(1)}, u32[]{:S(2)}, u32[]{:S(2)}) %collective-permute-start) | collective-permute-done | bytes 204832 | tf_op jit(solution)/shard_map/ppermute | solution.py:31
  30.2 28.1 %all-to-all-start = ((bf16[32,8,1024]{2,1,0:T(8,128)(2,1)}), bf16[32,8,1024]{2,1,0:T(8,128)(2,1)S(1)}, u32[]{:S(2)}, u32[]{:S(2)}) async-start(bf16[32,8,1024]{2,1,0:T(8,128)(2,1)} %bitcast.16), calls=%async_computation | async-start | bytes 1048576 | tf_op jit(solution)/shard_map/all_to_all | solution.py:227
  58.3 0.2 dynamic-slice_reduce_fusion
  58.5 0.2 fusion.1
  58.7 0.2 fusion.3
  58.9 3.5 %collective-permute-start.2 = (bf16[256,1024]{1,0:T(8,128)(2,1)}, bf16[256,1024]{1,0:T(8,128)(2,1)}, u32[]{:S(2)}, u32[]{:S(2)}) collective-permute-start(bf16[256,1024]{1,0:T(8,128)(2,1)} %pad_maximum_fusion), channel_id=1, source_target_pairs={{0,8},{8,16},{16,24},{24,32},{32,40},{40,48},{48,56},{56,64},{64,7... | collective-permute-start | bytes 1572872 | tf_op jit(solution)/shard_map/ppermute | solution.py:219
  62.5 0.1 copy.11
  62.5 0.1 copy.12
  62.6 7.3 %all-to-all-done = bf16[32,8,1024]{2,1,0:T(8,128)(2,1)S(1)} async-done(((bf16[32,8,1024]{2,1,0:T(8,128)(2,1)}), bf16[32,8,1024]{2,1,0:T(8,128)(2,1)S(1)}, u32[]{:S(2)}, u32[]{:S(2)}) %all-to-all-start) | async-done | bytes 524320 | tf_op jit(solution)/shard_map/all_to_all | solution.py:227
  69.9 16.5 %collective-permute-start.1 = (bf16[8,1024]{1,0:T(8,128)(2,1)S(1)}, bf16[8,1024]{1,0:T(8,128)(2,1)S(1)}, u32[]{:S(2)}, u32[]{:S(2)}) collective-permute-start(bf16[8,1024]{1,0:T(8,128)(2,1)S(1)} %slice_bitcast_fusion.3), channel_id=1, source_target_pairs={{0,256},{8,264},{16,272},{24,280},{32,288},{40,296},{48,304},{56,3... | collective-permute-start | bytes 49160 | tf_op jit(solution)/shard_map/ppermute | solution.py:230
  86.4 0.1 pad_add_fusion.refs_0_
  86.5 1.9 collective-permute-start.5
  88.4 0.0 collective-permute-done.1
  88.4 9.1 %collective-permute-start.6 = (bf16[2,200,256]{2,1,0:T(8,128)(2,1)S(1)}, bf16[2,200,256]{2,1,0:T(8,128)(2,1)S(1)}, u32[]{:S(2)}, u32[]{:S(2)}) collective-permute-start(bf16[2,200,256]{2,1,0:T(8,128)(2,1)S(1)} %get-tuple-element.47), channel_id=1, source_target_pairs={{0,6},{1,7},{2,0},{3,1},{4,2},{5,3},{6,4},{7,5},{8,14},{9,15},{10,... | collective-permute-start | bytes 614408 | tf_op jit(solution)/shard_map/ppermute | solution.py:31
  97.5 23.6 %all_gather.6 = bf16[256,1024]{1,0:T(8,128)(2,1)S(1)} all-gather(bf16[8,1024]{1,0:T(8,128)(2,1)S(1)} %collective-permute-done.1), channel_id=1, replica_groups={{0,8,16,24,32,40,48,56,64,72,80,88,96,104,112,120,128,136,144,152,160,1..., dimensions={0}, use_global_device_ids=true | all-gather | bytes 540672 | tf_op jit(solution)/shard_map/all_gather | solution.py:231
  121.1 0.0 collective-permute-done.2
  121.1 1.9 collective-permute-start.3
  123.1 1.1 broadcast_select_fusion.1
  124.2 0.0 collective-permute-done.7.refs_5_.refs_9_
  124.2 10.0 %collective-permute-start.4 = (bf16[2,200,256]{2,1,0:T(8,128)(2,1)S(1)}, bf16[2,200,256]{2,1,0:T(8,128)(2,1)S(1)}, u32[]{:S(2)}, u32[]{:S(2)}) collective-permute-start(bf16[2,200,256]{2,1,0:T(8,128)(2,1)S(1)} %get-tuple-element.43), channel_id=1, source_target_pairs={{0,7},{1,0},{2,1},{3,2},{4,3},{5,4},{6,5},{7,6},{8,15},{9,8},{10,9... | collective-permute-start | bytes 614408 | tf_op jit(solution)/shard_map/ppermute | solution.py:31
  134.2 0.0 collective-permute-done.8.refs_6_.refs_10_
  134.2 3.7 %attend.3 = (f32[2,128,1024]{2,1,0:T(8,128)S(1)}, f32[2,8,1024]{2,1,0:T(8,128)S(1)}) custom-call(s32[2,2]{1,0:T(2,128)S(1)} %pad_add_fusion.refs_0_, bf16[128,1024]{1,0:T(8,128)(2,1)S(1)} %copy-done, bf16[128,1024]{1,0:T(8,128)(2,1)S(1)} %get-tuple-element.82.refs_2_, bf16[2,200,256]{2,1,0:T(8,128)(2,1)S(1)} %get-tuple-element.48.refs_3_.refs_12_, ...), custom_call_target="tpu_custom_call" | custom-call | flops 838860800 | bytes 1048576 | tf_op jit(solution)/shard_map/attend/pallas_call | solution.py:203
  137.9 0.0 collective-permute-done.5.refs_3_.refs_8_
  137.9 2.3 attend.4
  140.2 0.0 collective-permute-done.3.refs_5_.refs_10_
  140.2 0.0 collective-permute-done.4.refs_6_.refs_11_
  140.3 2.5 attend.5
  142.8 3.5 %collective-permute-start.10 = (f32[8,1024]{1,0:T(8,128)S(1)}, f32[8,1024]{1,0:T(8,128)S(1)}, u32[]{:S(2)}, u32[]{:S(2)}) collective-permute-start(f32[8,1024]{1,0:T(8,128)S(1)} %get-tuple-element.83), channel_id=1, source_target_pairs={{0,8},{8,16},{16,24},{24,32},{32,40},{40,48},{48,56},{56,64},{64,7... | collective-permute-start | bytes 98312 | tf_op jit(solution)/shard_map/ppermute | solution.py:31
  146.3 2.1 collective-permute-start.9
  148.4 0.0 collective-permute-done.10.refs_7_
  148.4 3.1 %collective-permute-done.9.refs_6_.far = f32[8,1024]{1,0:T(8,128)S(1)} collective-permute-done((f32[8,1024]{1,0:T(8,128)S(1)}, f32[8,1024]{1,0:T(8,128)S(1)}, u32[]{:S(2)}, u32[]{:S(2)}) %collective-permute-start.9) | collective-permute-done | bytes 32800 | tf_op jit(solution)/shard_map/ppermute | solution.py:31
  151.5 4.1 %backward.2 = (f32[2,128,1024]{2,1,0:T(8,128)S(1)}, bf16[2,200,256]{2,1,0:T(8,128)(2,1)S(1)}, bf16[2,200,256]{2,1,0:T(8,128)(2,1)S(1)}, bf16[2,200,256]{2,1,0:T(8,128)(2,1)S(1)}) custom-call(s32[2,2]{1,0:T(2,128)S(1)} %pad_add_fusion.refs_0_, bf16[128,1024]{1,0:T(8,128)(2,1)S(1)} %copy-done, bf16[128,1024]{1,0:T(8,128)(2,1)S(1)} %get-tuple-element.82.refs_2_, ...), custom_call_target="tpu_custom_call" | custom-call | flops 1572864000 | bytes 1048576 | tf_op jit(solution)/shard_map/backward/pallas_call | solution.py:203
  155.7 1.9 collective-permute-start.11
  157.6 0.7 constant_dynamic-update-slice_fusion.1
  158.3 10.9 %collective-permute-done.11.refs_4_ = bf16[2,200,256]{2,1,0:T(8,128)(2,1)S(1)} collective-permute-done((bf16[2,200,256]{2,1,0:T(8,128)(2,1)S(1)}, bf16[2,200,256]{2,1,0:T(8,128)(2,1)S(1)}, u32[]{:S(2)}, u32[]{:S(2)}) %collective-permute-start.11) | collective-permute-done | bytes 204832 | tf_op jit(solution)/shard_map/ppermute | solution.py:31
  169.2 6.5 %backward.3 = (f32[128,1024]{1,0:T(8,128)S(1)}, bf16[128,1024]{1,0:T(8,128)(2,1)S(1)}, bf16[2,200,256]{2,1,0:T(8,128)(2,1)S(1)}, bf16[2,200,256]{2,1,0:T(8,128)(...) custom-call(s32[2,2]{1,0:T(2,128)S(1)} %pad_add_fusion.refs_0_, ...), custom_call_target="tpu_custom_call" | custom-call | flops 2621440000 | bytes 1048576 | tf_op jit(solution)/shard_map/backward/pallas_call | solution.py:203
  175.7 0.7 constant_dynamic-update-slice_fusion
  176.4 24.1 %all-to-all-start.1 = ((bf16[32,8,1024]{2,1,0:T(8,128)(2,1)}), bf16[32,8,1024]{2,1,0:T(8,128)(2,1)S(1)}, u32[]{:S(2)}, u32[]{:S(2)}) async-start(bf16[32,8,1024]{2,1,0:T(8,128)(2,1)} %bitcast.8), calls=%async_computation.1 | async-start | bytes 1048576 | tf_op jit(solution)/shard_map/all_to_all | solution.py:227
  200.5 2.1 collective-permute-start.13
  202.7 9.4 %all-to-all-done.1 = bf16[32,8,1024]{2,1,0:T(8,128)(2,1)S(1)} async-done(((bf16[32,8,1024]{2,1,0:T(8,128)(2,1)}), bf16[32,8,1024]{2,1,0:T(8,128)(2,1)S(1)}, u32[]{:S(2)}, u32[]{:S(2)}) %all-to-all-start.1) | async-done | bytes 524320 | tf_op jit(solution)/shard_map/all_to_all | solution.py:227
  212.1 2.2 collective-permute-start.12
  214.3 3.9 %collective-permute-start.16 = (bf16[2,200,256]{2,1,0:T(8,128)(2,1)S(1)}, bf16[2,200,256]{2,1,0:T(8,128)(2,1)S(1)}, u32[]{:S(2)}, u32[]{:S(2)}) collective-permute-start(bf16[2,200,256]{2,1,0:T(8,128)(2,1)S(1)} %get-tuple-element.69), channel_id=1, source_target_pairs={{0,5},{1,6},{2,7},{3,0},{4,1},{5,2},{6,3},{7,4},{8,13},{9,14},{10,... | collective-permute-start | bytes 614408 | tf_op jit(solution)/shard_map/ppermute | solution.py:31
  218.2 3.2 %collective-permute-start.17 = (bf16[2,200,256]{2,1,0:T(8,128)(2,1)S(1)}, bf16[2,200,256]{2,1,0:T(8,128)(2,1)S(1)}, u32[]{:S(2)}, u32[]{:S(2)}) collective-permute-start(bf16[2,200,256]{2,1,0:T(8,128)(2,1)S(1)} %get-tuple-element.70), channel_id=1, source_target_pairs={{0,3},{1,4},{2,5},{3,6},{4,7},{5,0},{6,1},{7,2},{8,11},{9,12},{10,... | collective-permute-start | bytes 614408 | tf_op jit(solution)/shard_map/ppermute | solution.py:31
  221.4 13.0 %collective-permute-start.14 = (bf16[2,200,256]{2,1,0:T(8,128)(2,1)S(1)}, bf16[2,200,256]{2,1,0:T(8,128)(2,1)S(1)}, u32[]{:S(2)}, u32[]{:S(2)}) collective-permute-start(bf16[2,200,256]{2,1,0:T(8,128)(2,1)S(1)} %get-tuple-element.67), channel_id=1, source_target_pairs={{0,7},{1,0},{2,1},{3,2},{4,3},{5,4},{6,5},{7,6},{8,15},{9,8},{10,9... | collective-permute-start | bytes 614408 | tf_op jit(solution)/shard_map/ppermute | solution.py:31
  234.4 0.0 collective-permute-done.12
  234.4 1.9 collective-permute-start.15
  236.3 23.9 %all_gather.7 = bf16[256,1024]{1,0:T(8,128)(2,1)S(1)} all-gather(bf16[8,1024]{1,0:T(8,128)(2,1)S(1)} %collective-permute-done.12), channel_id=1, replica_groups={{0,8,16,24,32,40,48,56,64,72,80,88,96,104,112,120,128,136,144,152,160,1..., dimensions={0}, use_global_device_ids=true | all-gather | bytes 540672 | tf_op jit(solution)/shard_map/all_gather | solution.py:231
  260.2 0.0 collective-permute-done.13
  260.2 4.5 %collective-permute-start.18 = (bf16[2,200,256]{2,1,0:T(8,128)(2,1)S(1)}, bf16[2,200,256]{2,1,0:T(8,128)(2,1)S(1)}, u32[]{:S(2)}, u32[]{:S(2)}) collective-permute-start(bf16[2,200,256]{2,1,0:T(8,128)(2,1)S(1)} %get-tuple-element.71), channel_id=1, source_target_pairs={{0,2},{1,3},{2,4},{3,5},{4,6},{5,7},{6,0},{7,1},{8,10},{9,11},{10,... | collective-permute-start | bytes 614408 | tf_op jit(solution)/shard_map/ppermute | solution.py:31
  264.7 1.1 broadcast_select_fusion
  265.8 1.9 collective-permute-start.19
  267.8 1.0 finish.1
  268.8 0.0 collective-permute-done.15.refs_2_
  268.8 14.8 %collective-permute-done.18.refs_6_ = bf16[2,200,256]{2,1,0:T(8,128)(2,1)S(1)} collective-permute-done((bf16[2,200,256]{2,1,0:T(8,128)(2,1)S(1)}, bf16[2,200,256]{2,1,0:T(8,128)(2,1)S(1)}, u32[]{:S(2)}, u32[]{:S(2)}) %collective-permute-start.18) | collective-permute-done | bytes 204832 | tf_op jit(solution)/shard_map/ppermute | solution.py:31
  283.6 0.0 collective-permute-done.19.refs_7_
  283.6 1.4 join.1
  (22 shorter events, 0.1 us)
Async XLA Ops:
  0.6 23.4 %copy-start = (bf16[128,1024]{1,0:T(8,128)(2,1)S(1)}, bf16[128,1024]{1,0:T(8,128)(2,1)}, u32[]{:S(2)}) copy-start(bf16[128,1024]{1,0:T(8,128)(2,1)} %refs_1_.9) | copy-start | bytes 786436
  0.6 1.5 copy-start.1
  2.1 20.0 %copy-start.5 = (s32[64]{0:T(128)S(1)}, s32[64]{0:T(128)}, u32[]{:S(2)}) copy-start(s32[64]{0:T(128)} %param.10) | copy-start | bytes 772
  2.1 22.0 %copy-start.2 = (bf16[128,1024]{1,0:T(8,128)(2,1)S(1)}, bf16[128,1024]{1,0:T(8,128)(2,1)}, u32[]{:S(2)}) copy-start(bf16[128,1024]{1,0:T(8,128)(2,1)} %refs_3_.5) | copy-start | bytes 786436
  2.1 56.2 %copy-start.3 = (s32[64,4]{0,1:T(4,128)S(1)}, s32[64,4]{0,1:T(4,128)}, u32[]{:S(2)}) copy-start(s32[64,4]{0,1:T(4,128)} %param.11) | copy-start | bytes 3076
  2.1 56.2 %copy-start.4 = (s32[64,4]{0,1:T(4,128)S(1)}, s32[64,4]{0,1:T(4,128)}, u32[]{:S(2)}) copy-start(s32[64,4]{0,1:T(4,128)} %param.9) | copy-start | bytes 3076
  2.4 27.8 %collective-permute-start = (bf16[2,200,256]{2,1,0:T(8,128)(2,1)S(1)}, bf16[2,200,256]{2,1,0:T(8,128)(2,1)S(1)}, u32[]{:S(2)}, u32[]{:S(2)}) collective-permute-start(bf16[2,200,256]{2,1,0:T(8,128)(2,1)S(1)} %get-tuple-element.38), channel_id=1, source_target_pairs={{0,4},{1,5},{2,6},{3,7},{4,0},{5,1},{6,2},{7,3},{8,12},{9,13},{10,... | collective-permute-start | bytes 614408 | tf_op jit(solution)/shard_map/ppermute | solution.py:31
  12.0 112.1 %collective-permute-start.7 = (bf16[2,200,256]{2,1,0:T(8,128)(2,1)S(1)}, bf16[2,200,256]{2,1,0:T(8,128)(2,1)S(1)}, u32[]{:S(2)}, u32[]{:S(2)}) collective-permute-start(bf16[2,200,256]{2,1,0:T(8,128)(2,1)S(1)} %get-tuple-element.49), channel_id=1, source_target_pairs={{0,3},{1,4},{2,5},{3,6},{4,7},{5,0},{6,1},{7,2},{8,11},{9,12},{10,... | collective-permute-start | bytes 614408 | tf_op jit(solution)/shard_map/ppermute | solution.py:31
  18.3 115.9 %collective-permute-start.8 = (bf16[2,200,256]{2,1,0:T(8,128)(2,1)S(1)}, bf16[2,200,256]{2,1,0:T(8,128)(2,1)S(1)}, u32[]{:S(2)}, u32[]{:S(2)}) collective-permute-start(bf16[2,200,256]{2,1,0:T(8,128)(2,1)S(1)} %get-tuple-element.50), channel_id=1, source_target_pairs={{0,5},{1,6},{2,7},{3,0},{4,1},{5,2},{6,3},{7,4},{8,13},{9,14},{10,... | collective-permute-start | bytes 614408 | tf_op jit(solution)/shard_map/ppermute | solution.py:31
  30.2 39.7 %all-to-all-start = ((bf16[32,8,1024]{2,1,0:T(8,128)(2,1)}), bf16[32,8,1024]{2,1,0:T(8,128)(2,1)S(1)}, u32[]{:S(2)}, u32[]{:S(2)}) async-start(bf16[32,8,1024]{2,1,0:T(8,128)(2,1)} %bitcast.16), calls=%async_computation | async-start | bytes 1048576 | tf_op jit(solution)/shard_map/all_to_all | solution.py:227
  58.9 62.2 %collective-permute-start.2 = (bf16[256,1024]{1,0:T(8,128)(2,1)}, bf16[256,1024]{1,0:T(8,128)(2,1)}, u32[]{:S(2)}, u32[]{:S(2)}) collective-permute-start(bf16[256,1024]{1,0:T(8,128)(2,1)} %pad_maximum_fusion), channel_id=1, source_target_pairs={{0,8},{8,16},{16,24},{24,32},{32,40},{40,48},{48,56},{56,64},{64,7... | collective-permute-start | bytes 1572872 | tf_op jit(solution)/shard_map/ppermute | solution.py:219
  69.9 18.5 %collective-permute-start.1 = (bf16[8,1024]{1,0:T(8,128)(2,1)S(1)}, bf16[8,1024]{1,0:T(8,128)(2,1)S(1)}, u32[]{:S(2)}, u32[]{:S(2)}) collective-permute-start(bf16[8,1024]{1,0:T(8,128)(2,1)S(1)} %slice_bitcast_fusion.3), channel_id=1, source_target_pairs={{0,256},{8,264},{16,272},{24,280},{32,288},{40,296},{48,304},{56,3... | collective-permute-start | bytes 49160 | tf_op jit(solution)/shard_map/ppermute | solution.py:230
  86.5 51.4 %collective-permute-start.5 = (bf16[2,200,256]{2,1,0:T(8,128)(2,1)S(1)}, bf16[2,200,256]{2,1,0:T(8,128)(2,1)S(1)}, u32[]{:S(2)}, u32[]{:S(2)}) collective-permute-start(bf16[2,200,256]{2,1,0:T(8,128)(2,1)S(1)} %get-tuple-element.45), channel_id=1, source_target_pairs={{0,2},{1,3},{2,4},{3,5},{4,6},{5,7},{6,0},{7,1},{8,10},{9,11},{10,... | collective-permute-start | bytes 614408 | tf_op jit(solution)/shard_map/ppermute | solution.py:31
  88.4 49.5 %collective-permute-start.6 = (bf16[2,200,256]{2,1,0:T(8,128)(2,1)S(1)}, bf16[2,200,256]{2,1,0:T(8,128)(2,1)S(1)}, u32[]{:S(2)}, u32[]{:S(2)}) collective-permute-start(bf16[2,200,256]{2,1,0:T(8,128)(2,1)S(1)} %get-tuple-element.47), channel_id=1, source_target_pairs={{0,6},{1,7},{2,0},{3,1},{4,2},{5,3},{6,4},{7,5},{8,14},{9,15},{10,... | collective-permute-start | bytes 614408 | tf_op jit(solution)/shard_map/ppermute | solution.py:31
  121.1 19.1 %collective-permute-start.3 = (bf16[2,200,256]{2,1,0:T(8,128)(2,1)S(1)}, bf16[2,200,256]{2,1,0:T(8,128)(2,1)S(1)}, u32[]{:S(2)}, u32[]{:S(2)}) collective-permute-start(bf16[2,200,256]{2,1,0:T(8,128)(2,1)S(1)} %get-tuple-element.41), channel_id=1, source_target_pairs={{0,1},{1,2},{2,3},{3,4},{4,5},{5,6},{6,7},{7,0},{8,9},{9,10},{10,1... | collective-permute-start | bytes 614408 | tf_op jit(solution)/shard_map/ppermute | solution.py:31
  124.2 16.1 %collective-permute-start.4 = (bf16[2,200,256]{2,1,0:T(8,128)(2,1)S(1)}, bf16[2,200,256]{2,1,0:T(8,128)(2,1)S(1)}, u32[]{:S(2)}, u32[]{:S(2)}) collective-permute-start(bf16[2,200,256]{2,1,0:T(8,128)(2,1)S(1)} %get-tuple-element.43), channel_id=1, source_target_pairs={{0,7},{1,0},{2,1},{3,2},{4,3},{5,4},{6,5},{7,6},{8,15},{9,8},{10,9... | collective-permute-start | bytes 614408 | tf_op jit(solution)/shard_map/ppermute | solution.py:31
  142.8 5.6 %collective-permute-start.10 = (f32[8,1024]{1,0:T(8,128)S(1)}, f32[8,1024]{1,0:T(8,128)S(1)}, u32[]{:S(2)}, u32[]{:S(2)}) collective-permute-start(f32[8,1024]{1,0:T(8,128)S(1)} %get-tuple-element.83), channel_id=1, source_target_pairs={{0,8},{8,16},{16,24},{24,32},{32,40},{40,48},{48,56},{56,64},{64,7... | collective-permute-start | bytes 98312 | tf_op jit(solution)/shard_map/ppermute | solution.py:31
  146.3 5.2 %collective-permute-start.9 = (f32[8,1024]{1,0:T(8,128)S(1)}, f32[8,1024]{1,0:T(8,128)S(1)}, u32[]{:S(2)}, u32[]{:S(2)}) collective-permute-start(f32[8,1024]{1,0:T(8,128)S(1)} %get-tuple-element.84), channel_id=1, source_target_pairs={{0,504},{8,0},{16,8},{24,16},{32,24},{40,32},{48,40},{56,48},{64,5... | collective-permute-start | bytes 98312 | tf_op jit(solution)/shard_map/ppermute | solution.py:31
  155.7 13.5 %collective-permute-start.11 = (bf16[2,200,256]{2,1,0:T(8,128)(2,1)S(1)}, bf16[2,200,256]{2,1,0:T(8,128)(2,1)S(1)}, u32[]{:S(2)}, u32[]{:S(2)}) collective-permute-start(bf16[2,200,256]{2,1,0:T(8,128)(2,1)S(1)} %get-tuple-element.59), channel_id=1, source_target_pairs={{0,4},{1,5},{2,6},{3,7},{4,0},{5,1},{6,2},{7,3},{8,12},{9,13},{10,... | collective-permute-start | bytes 614408 | tf_op jit(solution)/shard_map/ppermute | solution.py:31
  176.4 35.6 %all-to-all-start.1 = ((bf16[32,8,1024]{2,1,0:T(8,128)(2,1)}), bf16[32,8,1024]{2,1,0:T(8,128)(2,1)S(1)}, u32[]{:S(2)}, u32[]{:S(2)}) async-start(bf16[32,8,1024]{2,1,0:T(8,128)(2,1)} %bitcast.8), calls=%async_computation.1 | async-start | bytes 1048576 | tf_op jit(solution)/shard_map/all_to_all | solution.py:227
  200.5 59.7 %collective-permute-start.13 = (bf16[256,1024]{1,0:T(8,128)(2,1)}, bf16[256,1024]{1,0:T(8,128)(2,1)}, u32[]{:S(2)}, u32[]{:S(2)}) collective-permute-start(bf16[256,1024]{1,0:T(8,128)(2,1)} %constant_dynamic-update-slice_fusion), channel_id=1, source_target_pairs={{8,0},{16,8},{24,16},{32,24},{40,32},{48,40},{56,48},{64,56},{72,6... | collective-permute-start | bytes 1572872 | tf_op jit(solution)/shard_map/ppermute | solution.py:219
  212.1 22.3 %collective-permute-start.12 = (bf16[8,1024]{1,0:T(8,128)(2,1)S(1)}, bf16[8,1024]{1,0:T(8,128)(2,1)S(1)}, u32[]{:S(2)}, u32[]{:S(2)}) collective-permute-start(bf16[8,1024]{1,0:T(8,128)(2,1)S(1)} %slice_bitcast_fusion.2), channel_id=1, source_target_pairs={{0,256},{8,264},{16,272},{24,280},{32,288},{40,296},{48,304},{56,3... | collective-permute-start | bytes 49160 | tf_op jit(solution)/shard_map/ppermute | solution.py:230
  214.3 51.6 %collective-permute-start.16 = (bf16[2,200,256]{2,1,0:T(8,128)(2,1)S(1)}, bf16[2,200,256]{2,1,0:T(8,128)(2,1)S(1)}, u32[]{:S(2)}, u32[]{:S(2)}) collective-permute-start(bf16[2,200,256]{2,1,0:T(8,128)(2,1)S(1)} %get-tuple-element.69), channel_id=1, source_target_pairs={{0,5},{1,6},{2,7},{3,0},{4,1},{5,2},{6,3},{7,4},{8,13},{9,14},{10,... | collective-permute-start | bytes 614408 | tf_op jit(solution)/shard_map/ppermute | solution.py:31
  218.2 50.7 %collective-permute-start.17 = (bf16[2,200,256]{2,1,0:T(8,128)(2,1)S(1)}, bf16[2,200,256]{2,1,0:T(8,128)(2,1)S(1)}, u32[]{:S(2)}, u32[]{:S(2)}) collective-permute-start(bf16[2,200,256]{2,1,0:T(8,128)(2,1)S(1)} %get-tuple-element.70), channel_id=1, source_target_pairs={{0,3},{1,4},{2,5},{3,6},{4,7},{5,0},{6,1},{7,2},{8,11},{9,12},{10,... | collective-permute-start | bytes 614408 | tf_op jit(solution)/shard_map/ppermute | solution.py:31
  221.4 47.4 %collective-permute-start.14 = (bf16[2,200,256]{2,1,0:T(8,128)(2,1)S(1)}, bf16[2,200,256]{2,1,0:T(8,128)(2,1)S(1)}, u32[]{:S(2)}, u32[]{:S(2)}) collective-permute-start(bf16[2,200,256]{2,1,0:T(8,128)(2,1)S(1)} %get-tuple-element.67), channel_id=1, source_target_pairs={{0,7},{1,0},{2,1},{3,2},{4,3},{5,4},{6,5},{7,6},{8,15},{9,8},{10,9... | collective-permute-start | bytes 614408 | tf_op jit(solution)/shard_map/ppermute | solution.py:31
  234.4 34.5 %collective-permute-start.15 = (bf16[2,200,256]{2,1,0:T(8,128)(2,1)S(1)}, bf16[2,200,256]{2,1,0:T(8,128)(2,1)S(1)}, u32[]{:S(2)}, u32[]{:S(2)}) collective-permute-start(bf16[2,200,256]{2,1,0:T(8,128)(2,1)S(1)} %get-tuple-element.68), channel_id=1, source_target_pairs={{0,6},{1,7},{2,0},{3,1},{4,2},{5,3},{6,4},{7,5},{8,14},{9,15},{10,... | collective-permute-start | bytes 614408 | tf_op jit(solution)/shard_map/ppermute | solution.py:31
  260.2 23.4 %collective-permute-start.18 = (bf16[2,200,256]{2,1,0:T(8,128)(2,1)S(1)}, bf16[2,200,256]{2,1,0:T(8,128)(2,1)S(1)}, u32[]{:S(2)}, u32[]{:S(2)}) collective-permute-start(bf16[2,200,256]{2,1,0:T(8,128)(2,1)S(1)} %get-tuple-element.71), channel_id=1, source_target_pairs={{0,2},{1,3},{2,4},{3,5},{4,6},{5,7},{6,0},{7,1},{8,10},{9,11},{10,... | collective-permute-start | bytes 614408 | tf_op jit(solution)/shard_map/ppermute | solution.py:31
  265.8 17.7 %collective-permute-start.19 = (bf16[2,200,256]{2,1,0:T(8,128)(2,1)S(1)}, bf16[2,200,256]{2,1,0:T(8,128)(2,1)S(1)}, u32[]{:S(2)}, u32[]{:S(2)}) collective-permute-start(bf16[2,200,256]{2,1,0:T(8,128)(2,1)S(1)} %get-tuple-element.72), channel_id=1, source_target_pairs={{0,1},{1,2},{2,3},{3,4},{4,5},{5,6},{6,7},{7,0},{8,9},{9,10},{10,1... | collective-permute-start | bytes 614408 | tf_op jit(solution)/shard_map/ppermute | solution.py:31

commit v3 on v2

--- a/solution.py
+++ b/solution.py
@@ -15,6 +15,7 @@
 LOG2E = 1.4426950408889634
 SCALE = HEAD ** (-0.5)
 SCALE2 = SCALE * LOG2E
+WINDOW = 4
 
 NT = (((1,), (1,)), ((), ()))
 TN = (((0,), (0,)), ((), ()))
@@ -54,10 +55,11 @@
         piece[...] = store[:, :, pl.ds(pl.multiple_of(col, width), width)]
 
 
-def join_kernel(axis, *refs):
-    pieces, out = refs[:-1], refs[-1]
-    n, width = len(pieces), pieces[0].shape[-1]
-    for k, piece in enumerate(pieces):
+def join_kernel(axis, shifts, *refs):
+    pieces, out = refs[-1 - len(shifts) : -1], refs[-1]
+    width = pieces[0].shape[-1]
+    n = out.shape[-1] // width
+    for k, piece in zip(shifts, pieces):
         col = lax.rem(lax.axis_index(axis) + k, n) * width
         out[:, :, pl.ds(pl.multiple_of(col, width), width)] = piece[...]
 
@@ -199,7 +201,7 @@
 SMEM = pl.BlockSpec(memory_space=pltpu.SMEM)
 
 
-def call(kernel, name, outs, operands, scratch=(), smem=0, flops=0):
+def call(kernel, name, outs, operands, scratch=(), smem=0, flops=0, aliases=None):
     return pl.pallas_call(
         kernel,
         out_shape=[jax.ShapeDtypeStruct(*o) for o in outs],
@@ -208,27 +210,47 @@
         scratch_shapes=list(scratch),
         compiler_params=pltpu.CompilerParams(vmem_limit_bytes=32 * 1024 * 1024),
         cost_estimate=pl.CostEstimate(flops=flops, bytes_accessed=1 << 20, transcendentals=0),
+        input_output_aliases=aliases or {},
         name=name,
     )(*operands)
 
 
-def hop(value, steps):
+def after(value, *others):
+    return lax.optimization_barrier((value, *others))[0]
+
+
+def within(value, steps):
     count = lax.axis_size("dp")
     half = count // 2
-    pairs = [(s, (s + steps) % count) for s in range(count) if s // half == (s + steps) % count // half]
-    return lax.ppermute(value, "dp", pairs)
-
-
-def over_seam(value, steps):
-    count = lax.axis_size("dp")
+    inside = [(s, s + steps) for s in range(count) if s // half == (s + steps) // half and s + steps >= 0]
+    return lax.ppermute(value, "dp", inside)
+
+
+def seam_legs(steps):
+    count, n = lax.axis_size("dp"), lax.axis_size("tensor")
     half = count // 2
-    groups = [list(range(half)), list(range(half, count))]
-    source = half - 1 if steps > 0 else 0
-    spread = lax.all_to_all(value, "dp", 0, 0, axis_index_groups=groups, tiled=True)
-    rows = value.shape[0] // half
-    part = spread[source * rows : (source + 1) * rows]
-    part = lax.ppermute(part, "dp", [(s, (s + half) % count) for s in range(count)])
-    return lax.all_gather(part, "dp", axis_index_groups=groups, tiled=True)
+    source, near = (half - 1, 0) if steps > 0 else (0, half - 1)
+    relays = [31, 0, 25, 7, 29, 23, 3, 9] if half == 32 and n == 8 else [half - 1] * n
+
+    def send(part, pairs):
+        return lax.ppermute(part, ("dp", "tensor"), [(d * n + t, e * n + t) for d, e, t in pairs])
+
+    fan = [(source + base, relays[t] + base, t) for base in (0, half) for t in range(n)]
+    over = [(relays[t] + base, near + half - base, t) for base in (0, half) for t in range(n)]
+    return lambda part: send(part, fan), lambda part: send(part, over)
+
+
+def exchange(pieces, order, sign, both, steps):
+    half = lax.axis_size("dp") // 2
+    near = 0 if steps > 0 else half - 1
+    first_leg, second_leg = seam_legs(steps)
+    fan = first_leg(both)
+    got = {}
+    for i, k in enumerate(order):
+        gate = fan if i < WINDOW else got[order[i - WINDOW]]
+        got[k] = shift(after(pieces[k], gate), "tensor", sign * k) if k else pieces[k]
+    both = jnp.where(lax.axis_index("dp") % half == near, second_leg(fan), within(both, steps))
+    return got, both
 
 
 def local(queries, key_value_store, output_gradient, image_ids, image_counts, image_start):
@@ -241,21 +263,12 @@
     n_img, part_keys, store_cols = key_value_store.shape
     pair = store_cols // n
     piece_shape = ((n_img, part_keys, pair), bf16)
-    after = lambda value, *others: lax.optimization_barrier((value, *others))[0]
-    block_flops = n_img * part_keys * width * HEAD * 2
 
     sends = call(functools.partial(split_kernel, "tensor"), "split", [piece_shape] * n, (key_value_store,))
-    half = n // 2
-    waves = [[half], [half - 1, half + 1], [k for d in range(half - 2, 0, -1) for k in (d, n - d)]]
-    kv = {0: sends[0]}
-    for i, wave in enumerate(waves):
-        for k in wave:
-            kv[k] = shift(after(sends[k], kv[half]) if i == 2 else sends[k], "tensor", k)
-
-    both = after(jnp.concatenate([queries, output_gradient], axis=0), kv[half])
-    on_seam = me_d % (n_dp // 2) == 0
-    both_back = jnp.where(on_seam, over_seam(both, 1), hop(both, 1))
-    q_back, g_back = both_back[:tok], both_back[tok:]
+    order = [k for d in range(n // 2, 0, -1) for k in sorted({d, n - d})] + [0]
+    both = jnp.concatenate([queries, output_gradient], axis=0)
+    kv, both = exchange(sends, order, 1, both, 1)
+    q_back, g_back = both[:tok], both[tok:]
 
     mine = me_d * IMG_DEV + jnp.arange(IMG_DEV, dtype=jnp.int32)
     rows = []
@@ -272,54 +285,32 @@
     stat_shape = ((2, 8, width), f32)
     acc_shape = ((2, HEAD, width), f32)
     rows_scratch = pltpu.VMEM((2, width, HEAD), bf16)
-    state = ()
-    stages = [[0] + waves[0] + waves[1], waves[2][:-2], waves[2][-2:]]
-    for i, stage in enumerate(stages):
-        first, last = i == 0, i == len(stages) - 1
-        operands = (meta, queries, q_back) + ((output_gradient, g_back) if last else ())
-        operands += tuple(kv[k] for k in stage) + tuple(state)
-        outs = [((HEAD, width), f32), ((HEAD, width), bf16), stat_shape] if last else [acc_shape, stat_shape]
-        scratch = [rows_scratch] + ([rows_scratch, pltpu.VMEM(*acc_shape)] if last else [])
-        state = call(
-            functools.partial(fwd_kernel, first, last, len(stage)), "attend", outs, operands, scratch, 1,
-            2 * len(stage) * block_flops,
-        )
-    o_own, o_back, stats = state
+    o_own, o_back, stats = call(
+        functools.partial(fwd_kernel, True, True, n), "attend",
+        [((HEAD, width), f32), ((HEAD, width), bf16), stat_shape],
+        (meta, queries, q_back, output_gradient, g_back) + tuple(kv[k] for k in order),
+        [rows_scratch, rows_scratch, pltpu.VMEM(*acc_shape)], 1,
+    )
 
     far_own = shift(stats[1], "dp", -1)
     far_back = shift(stats[0], "dp", 1)
 
-    back = {}
-    acc = ()
-    parts = [waves[0] + waves[1], waves[2] + [0]]
-    for i, stage in enumerate(parts):
-        first, last = i == 0, i == len(parts) - 1
-        operands = (meta, queries, q_back, output_gradient, g_back, stats, far_own, far_back)
-        if not first:
-            acc = (after(acc[0], back[half]),)
-        operands += tuple(kv[k] for k in stage) + tuple(acc)
-        outs = [((tok, cols), f32), ((tok, cols), bf16)] if last else [acc_shape]
-        scratch = [rows_scratch] * 2 + ([pltpu.VMEM(*acc_shape)] if last else [])
-        got = call(
-            functools.partial(bwd_kernel, first, last, len(stage)), "backward", outs + [piece_shape] * len(stage),
-            operands, scratch, 1, 5 * len(stage) * block_flops,
-        )
-        for k, piece in zip(stage, got[len(outs) :]):
-            back[k] = shift(piece, "tensor", -k) if k else piece
-        acc = got[: len(outs)]
-    dq_own, dq_back = acc
-
+    operands = (meta, queries, q_back, output_gradient, g_back, stats, far_own, far_back)
+    dq_own, dq_back, *pieces = call(
+        functools.partial(bwd_kernel, True, True, n), "backward",
+        [((tok, cols), f32), ((tok, cols), bf16)] + [piece_shape] * n,
+        operands + tuple(kv[k] for k in order), [rows_scratch] * 2 + [pltpu.VMEM(*acc_shape)], 1,
+    )
     both = jnp.concatenate([o_back.reshape(tok, cols), dq_back], axis=0)
-    on_seam = me_d % (n_dp // 2) == n_dp // 2 - 1
-    both_far = jnp.where(on_seam, over_seam(both, -1), hop(both, -1))
-    o_far, dq_far = both_far[:tok].reshape(HEAD, width), both_far[tok:]
+    back, both = exchange(dict(zip(order, pieces)), order, -1, both, -1)
+    o_far, dq_far = both[:tok].reshape(HEAD, width), both[tok:]
 
     attended, grad_queries = call(
         finish_kernel, "finish", [((tok, cols), bf16)] * 2, (o_own, o_far, stats, far_own, dq_own, dq_far)
     )
     (grad_kv,) = call(
-        functools.partial(join_kernel, "tensor"), "join", [((n_img, part_keys, store_cols), bf16)],
-        [after(back[0], attended)] + [back[k] for k in range(1, n)],
+        functools.partial(join_kernel, "tensor", range(n)), "join", [((n_img, part_keys, store_cols), bf16)],
+        [back[k] for k in range(n)],
     )
     return attended, grad_queries, grad_kv
 

time: 286 us -> 238 us (0.83)
  blocking collectives: 47.5 us -> 0 us
  waiting for transfers between devices: 50.8 us -> 66.5 us
  starting transfers between devices: 155 us -> 141 us
  local copies, waits for them, and re-layouts: 4.01 us -> 7.34 us
  Pallas kernels: 21.7 us -> 18.7 us
    all_to_all x2 -> x0, starting transfers between devices: 52.1 us -> none  [over_seam(): lax.all_to_all(value, 'dp', 0, 0, axis_index_groups=groups, tiled=True)]
    all_gather x2 -> x0, blocking collectives: 47.5 us -> none  [over_seam(): return lax.all_gather(part, 'dp', axis_index_groups=groups, tiled=True)]
    ppermute x16, waiting for transfers between devices: 34.1 us -> 66.5 us  [shift(): return lax.ppermute(value, axis, pairs)]
    ppermute x4 -> x6, starting transfers between devices: 24.4 us -> 46.2 us  [the longest x2 40.3 us: within(): return lax.ppermute(value, 'dp', inside)]
    all_to_all x2 -> x0, waiting for transfers between devices: 16.7 us -> none  [over_seam(): lax.all_to_all(value, 'dp', 0, 0, axis_index_groups=groups, tiled=True)]
    ppermute x16, starting transfers between devices: 78.5 us -> 94.4 us  [shift(): return lax.ppermute(value, axis, pairs)]
    pallas_call x8 -> x5, Pallas kernels: 21.7 us -> 18.7 us  [call(): pl.pallas_call(kernel, out_shape=[jax.ShapeDtypeStruct(*o) for o in outs]...]
  transfers between devices with their start and end apart: 22 -> 22, of which waited for: 6 -> 7; matrix products, arithmetic and copies ran while one was open for 2% -> 2% of each run, Pallas kernels for 2% -> 1%
where the time goes in v3:
time: 238 us; the launch traced here: 237 us
  starting transfers between devices  141 us (59%)
  waiting for transfers between devices  66.5 us (28%)
  Pallas kernels  18.7 us (8%)
  local copies, waits for them, and re-layouts  7.34 us (3%)
  other arithmetic  2.94 us (1%)
    ppermute x16, starting transfers between devices, shift(): return lax.ppermute(value, axis, pairs)  94.4 us
    ppermute x16, waiting for transfers between devices, shift(): return lax.ppermute(value, axis, pairs)  66.5 us
    ppermute x2, starting transfers between devices, within(): return lax.ppermute(value, 'dp', inside)  40.3 us
    pallas_call x5, Pallas kernels, call(): pl.pallas_call(kernel, out_shape=[jax.ShapeDtypeStruct(*o) for o in outs]...  18.7 us
    ppermute x4, starting transfers between devices, send(): lax.ppermute(part, ('dp', 'tensor'), [(d * n + t, e * n + t) for d, e, t...  5.85 us
  transfers between devices with their start and end apart: 22, of which 7 were waited for; matrix products, arithmetic and copies ran while one was open for 2% of the time, Pallas kernels for 1%

profile of v3, /device:TPU:1, one launch (start us, length us, event | category | flops | bytes accessed | tf_op | source)
XLA Modules:
  0.0 237.1 jit_solution(8437994424770828544)
XLA Ops:
  0.7 1.7 constant_dynamic-update-slice_fusion.1
  2.3 1.7 constant_dynamic-update-slice_fusion
  4.0 1.5 collective-permute-start
  5.5 4.5 %collective-permute-start.2 = (bf16[256,1024]{1,0:T(8,128)(2,1)}, bf16[256,1024]{1,0:T(8,128)(2,1)S(1)}, u32[]{:S(2)}, u32[]{:S(2)}) collective-permute-start(bf16[256,1024]{1,0:T(8,128)(2,1)} %constant_dynamic-update-slice_fusion), channel_id=1, source_target_pairs={{0,8},{8,16},{16,24},{24,32},{32,40},{40,48},{48,56},{56,64},{64,7... | collective-permute-start | bytes 1572872 | tf_op jit(solution)/shard_map/ppermute | solution.py:226
  10.0 0.0 copy-start.2
  10.0 1.4 copy-done.2
  11.4 0.2 split.1
  11.7 0.0 copy-start
  11.7 0.0 copy-start.1
  11.7 0.6 fusion.6
  12.3 0.2 dynamic-slice_reduce_fusion
  12.6 1.3 iota_compare_fusion
  13.9 0.0 collective-permute-done
  13.9 1.5 collective-permute-start.1
  15.3 0.2 fusion.1
  15.5 0.2 fusion.3
  15.7 10.2 %collective-permute-start.5 = (bf16[2,200,256]{2,1,0:T(8,128)(2,1)S(1)}, bf16[2,200,256]{2,1,0:T(8,128)(2,1)S(1)}, u32[]{:S(2)}, u32[]{:S(2)}) collective-permute-start(bf16[2,200,256]{2,1,0:T(8,128)(2,1)S(1)} %get-tuple-element.45), channel_id=1, source_target_pairs={{0,5},{1,6},{2,7},{3,0},{4,1},{5,2},{6,3},{7,4},{8,13},{9,14},{10,... | collective-permute-start | bytes 614408 | tf_op jit(solution)/shard_map/ppermute | solution.py:32
  25.9 1.9 collective-permute-start.4
  27.8 4.9 %collective-permute-start.3 = (bf16[2,200,256]{2,1,0:T(8,128)(2,1)S(1)}, bf16[2,200,256]{2,1,0:T(8,128)(2,1)S(1)}, u32[]{:S(2)}, u32[]{:S(2)}) collective-permute-start(bf16[2,200,256]{2,1,0:T(8,128)(2,1)S(1)} %get-tuple-element.41), channel_id=1, source_target_pairs={{0,4},{1,5},{2,6},{3,7},{4,0},{5,1},{6,2},{7,3},{8,12},{9,13},{10,... | collective-permute-start | bytes 614408 | tf_op jit(solution)/shard_map/ppermute | solution.py:32
  32.7 0.1 copy.11
  32.8 0.1 copy.12
  32.9 0.1 pad_add_fusion.refs_0_
  33.0 0.0 collective-permute-done.5.refs_7_.refs_10_
  33.0 37.2 %collective-permute-start.6 = (bf16[2,200,256]{2,1,0:T(8,128)(2,1)S(1)}, bf16[2,200,256]{2,1,0:T(8,128)(2,1)S(1)}, u32[]{:S(2)}, u32[]{:S(2)}) collective-permute-start(bf16[2,200,256]{2,1,0:T(8,128)(2,1)S(1)} %get-tuple-element.47), channel_id=1, source_target_pairs={{0,2},{1,3},{2,4},{3,5},{4,6},{5,7},{6,0},{7,1},{8,10},{9,11},{10,... | collective-permute-start | bytes 614408 | tf_op jit(solution)/shard_map/ppermute | solution.py:32
  70.2 4.1 %collective-permute-done.4.refs_6_.refs_9_ = bf16[2,200,256]{2,1,0:T(8,128)(2,1)S(1)} collective-permute-done((bf16[2,200,256]{2,1,0:T(8,128)(2,1)S(1)}, bf16[2,200,256]{2,1,0:T(8,128)(2,1)S(1)}, u32[]{:S(2)}, u32[]{:S(2)}) %collective-permute-start.4) | collective-permute-done | bytes 204832 | tf_op jit(solution)/shard_map/ppermute | solution.py:32
  74.3 1.9 collective-permute-start.9
  76.3 5.5 %collective-permute-done.3.refs_5_.refs_8_ = bf16[2,200,256]{2,1,0:T(8,128)(2,1)S(1)} collective-permute-done((bf16[2,200,256]{2,1,0:T(8,128)(2,1)S(1)}, bf16[2,200,256]{2,1,0:T(8,128)(2,1)S(1)}, u32[]{:S(2)}, u32[]{:S(2)}) %collective-permute-start.3) | collective-permute-done | bytes 204832 | tf_op jit(solution)/shard_map/ppermute | solution.py:32
  81.8 1.9 collective-permute-start.8
  83.7 0.0 collective-permute-done.2
  83.7 1.9 collective-permute-start.7
  85.6 0.0 collective-permute-done.1
  85.7 0.1 broadcast_select_fusion.1
  85.8 0.0 collective-permute-done.6.refs_8_.refs_11_
  85.8 0.0 collective-permute-done.9.refs_11_.refs_14_
  85.8 11.2 %collective-permute-done.8.refs_10_.refs_13_ = bf16[2,200,256]{2,1,0:T(8,128)(2,1)S(1)} collective-permute-done((bf16[2,200,256]{2,1,0:T(8,128)(2,1)S(1)}, bf16[2,200,256]{2,1,0:T(8,128)(2,1)S(1)}, u32[]{:S(2)}, u32[]{:S(2)}) %collective-permute-start.8) | collective-permute-done | bytes 204832 | tf_op jit(solution)/shard_map/ppermute | solution.py:32
  97.0 3.5 %collective-permute-done.7.refs_9_.refs_12_ = bf16[2,200,256]{2,1,0:T(8,128)(2,1)S(1)} collective-permute-done((bf16[2,200,256]{2,1,0:T(8,128)(2,1)S(1)}, bf16[2,200,256]{2,1,0:T(8,128)(2,1)S(1)}, u32[]{:S(2)}, u32[]{:S(2)}) %collective-permute-start.7) | collective-permute-done | bytes 204832 | tf_op jit(solution)/shard_map/ppermute | solution.py:32
  100.5 6.4 %attend.1 = (f32[128,1024]{1,0:T(8,128)S(1)}, bf16[128,1024]{1,0:T(8,128)(2,1)S(1)}, f32[2,8,1024]{2,1,0:T(8,128)S(1)}) custom-call(s32[2,2]{1,0:T(2,128)S(1)} %pad_add_fusion.refs_0_, bf16[128,1024]{1,0:T(8,128)(2,1)S(1)} %copy-done, bf16[128,1024]{1,0:T(8,128)(2,1)S(1)} %get-tuple-element.86.refs_2_, bf16[128,1024]{1,0:T(8,128)(2,1)S(1)} %copy-done.1, ...), custom_call_target="tpu_custom_call" | custom-call | bytes 1048576 | tf_op jit(solution)/shard_map/attend/pallas_call | solution.py:205
  106.8 1.9 collective-permute-start.11
  108.8 10.1 %collective-permute-start.10 = (f32[8,1024]{1,0:T(8,128)S(1)}, f32[8,1024]{1,0:T(8,128)S(1)}, u32[]{:S(2)}, u32[]{:S(2)}) collective-permute-start(f32[8,1024]{1,0:T(8,128)S(1)} %get-tuple-element.88), channel_id=1, source_target_pairs={{0,504},{8,0},{16,8},{24,16},{32,24},{40,32},{48,40},{56,48},{64,5... | collective-permute-start | bytes 98312 | tf_op jit(solution)/shard_map/ppermute | solution.py:32
  118.8 0.7 constant_dynamic-update-slice_fusion.3
  119.6 9.7 %backward.1 = (f32[128,1024]{1,0:T(8,128)S(1)}, bf16[128,1024]{1,0:T(8,128)(2,1)S(1)}, bf16[2,200,256]{2,1,0:T(8,128)(2,1)S(1)}, bf16[2,200,256]{2,1,0:T(8,128)(...) custom-call(s32[2,2]{1,0:T(2,128)S(1)} %pad_add_fusion.refs_0_, ...), custom_call_target="tpu_custom_call" | custom-call | bytes 1048576 | tf_op jit(solution)/shard_map/backward/pallas_call | solution.py:205
  129.3 0.7 constant_dynamic-update-slice_fusion.2
  130.0 1.5 collective-permute-start.12
  131.5 0.0 collective-permute-done.12
  131.5 6.0 %collective-permute-start.15 = (bf16[2,200,256]{2,1,0:T(8,128)(2,1)S(1)}, bf16[2,200,256]{2,1,0:T(8,128)(2,1)S(1)}, u32[]{:S(2)}, u32[]{:S(2)}) collective-permute-start(bf16[2,200,256]{2,1,0:T(8,128)(2,1)S(1)} %get-tuple-element.65), channel_id=1, source_target_pairs={{0,5},{1,6},{2,7},{3,0},{4,1},{5,2},{6,3},{7,4},{8,13},{9,14},{10,... | collective-permute-start | bytes 614408 | tf_op jit(solution)/shard_map/ppermute | solution.py:32
  137.5 35.8 %collective-permute-start.14 = (bf16[256,1024]{1,0:T(8,128)(2,1)}, bf16[256,1024]{1,0:T(8,128)(2,1)}, u32[]{:S(2)}, u32[]{:S(2)}) collective-permute-start(bf16[256,1024]{1,0:T(8,128)(2,1)} %constant_dynamic-update-slice_fusion.2), channel_id=1, source_target_pairs={{8,0},{16,8},{24,16},{32,24},{40,32},{48,40},{56,48},{64,56},{72,6... | collective-permute-start | bytes 1572872 | tf_op jit(solution)/shard_map/ppermute | solution.py:226
  173.3 1.5 collective-permute-start.13
  174.8 1.9 collective-permute-start.18
  176.7 5.4 %collective-permute-start.19 = (bf16[2,200,256]{2,1,0:T(8,128)(2,1)S(1)}, bf16[2,200,256]{2,1,0:T(8,128)(2,1)S(1)}, u32[]{:S(2)}, u32[]{:S(2)}) collective-permute-start(bf16[2,200,256]{2,1,0:T(8,128)(2,1)S(1)} %get-tuple-element.72), channel_id=1, source_target_pairs={{0,3},{1,4},{2,5},{3,6},{4,7},{5,0},{6,1},{7,2},{8,11},{9,12},{10,... | collective-permute-start | bytes 614408 | tf_op jit(solution)/shard_map/ppermute | solution.py:32
  182.2 0.0 collective-permute-done.15.refs_3_
  182.2 1.9 collective-permute-start.17
  184.1 25.3 %collective-permute-done.18.refs_4_ = bf16[2,200,256]{2,1,0:T(8,128)(2,1)S(1)} collective-permute-done((bf16[2,200,256]{2,1,0:T(8,128)(2,1)S(1)}, bf16[2,200,256]{2,1,0:T(8,128)(2,1)S(1)}, u32[]{:S(2)}, u32[]{:S(2)}) %collective-permute-start.18) | collective-permute-done | bytes 204832 | tf_op jit(solution)/shard_map/ppermute | solution.py:32
  209.4 1.9 collective-permute-start.16
  211.3 0.0 collective-permute-done.19.refs_5_
  211.4 1.9 collective-permute-start.20
  213.3 0.0 collective-permute-done.17.refs_2_
  213.3 3.4 %collective-permute-start.21 = (bf16[2,200,256]{2,1,0:T(8,128)(2,1)S(1)}, bf16[2,200,256]{2,1,0:T(8,128)(2,1)S(1)}, u32[]{:S(2)}, u32[]{:S(2)}) collective-permute-start(bf16[2,200,256]{2,1,0:T(8,128)(2,1)S(1)} %get-tuple-element.76), channel_id=1, source_target_pairs={{0,1},{1,2},{2,3},{3,4},{4,5},{5,6},{6,7},{7,0},{8,9},{9,10},{10,1... | collective-permute-start | bytes 614408 | tf_op jit(solution)/shard_map/ppermute | solution.py:32
  216.7 1.3 collective-permute-done.16.refs_1_
  217.9 15.6 %collective-permute-done.20.refs_6_ = bf16[2,200,256]{2,1,0:T(8,128)(2,1)S(1)} collective-permute-done((bf16[2,200,256]{2,1,0:T(8,128)(2,1)S(1)}, bf16[2,200,256]{2,1,0:T(8,128)(2,1)S(1)}, u32[]{:S(2)}, u32[]{:S(2)}) %collective-permute-start.20) | collective-permute-done | bytes 204832 | tf_op jit(solution)/shard_map/ppermute | solution.py:32
  233.5 1.4 join.1
  234.9 0.0 collective-permute-done.14
  234.9 0.0 collective-permute-done.13
  234.9 1.1 broadcast_select_fusion
  236.1 1.0 finish.1
  (16 shorter events, 0.1 us)
Async XLA Ops:
  0.6 11.1 %copy-start.5 = (s32[64]{0:T(128)S(1)}, s32[64]{0:T(128)}, u32[]{:S(2)}) copy-start(s32[64]{0:T(128)} %param.10) | copy-start | bytes 772
  0.6 11.7 %copy-start.3 = (s32[64,4]{0,1:T(4,128)S(1)}, s32[64,4]{0,1:T(4,128)}, u32[]{:S(2)}) copy-start(s32[64,4]{0,1:T(4,128)} %param.11) | copy-start | bytes 3076
  0.7 11.7 %copy-start.4 = (s32[64,4]{0,1:T(4,128)S(1)}, s32[64,4]{0,1:T(4,128)}, u32[]{:S(2)}) copy-start(s32[64,4]{0,1:T(4,128)} %param.9) | copy-start | bytes 3076
  4.0 9.8 %collective-permute-start = (bf16[256,1024]{1,0:T(8,128)(2,1)}, bf16[256,1024]{1,0:T(8,128)(2,1)}, u32[]{:S(2)}, u32[]{:S(2)}) collective-permute-start(bf16[256,1024]{1,0:T(8,128)(2,1)} %constant_dynamic-update-slice_fusion), channel_id=1, source_target_pairs={{248,248},{249,1},{250,202},{251,59},{252,236},{253,189},{254,30},... | collective-permute-start | bytes 1572872 | tf_op jit(solution)/shard_map/ppermute | solution.py:236
  5.5 78.2 %collective-permute-start.2 = (bf16[256,1024]{1,0:T(8,128)(2,1)}, bf16[256,1024]{1,0:T(8,128)(2,1)S(1)}, u32[]{:S(2)}, u32[]{:S(2)}) collective-permute-start(bf16[256,1024]{1,0:T(8,128)(2,1)} %constant_dynamic-update-slice_fusion), channel_id=1, source_target_pairs={{0,8},{8,16},{16,24},{24,32},{32,40},{40,48},{48,56},{56,64},{64,7... | collective-permute-start | bytes 1572872 | tf_op jit(solution)/shard_map/ppermute | solution.py:226
  10.0 1.4 copy-start.2
  11.7 88.8 %copy-start = (bf16[128,1024]{1,0:T(8,128)(2,1)S(1)}, bf16[128,1024]{1,0:T(8,128)(2,1)}, u32[]{:S(2)}) copy-start(bf16[128,1024]{1,0:T(8,128)(2,1)} %refs_1_.3) | copy-start | bytes 786436
  11.7 88.8 %copy-start.1 = (bf16[128,1024]{1,0:T(8,128)(2,1)S(1)}, bf16[128,1024]{1,0:T(8,128)(2,1)}, u32[]{:S(2)}) copy-start(bf16[128,1024]{1,0:T(8,128)(2,1)} %refs_3_.3) | copy-start | bytes 786436
  13.9 71.8 %collective-permute-start.1 = (bf16[256,1024]{1,0:T(8,128)(2,1)}, bf16[256,1024]{1,0:T(8,128)(2,1)}, u32[]{:S(2)}, u32[]{:S(2)}) collective-permute-start(bf16[256,1024]{1,0:T(8,128)(2,1)} %collective-permute-done), channel_id=1, source_target_pairs={{248,256},{1,257},{202,258},{59,259},{236,260},{189,261},{30,262},... | collective-permute-start | bytes 1572872 | tf_op jit(solution)/shard_map/ppermute | solution.py:236
  15.7 17.3 %collective-permute-start.5 = (bf16[2,200,256]{2,1,0:T(8,128)(2,1)S(1)}, bf16[2,200,256]{2,1,0:T(8,128)(2,1)S(1)}, u32[]{:S(2)}, u32[]{:S(2)}) collective-permute-start(bf16[2,200,256]{2,1,0:T(8,128)(2,1)S(1)} %get-tuple-element.45), channel_id=1, source_target_pairs={{0,5},{1,6},{2,7},{3,0},{4,1},{5,2},{6,3},{7,4},{8,13},{9,14},{10,... | collective-permute-start | bytes 614408 | tf_op jit(solution)/shard_map/ppermute | solution.py:32
  25.9 48.5 %collective-permute-start.4 = (bf16[2,200,256]{2,1,0:T(8,128)(2,1)S(1)}, bf16[2,200,256]{2,1,0:T(8,128)(2,1)S(1)}, u32[]{:S(2)}, u32[]{:S(2)}) collective-permute-start(bf16[2,200,256]{2,1,0:T(8,128)(2,1)S(1)} %get-tuple-element.43), channel_id=1, source_target_pairs={{0,3},{1,4},{2,5},{3,6},{4,7},{5,0},{6,1},{7,2},{8,11},{9,12},{10,... | collective-permute-start | bytes 614408 | tf_op jit(solution)/shard_map/ppermute | solution.py:32
  27.8 54.0 %collective-permute-start.3 = (bf16[2,200,256]{2,1,0:T(8,128)(2,1)S(1)}, bf16[2,200,256]{2,1,0:T(8,128)(2,1)S(1)}, u32[]{:S(2)}, u32[]{:S(2)}) collective-permute-start(bf16[2,200,256]{2,1,0:T(8,128)(2,1)S(1)} %get-tuple-element.41), channel_id=1, source_target_pairs={{0,4},{1,5},{2,6},{3,7},{4,0},{5,1},{6,2},{7,3},{8,12},{9,13},{10,... | collective-permute-start | bytes 614408 | tf_op jit(solution)/shard_map/ppermute | solution.py:32
  33.0 52.8 %collective-permute-start.6 = (bf16[2,200,256]{2,1,0:T(8,128)(2,1)S(1)}, bf16[2,200,256]{2,1,0:T(8,128)(2,1)S(1)}, u32[]{:S(2)}, u32[]{:S(2)}) collective-permute-start(bf16[2,200,256]{2,1,0:T(8,128)(2,1)S(1)} %get-tuple-element.47), channel_id=1, source_target_pairs={{0,2},{1,3},{2,4},{3,5},{4,6},{5,7},{6,0},{7,1},{8,10},{9,11},{10,... | collective-permute-start | bytes 614408 | tf_op jit(solution)/shard_map/ppermute | solution.py:32
  74.3 11.4 %collective-permute-start.9 = (bf16[2,200,256]{2,1,0:T(8,128)(2,1)S(1)}, bf16[2,200,256]{2,1,0:T(8,128)(2,1)S(1)}, u32[]{:S(2)}, u32[]{:S(2)}) collective-permute-start(bf16[2,200,256]{2,1,0:T(8,128)(2,1)S(1)} %get-tuple-element.53), channel_id=1, source_target_pairs={{0,7},{1,0},{2,1},{3,2},{4,3},{5,4},{6,5},{7,6},{8,15},{9,8},{10,9... | collective-permute-start | bytes 614408 | tf_op jit(solution)/shard_map/ppermute | solution.py:32
  81.8 15.2 %collective-permute-start.8 = (bf16[2,200,256]{2,1,0:T(8,128)(2,1)S(1)}, bf16[2,200,256]{2,1,0:T(8,128)(2,1)S(1)}, u32[]{:S(2)}, u32[]{:S(2)}) collective-permute-start(bf16[2,200,256]{2,1,0:T(8,128)(2,1)S(1)} %get-tuple-element.51), channel_id=1, source_target_pairs={{0,1},{1,2},{2,3},{3,4},{4,5},{5,6},{6,7},{7,0},{8,9},{9,10},{10,1... | collective-permute-start | bytes 614408 | tf_op jit(solution)/shard_map/ppermute | solution.py:32
  83.7 16.7 %collective-permute-start.7 = (bf16[2,200,256]{2,1,0:T(8,128)(2,1)S(1)}, bf16[2,200,256]{2,1,0:T(8,128)(2,1)S(1)}, u32[]{:S(2)}, u32[]{:S(2)}) collective-permute-start(bf16[2,200,256]{2,1,0:T(8,128)(2,1)S(1)} %get-tuple-element.49), channel_id=1, source_target_pairs={{0,6},{1,7},{2,0},{3,1},{4,2},{5,3},{6,4},{7,5},{8,14},{9,15},{10,... | collective-permute-start | bytes 614408 | tf_op jit(solution)/shard_map/ppermute | solution.py:32
  106.8 12.7 %collective-permute-start.11 = (f32[8,1024]{1,0:T(8,128)S(1)}, f32[8,1024]{1,0:T(8,128)S(1)}, u32[]{:S(2)}, u32[]{:S(2)}) collective-permute-start(f32[8,1024]{1,0:T(8,128)S(1)} %get-tuple-element.87), channel_id=1, source_target_pairs={{0,8},{8,16},{16,24},{24,32},{32,40},{40,48},{48,56},{56,64},{64,7... | collective-permute-start | bytes 98312 | tf_op jit(solution)/shard_map/ppermute | solution.py:32
  108.8 10.8 %collective-permute-start.10 = (f32[8,1024]{1,0:T(8,128)S(1)}, f32[8,1024]{1,0:T(8,128)S(1)}, u32[]{:S(2)}, u32[]{:S(2)}) collective-permute-start(f32[8,1024]{1,0:T(8,128)S(1)} %get-tuple-element.88), channel_id=1, source_target_pairs={{0,504},{8,0},{16,8},{24,16},{32,24},{40,32},{48,40},{56,48},{64,5... | collective-permute-start | bytes 98312 | tf_op jit(solution)/shard_map/ppermute | solution.py:32
  130.0 1.5 collective-permute-start.12
  131.5 50.7 %collective-permute-start.15 = (bf16[2,200,256]{2,1,0:T(8,128)(2,1)S(1)}, bf16[2,200,256]{2,1,0:T(8,128)(2,1)S(1)}, u32[]{:S(2)}, u32[]{:S(2)}) collective-permute-start(bf16[2,200,256]{2,1,0:T(8,128)(2,1)S(1)} %get-tuple-element.65), channel_id=1, source_target_pairs={{0,5},{1,6},{2,7},{3,0},{4,1},{5,2},{6,3},{7,4},{8,13},{9,14},{10,... | collective-permute-start | bytes 614408 | tf_op jit(solution)/shard_map/ppermute | solution.py:32
  137.5 97.4 %collective-permute-start.14 = (bf16[256,1024]{1,0:T(8,128)(2,1)}, bf16[256,1024]{1,0:T(8,128)(2,1)}, u32[]{:S(2)}, u32[]{:S(2)}) collective-permute-start(bf16[256,1024]{1,0:T(8,128)(2,1)} %constant_dynamic-update-slice_fusion.2), channel_id=1, source_target_pairs={{8,0},{16,8},{24,16},{32,24},{40,32},{48,40},{56,48},{64,56},{72,6... | collective-permute-start | bytes 1572872 | tf_op jit(solution)/shard_map/ppermute | solution.py:226
  173.3 61.6 %collective-permute-start.13 = (bf16[256,1024]{1,0:T(8,128)(2,1)}, bf16[256,1024]{1,0:T(8,128)(2,1)}, u32[]{:S(2)}, u32[]{:S(2)}) collective-permute-start(bf16[256,1024]{1,0:T(8,128)(2,1)} %collective-permute-done.12), channel_id=1, source_target_pairs={{248,504},{1,505},{202,506},{59,507},{236,508},{189,509},{30,510},... | collective-permute-start | bytes 1572872 | tf_op jit(solution)/shard_map/ppermute | solution.py:236
  174.8 34.6 %collective-permute-start.18 = (bf16[2,200,256]{2,1,0:T(8,128)(2,1)S(1)}, bf16[2,200,256]{2,1,0:T(8,128)(2,1)S(1)}, u32[]{:S(2)}, u32[]{:S(2)}) collective-permute-start(bf16[2,200,256]{2,1,0:T(8,128)(2,1)S(1)} %get-tuple-element.70), channel_id=1, source_target_pairs={{0,4},{1,5},{2,6},{3,7},{4,0},{5,1},{6,2},{7,3},{8,12},{9,13},{10,... | collective-permute-start | bytes 614408 | tf_op jit(solution)/shard_map/ppermute | solution.py:32
  176.7 34.6 %collective-permute-start.19 = (bf16[2,200,256]{2,1,0:T(8,128)(2,1)S(1)}, bf16[2,200,256]{2,1,0:T(8,128)(2,1)S(1)}, u32[]{:S(2)}, u32[]{:S(2)}) collective-permute-start(bf16[2,200,256]{2,1,0:T(8,128)(2,1)S(1)} %get-tuple-element.72), channel_id=1, source_target_pairs={{0,3},{1,4},{2,5},{3,6},{4,7},{5,0},{6,1},{7,2},{8,11},{9,12},{10,... | collective-permute-start | bytes 614408 | tf_op jit(solution)/shard_map/ppermute | solution.py:32
  182.2 31.1 %collective-permute-start.17 = (bf16[2,200,256]{2,1,0:T(8,128)(2,1)S(1)}, bf16[2,200,256]{2,1,0:T(8,128)(2,1)S(1)}, u32[]{:S(2)}, u32[]{:S(2)}) collective-permute-start(bf16[2,200,256]{2,1,0:T(8,128)(2,1)S(1)} %get-tuple-element.68), channel_id=1, source_target_pairs={{0,6},{1,7},{2,0},{3,1},{4,2},{5,3},{6,4},{7,5},{8,14},{9,15},{10,... | collective-permute-start | bytes 614408 | tf_op jit(solution)/shard_map/ppermute | solution.py:32
  209.4 8.5 %collective-permute-start.16 = (bf16[2,200,256]{2,1,0:T(8,128)(2,1)S(1)}, bf16[2,200,256]{2,1,0:T(8,128)(2,1)S(1)}, u32[]{:S(2)}, u32[]{:S(2)}) collective-permute-start(bf16[2,200,256]{2,1,0:T(8,128)(2,1)S(1)} %get-tuple-element.66), channel_id=1, source_target_pairs={{0,7},{1,0},{2,1},{3,2},{4,3},{5,4},{6,5},{7,6},{8,15},{9,8},{10,9... | collective-permute-start | bytes 614408 | tf_op jit(solution)/shard_map/ppermute | solution.py:32
  211.4 22.1 %collective-permute-start.20 = (bf16[2,200,256]{2,1,0:T(8,128)(2,1)S(1)}, bf16[2,200,256]{2,1,0:T(8,128)(2,1)S(1)}, u32[]{:S(2)}, u32[]{:S(2)}) collective-permute-start(bf16[2,200,256]{2,1,0:T(8,128)(2,1)S(1)} %get-tuple-element.74), channel_id=1, source_target_pairs={{0,2},{1,3},{2,4},{3,5},{4,6},{5,7},{6,0},{7,1},{8,10},{9,11},{10,... | collective-permute-start | bytes 614408 | tf_op jit(solution)/shard_map/ppermute | solution.py:32
  213.3 20.2 %collective-permute-start.21 = (bf16[2,200,256]{2,1,0:T(8,128)(2,1)S(1)}, bf16[2,200,256]{2,1,0:T(8,128)(2,1)S(1)}, u32[]{:S(2)}, u32[]{:S(2)}) collective-permute-start(bf16[2,200,256]{2,1,0:T(8,128)(2,1)S(1)} %get-tuple-element.76), channel_id=1, source_target_pairs={{0,1},{1,2},{2,3},{3,4},{4,5},{5,6},{6,7},{7,0},{8,9},{9,10},{10,1... | collective-permute-start | bytes 614408 | tf_op jit(solution)/shard_map/ppermute | solution.py:32

commit v4 on v3

--- a/solution.py
+++ b/solution.py
@@ -48,20 +48,14 @@
         stack_heads(ref, dst_ref, slot)
 
 
-def split_kernel(axis, store, *pieces):
+def split_kernel(axis, queries, cots, store, both, *pieces):
     n, width = len(pieces), pieces[0].shape[-1]
+    tok = queries.shape[0]
+    both[:tok, :] = queries[...]
+    both[tok:, :] = cots[...]
     for k, piece in enumerate(pieces):
         col = lax.rem(lax.axis_index(axis) + k, n) * width
         piece[...] = store[:, :, pl.ds(pl.multiple_of(col, width), width)]
-
-
-def join_kernel(axis, shifts, *refs):
-    pieces, out = refs[-1 - len(shifts) : -1], refs[-1]
-    width = pieces[0].shape[-1]
-    n = out.shape[-1] // width
-    for k, piece in zip(shifts, pieces):
-        col = lax.rem(lax.axis_index(axis) + k, n) * width
-        out[:, :, pl.ds(pl.multiple_of(col, width), width)] = piece[...]
 
 
 def fwd_kernel(first, last, blocks, *refs):
@@ -188,13 +182,19 @@
                 out[:, h * HEAD : (h + 1) * HEAD] = block.T.astype(out.dtype)
 
 
-def finish_kernel(o_own, o_far, stats, far, dq_own, dq_far, out, dq):
+def finish_kernel(axis, o_own, stats, far, dq_own, both, *refs):
+    pieces, (out, dq, dkv) = refs[:-3], refs[-3:]
     tok, cols = out.shape
+    n, pair = len(pieces), pieces[0].shape[-1]
+    for k, piece in enumerate(pieces):
+        col = lax.rem(lax.axis_index(axis) + k, n) * pair
+        dkv[:, :, pl.ds(pl.multiple_of(col, pair), pair)] = piece[...]
     _, _, w_near, w_far = merge(stats[0], far[...])
-    whole = o_own[...] * w_near + o_far[...].astype(jnp.float32) * w_far
     for h in range(cols // HEAD):
-        out[:, h * HEAD : (h + 1) * HEAD] = whole[:, h * tok : (h + 1) * tok].T.astype(out.dtype)
-    dq[...] = (dq_own[...] + dq_far[...].astype(jnp.float32)).astype(dq.dtype)
+        rows = slice(h * tok, (h + 1) * tok)
+        whole = o_own[:, rows] * w_near[:, rows] + both[:tok, rows].astype(jnp.float32) * w_far[:, rows]
+        out[:, h * HEAD : (h + 1) * HEAD] = whole.T.astype(out.dtype)
+    dq[...] = (dq_own[...] + both[tok:, :].astype(jnp.float32)).astype(dq.dtype)
 
 
 VMEM = pl.BlockSpec(memory_space=pltpu.VMEM)
@@ -230,7 +230,7 @@
     count, n = lax.axis_size("dp"), lax.axis_size("tensor")
     half = count // 2
     source, near = (half - 1, 0) if steps > 0 else (0, half - 1)
-    relays = [31, 0, 25, 7, 29, 23, 3, 9] if half == 32 and n == 8 else [half - 1] * n
+    relays = [5, 17, 25, 7, 29, 23, 3, 9] if half == 32 and n == 8 else [half - 1] * n
 
     def send(part, pairs):
         return lax.ppermute(part, ("dp", "tensor"), [(d * n + t, e * n + t) for d, e, t in pairs])
@@ -244,12 +244,12 @@
     half = lax.axis_size("dp") // 2
     near = 0 if steps > 0 else half - 1
     first_leg, second_leg = seam_legs(steps)
-    fan = first_leg(both)
     got = {}
     for i, k in enumerate(order):
-        gate = fan if i < WINDOW else got[order[i - WINDOW]]
-        got[k] = shift(after(pieces[k], gate), "tensor", sign * k) if k else pieces[k]
-    both = jnp.where(lax.axis_index("dp") % half == near, second_leg(fan), within(both, steps))
+        piece = after(pieces[k], got[order[i - WINDOW]]) if i >= WINDOW else pieces[k]
+        got[k] = shift(piece, "tensor", sign * k) if k else piece
+    over = second_leg(first_leg(both))
+    both = jnp.where(lax.axis_index("dp") % half == near, over, within(both, steps))
     return got, both
 
 
@@ -264,9 +264,11 @@
     pair = store_cols // n
     piece_shape = ((n_img, part_keys, pair), bf16)
 
-    sends = call(functools.partial(split_kernel, "tensor"), "split", [piece_shape] * n, (key_value_store,))
-    order = [k for d in range(n // 2, 0, -1) for k in sorted({d, n - d})] + [0]
-    both = jnp.concatenate([queries, output_gradient], axis=0)
+    both, *sends = call(
+        functools.partial(split_kernel, "tensor"), "split", [((2 * tok, cols), bf16)] + [piece_shape] * n,
+        (queries, output_gradient, key_value_store),
+    )
+    order = [1, n - 1, n // 2] + [k for d in range(2, n // 2) for k in (d, n - d)] + [0]
     kv, both = exchange(sends, order, 1, both, 1)
     q_back, g_back = both[:tok], both[tok:]
 
@@ -285,10 +287,15 @@
     stat_shape = ((2, 8, width), f32)
     acc_shape = ((2, HEAD, width), f32)
     rows_scratch = pltpu.VMEM((2, width, HEAD), bf16)
+    early, rest = [0] + order[:WINDOW], order[WINDOW:-1]
+    state = call(
+        functools.partial(fwd_kernel, True, False, len(early)), "attend", [acc_shape, stat_shape],
+        (meta, queries, q_back) + tuple(kv[k] for k in early), [rows_scratch], 1,
+    )
     o_own, o_back, stats = call(
-        functools.partial(fwd_kernel, True, True, n), "attend",
+        functools.partial(fwd_kernel, False, True, len(rest)), "attend",
         [((HEAD, width), f32), ((HEAD, width), bf16), stat_shape],
-        (meta, queries, q_back, output_gradient, g_back) + tuple(kv[k] for k in order),
+        (meta, queries, q_back, output_gradient, g_back) + tuple(kv[k] for k in rest) + tuple(state),
         [rows_scratch, rows_scratch, pltpu.VMEM(*acc_shape)], 1,
     )
 
@@ -303,14 +310,10 @@
     )
     both = jnp.concatenate([o_back.reshape(tok, cols), dq_back], axis=0)
     back, both = exchange(dict(zip(order, pieces)), order, -1, both, -1)
-    o_far, dq_far = both[:tok].reshape(HEAD, width), both[tok:]
-
-    attended, grad_queries = call(
-        finish_kernel, "finish", [((tok, cols), bf16)] * 2, (o_own, o_far, stats, far_own, dq_own, dq_far)
-    )
-    (grad_kv,) = call(
-        functools.partial(join_kernel, "tensor", range(n)), "join", [((n_img, part_keys, store_cols), bf16)],
-        [back[k] for k in range(n)],
+    attended, grad_queries, grad_kv = call(
+        functools.partial(finish_kernel, "tensor"), "finish",
+        [((tok, cols), bf16)] * 2 + [((n_img, part_keys, store_cols), bf16)],
+        (o_own, stats, far_own, dq_own, both) + tuple(back[k] for k in range(n)),
     )
     return attended, grad_queries, grad_kv
 

time: 238 us -> 220 us (0.924)
  starting transfers between devices: 141 us -> 115 us
  waiting for transfers between devices: 66.5 us -> 73.3 us
    ppermute x2, starting transfers between devices: 40.3 us -> 21 us  [within(): return lax.ppermute(value, 'dp', inside)]
    ppermute x16, waiting for transfers between devices: 66.5 us -> 73.2 us  [shift(): return lax.ppermute(value, axis, pairs)]
    ppermute x16, starting transfers between devices: 94.4 us -> 88.5 us  [shift(): return lax.ppermute(value, axis, pairs)]
  transfers between devices with their start and end apart: 22 -> 22, of which waited for: 7 -> 6; matrix products, arithmetic and copies ran while one was open for 2% -> 3% of each run, Pallas kernels for 1% -> 2%
where the time goes in v4:
time: 220 us; the launch traced here: 219 us
  starting transfers between devices  115 us (52%)
  waiting for transfers between devices  73.3 us (33%)
  Pallas kernels  19.4 us (9%)
  local copies, waits for them, and re-layouts  5.83 us (3%)
  other arithmetic  3.98 us (2%)
    ppermute x16, starting transfers between devices, shift(): return lax.ppermute(value, axis, pairs)  88.5 us
    ppermute x16, waiting for transfers between devices, shift(): return lax.ppermute(value, axis, pairs)  73.2 us
    ppermute x2, starting transfers between devices, within(): return lax.ppermute(value, 'dp', inside)  21 us
    pallas_call x5, Pallas kernels, call(): pl.pallas_call(kernel, out_shape=[jax.ShapeDtypeStruct(*o) for o in outs]...  19.4 us
    ppermute x4, starting transfers between devices, send(): lax.ppermute(part, ('dp', 'tensor'), [(d * n + t, e * n + t) for d, e, t...  5.97 us
  transfers between devices with their start and end apart: 22, of which 6 were waited for; matrix products, arithmetic and copies ran while one was open for 3% of the time, Pallas kernels for 2%

profile of v4, /device:TPU:1, one launch (start us, length us, event | category | flops | bytes accessed | tf_op | source)
XLA Modules:
  0.0 219.0 jit_solution(11179294985494585712)
XLA Ops:
  0.6 0.0 copy-start
  0.6 0.9 copy-done
  1.6 0.9 copy-done.2
  2.5 1.4 copy-done.4
  4.0 0.3 split.1
  4.2 0.0 copy-start.1
  4.2 1.6 collective-permute-start
  5.8 4.5 %collective-permute-start.2 = (bf16[256,1024]{1,0:T(8,128)(2,1)S(1)}, bf16[256,1024]{1,0:T(8,128)(2,1)}, u32[]{:S(2)}, u32[]{:S(2)}) collective-permute-start(bf16[256,1024]{1,0:T(8,128)(2,1)S(1)} %get-tuple-element.35), channel_id=1, source_target_pairs={{0,8},{8,16},{16,24},{24,32},{32,40},{40,48},{48,56},{56,64},{64,7... | collective-permute-start | bytes 1572872 | tf_op jit(solution)/shard_map/ppermute | solution.py:226
  10.3 3.5 %collective-permute-start.3 = (bf16[2,200,256]{2,1,0:T(8,128)(2,1)S(1)}, bf16[2,200,256]{2,1,0:T(8,128)(2,1)S(1)}, u32[]{:S(2)}, u32[]{:S(2)}) collective-permute-start(bf16[2,200,256]{2,1,0:T(8,128)(2,1)S(1)} %get-tuple-element.37), channel_id=1, source_target_pairs={{0,1},{1,2},{2,3},{3,4},{4,5},{5,6},{6,7},{7,0},{8,9},{9,10},{10,1... | collective-permute-start | bytes 614408 | tf_op jit(solution)/shard_map/ppermute | solution.py:32
  13.9 11.3 %collective-permute-start.5 = (bf16[2,200,256]{2,1,0:T(8,128)(2,1)S(1)}, bf16[2,200,256]{2,1,0:T(8,128)(2,1)S(1)}, u32[]{:S(2)}, u32[]{:S(2)}) collective-permute-start(bf16[2,200,256]{2,1,0:T(8,128)(2,1)S(1)} %get-tuple-element.40), channel_id=1, source_target_pairs={{0,7},{1,0},{2,1},{3,2},{4,3},{5,4},{6,5},{7,6},{8,15},{9,8},{10,9... | collective-permute-start | bytes 614408 | tf_op jit(solution)/shard_map/ppermute | solution.py:32
  25.2 1.9 collective-permute-start.7
  27.1 0.6 fusion.5
  27.7 0.2 dynamic-slice_reduce_fusion
  28.0 1.3 iota_compare_fusion
  29.3 0.0 collective-permute-done
  29.3 1.5 collective-permute-start.1
  30.7 0.2 fusion.1
  30.9 0.2 fusion.3
  31.1 0.0 collective-permute-done.3.refs_4_.refs_8_
  31.1 2.5 %collective-permute-start.9 = (bf16[2,200,256]{2,1,0:T(8,128)(2,1)S(1)}, bf16[2,200,256]{2,1,0:T(8,128)(2,1)S(1)}, u32[]{:S(2)}, u32[]{:S(2)}) collective-permute-start(bf16[2,200,256]{2,1,0:T(8,128)(2,1)S(1)} %get-tuple-element.46), channel_id=1, source_target_pairs={{0,2},{1,3},{2,4},{3,5},{4,6},{5,7},{6,0},{7,1},{8,10},{9,11},{10,... | collective-permute-start | bytes 614408 | tf_op jit(solution)/shard_map/ppermute | solution.py:32
  33.6 0.1 copy.11
  33.7 0.1 copy.12
  33.8 0.1 pad_add_fusion.refs_0_
  33.9 0.0 collective-permute-done.5.refs_5_.refs_9_
  33.9 8.5 %collective-permute-start.4 = (bf16[2,200,256]{2,1,0:T(8,128)(2,1)S(1)}, bf16[2,200,256]{2,1,0:T(8,128)(2,1)S(1)}, u32[]{:S(2)}, u32[]{:S(2)}) collective-permute-start(bf16[2,200,256]{2,1,0:T(8,128)(2,1)S(1)} %get-tuple-element.38), channel_id=1, source_target_pairs={{0,6},{1,7},{2,0},{3,1},{4,2},{5,3},{6,4},{7,5},{8,14},{9,15},{10,... | collective-permute-start | bytes 614408 | tf_op jit(solution)/shard_map/ppermute | solution.py:32
  42.4 17.1 %collective-permute-done.7.refs_6_.refs_10_ = bf16[2,200,256]{2,1,0:T(8,128)(2,1)S(1)} collective-permute-done((bf16[2,200,256]{2,1,0:T(8,128)(2,1)S(1)}, bf16[2,200,256]{2,1,0:T(8,128)(2,1)S(1)}, u32[]{:S(2)}, u32[]{:S(2)}) %collective-permute-start.7) | collective-permute-done | bytes 204832 | tf_op jit(solution)/shard_map/ppermute | solution.py:32
  59.6 1.9 collective-permute-start.6
  61.5 0.0 collective-permute-done.9.refs_7_.refs_11_
  61.5 27.7 %collective-permute-start.8 = (bf16[2,200,256]{2,1,0:T(8,128)(2,1)S(1)}, bf16[2,200,256]{2,1,0:T(8,128)(2,1)S(1)}, u32[]{:S(2)}, u32[]{:S(2)}) collective-permute-start(bf16[2,200,256]{2,1,0:T(8,128)(2,1)S(1)} %get-tuple-element.44), channel_id=1, source_target_pairs={{0,5},{1,6},{2,7},{3,0},{4,1},{5,2},{6,3},{7,4},{8,13},{9,14},{10,... | collective-permute-start | bytes 614408 | tf_op jit(solution)/shard_map/ppermute | solution.py:32
  89.2 0.0 collective-permute-done.2
  89.2 0.0 collective-permute-done.1
  89.2 1.1 broadcast_select_fusion.1
  90.3 0.0 copy-start.3
  90.4 4.2 %attend.2 = (f32[2,128,1024]{2,1,0:T(8,128)S(1)}, f32[2,8,1024]{2,1,0:T(8,128)S(1)}) custom-call(s32[2,2]{1,0:T(2,128)S(1)} %pad_add_fusion.refs_0_, bf16[128,1024]{1,0:T(8,128)(2,1)S(1)} %copy-done.1, bf16[128,1024]{1,0:T(8,128)(2,1)S(1)} %get-tuple-element.74.refs_2_, bf16[2,200,256]{2,1,0:T(8,128)(2,1)S(1)} %get-tuple-element.47.refs_3_.refs_15_, ...), custom_call_target="tpu_custom_call" | custom-call | bytes 1048576 | tf_op jit(solution)/shard_map/attend/pallas_call | solution.py:205
  94.6 0.0 collective-permute-done.4.refs_5_.refs_12_
  94.6 0.0 collective-permute-done.6.refs_6_.refs_13_
  94.6 0.0 collective-permute-done.8.refs_7_.refs_14_
  94.6 3.2 %attend.3 = (f32[128,1024]{1,0:T(8,128)S(1)}, bf16[128,1024]{1,0:T(8,128)(2,1)S(1)}, f32[2,8,1024]{2,1,0:T(8,128)S(1)}) custom-call(s32[2,2]{1,0:T(2,128)S(1)} %pad_add_fusion.refs_0_, bf16[128,1024]{1,0:T(8,128)(2,1)S(1)} %copy-done.1, bf16[128,1024]{1,0:T(8,128)(2,1)S(1)} %get-tuple-element.74.refs_2_, bf16[128,1024]{1,0:T(8,128)(2,1)S(1)} %copy-done.3, ...), custom_call_target="tpu_custom_call" | custom-call | bytes 1048576 | tf_op jit(solution)/shard_map/attend/pallas_call | solution.py:205
  97.8 1.9 collective-permute-start.11
  99.7 2.9 %collective-permute-start.10 = (f32[8,1024]{1,0:T(8,128)S(1)}, f32[8,1024]{1,0:T(8,128)S(1)}, u32[]{:S(2)}, u32[]{:S(2)}) collective-permute-start(f32[8,1024]{1,0:T(8,128)S(1)} %get-tuple-element.76), channel_id=1, source_target_pairs={{0,504},{8,0},{16,8},{24,16},{32,24},{40,32},{48,40},{56,48},{64,5... | collective-permute-start | bytes 98312 | tf_op jit(solution)/shard_map/ppermute | solution.py:32
  102.7 0.7 constant_dynamic-update-slice_fusion.1
  103.4 1.6 collective-permute-done.10.refs_6_.far
  105.0 10.1 %backward.1 = (f32[128,1024]{1,0:T(8,128)S(1)}, bf16[128,1024]{1,0:T(8,128)(2,1)S(1)}, bf16[2,200,256]{2,1,0:T(8,128)(2,1)}, bf16[2,200,256]{2,1,0:T(8,128)(2,1)...) custom-call(s32[2,2]{1,0:T(2,128)S(1)} %pad_add_fusion.refs_0_, ...), custom_call_target="tpu_custom_call" | custom-call | bytes 1048576 | tf_op jit(solution)/shard_map/backward/pallas_call | solution.py:205
  115.1 0.7 constant_dynamic-update-slice_fusion
  115.8 1.4 collective-permute-start.12
  117.3 16.5 %collective-permute-start.14 = (bf16[256,1024]{1,0:T(8,128)(2,1)}, bf16[256,1024]{1,0:T(8,128)(2,1)}, u32[]{:S(2)}, u32[]{:S(2)}) collective-permute-start(bf16[256,1024]{1,0:T(8,128)(2,1)} %constant_dynamic-update-slice_fusion), channel_id=1, source_target_pairs={{8,0},{16,8},{24,16},{32,24},{40,32},{48,40},{56,48},{64,56},{72,6... | collective-permute-start | bytes 1572872 | tf_op jit(solution)/shard_map/ppermute | solution.py:226
  133.8 0.0 collective-permute-done.12
  133.8 1.5 collective-permute-start.13
  135.2 2.7 %collective-permute-start.15 = (bf16[2,200,256]{2,1,0:T(8,128)(2,1)S(1)}, bf16[2,200,256]{2,1,0:T(8,128)(2,1)S(1)}, u32[]{:S(2)}, u32[]{:S(2)}) collective-permute-start(bf16[2,200,256]{2,1,0:T(8,128)(2,1)S(1)} %get-tuple-element.56), channel_id=1, source_target_pairs={{0,6},{1,7},{2,0},{3,1},{4,2},{5,3},{6,4},{7,5},{8,14},{9,15},{10,... | collective-permute-start | bytes 614408 | tf_op jit(solution)/shard_map/ppermute | solution.py:32
  138.0 8.9 %collective-permute-start.16 = (bf16[2,200,256]{2,1,0:T(8,128)(2,1)}, bf16[2,200,256]{2,1,0:T(8,128)(2,1)S(1)}, u32[]{:S(2)}, u32[]{:S(2)}) collective-permute-start(bf16[2,200,256]{2,1,0:T(8,128)(2,1)} %get-tuple-element.58), channel_id=1, source_target_pairs={{0,7},{1,0},{2,1},{3,2},{4,3},{5,4},{6,5},{7,6},{8,15},{9,8},{10,9... | collective-permute-start | bytes 614408 | tf_op jit(solution)/shard_map/ppermute | solution.py:32
  146.9 1.9 collective-permute-start.17
  148.9 0.0 collective-permute-done.15.refs_2_
  148.9 5.2 %collective-permute-start.19 = (bf16[2,200,256]{2,1,0:T(8,128)(2,1)S(1)}, bf16[2,200,256]{2,1,0:T(8,128)(2,1)S(1)}, u32[]{:S(2)}, u32[]{:S(2)}) collective-permute-start(bf16[2,200,256]{2,1,0:T(8,128)(2,1)S(1)} %get-tuple-element.62), channel_id=1, source_target_pairs={{0,4},{1,5},{2,6},{3,7},{4,0},{5,1},{6,2},{7,3},{8,12},{9,13},{10,... | collective-permute-start | bytes 614408 | tf_op jit(solution)/shard_map/ppermute | solution.py:32
  154.1 0.0 collective-permute-done.16.refs_1_
  154.1 3.1 %collective-permute-start.21 = (bf16[2,200,256]{2,1,0:T(8,128)(2,1)S(1)}, bf16[2,200,256]{2,1,0:T(8,128)(2,1)S(1)}, u32[]{:S(2)}, u32[]{:S(2)}) collective-permute-start(bf16[2,200,256]{2,1,0:T(8,128)(2,1)S(1)} %get-tuple-element.66), channel_id=1, source_target_pairs={{0,2},{1,3},{2,4},{3,5},{4,6},{5,7},{6,0},{7,1},{8,10},{9,11},{10,... | collective-permute-start | bytes 614408 | tf_op jit(solution)/shard_map/ppermute | solution.py:32
  157.2 3.2 %collective-permute-done.17.refs_7_ = bf16[2,200,256]{2,1,0:T(8,128)(2,1)S(1)} collective-permute-done((bf16[2,200,256]{2,1,0:T(8,128)(2,1)}, bf16[2,200,256]{2,1,0:T(8,128)(2,1)S(1)}, u32[]{:S(2)}, u32[]{:S(2)}) %collective-permute-start.17) | collective-permute-done | bytes 204832 | tf_op jit(solution)/shard_map/ppermute | solution.py:32
  160.4 2.6 %collective-permute-start.18 = (bf16[2,200,256]{2,1,0:T(8,128)(2,1)S(1)}, bf16[2,200,256]{2,1,0:T(8,128)(2,1)S(1)}, u32[]{:S(2)}, u32[]{:S(2)}) collective-permute-start(bf16[2,200,256]{2,1,0:T(8,128)(2,1)S(1)} %get-tuple-element.61), channel_id=1, source_target_pairs={{0,5},{1,6},{2,7},{3,0},{4,1},{5,2},{6,3},{7,4},{8,13},{9,14},{10,... | collective-permute-start | bytes 614408 | tf_op jit(solution)/shard_map/ppermute | solution.py:32
  163.0 25.2 %collective-permute-done.19.refs_4_ = bf16[2,200,256]{2,1,0:T(8,128)(2,1)S(1)} collective-permute-done((bf16[2,200,256]{2,1,0:T(8,128)(2,1)S(1)}, bf16[2,200,256]{2,1,0:T(8,128)(2,1)S(1)}, u32[]{:S(2)}, u32[]{:S(2)}) %collective-permute-start.19) | collective-permute-done | bytes 204832 | tf_op jit(solution)/shard_map/ppermute | solution.py:32
  188.2 1.9 collective-permute-start.20
  190.1 1.1 broadcast_select_fusion.both
  191.2 0.0 collective-permute-done.21.refs_6_
  191.2 0.3 collective-permute-done.18.refs_3_
  191.6 25.8 %collective-permute-done.20.refs_5_ = bf16[2,200,256]{2,1,0:T(8,128)(2,1)S(1)} collective-permute-done((bf16[2,200,256]{2,1,0:T(8,128)(2,1)S(1)}, bf16[2,200,256]{2,1,0:T(8,128)(2,1)S(1)}, u32[]{:S(2)}, u32[]{:S(2)}) %collective-permute-start.20) | collective-permute-done | bytes 204832 | tf_op jit(solution)/shard_map/ppermute | solution.py:32
  217.3 1.6 finish.1
  (17 shorter events, 0.1 us)
Async XLA Ops:
  0.6 1.0 copy-start
  1.6 0.9 copy-start.2
  2.5 1.4 copy-start.4
  4.0 23.2 %copy-start.7 = (s32[64]{0:T(128)S(1)}, s32[64]{0:T(128)}, u32[]{:S(2)}) copy-start(s32[64]{0:T(128)} %param.10) | copy-start | bytes 772
  4.0 23.8 %copy-start.5 = (s32[64,4]{0,1:T(4,128)S(1)}, s32[64,4]{0,1:T(4,128)}, u32[]{:S(2)}) copy-start(s32[64,4]{0,1:T(4,128)} %param.11) | copy-start | bytes 3076
  4.0 23.8 %copy-start.6 = (s32[64,4]{0,1:T(4,128)S(1)}, s32[64,4]{0,1:T(4,128)}, u32[]{:S(2)}) copy-start(s32[64,4]{0,1:T(4,128)} %param.9) | copy-start | bytes 3076
  4.2 86.1 %copy-start.1 = (bf16[128,1024]{1,0:T(8,128)(2,1)S(1)}, bf16[128,1024]{1,0:T(8,128)(2,1)}, u32[]{:S(2)}) copy-start(bf16[128,1024]{1,0:T(8,128)(2,1)} %refs_1_.5) | copy-start | bytes 786436
  4.2 25.0 %collective-permute-start = (bf16[256,1024]{1,0:T(8,128)(2,1)S(1)}, bf16[256,1024]{1,0:T(8,128)(2,1)}, u32[]{:S(2)}, u32[]{:S(2)}) collective-permute-start(bf16[256,1024]{1,0:T(8,128)(2,1)S(1)} %get-tuple-element.35), channel_id=1, source_target_pairs={{248,40},{249,137},{250,202},{251,59},{252,236},{253,189},{254,30}... | collective-permute-start | bytes 1572872 | tf_op jit(solution)/shard_map/ppermute | solution.py:236
  5.8 83.3 %collective-permute-start.2 = (bf16[256,1024]{1,0:T(8,128)(2,1)S(1)}, bf16[256,1024]{1,0:T(8,128)(2,1)}, u32[]{:S(2)}, u32[]{:S(2)}) collective-permute-start(bf16[256,1024]{1,0:T(8,128)(2,1)S(1)} %get-tuple-element.35), channel_id=1, source_target_pairs={{0,8},{8,16},{16,24},{24,32},{32,40},{40,48},{48,56},{56,64},{64,7... | collective-permute-start | bytes 1572872 | tf_op jit(solution)/shard_map/ppermute | solution.py:226
  10.3 20.8 %collective-permute-start.3 = (bf16[2,200,256]{2,1,0:T(8,128)(2,1)S(1)}, bf16[2,200,256]{2,1,0:T(8,128)(2,1)S(1)}, u32[]{:S(2)}, u32[]{:S(2)}) collective-permute-start(bf16[2,200,256]{2,1,0:T(8,128)(2,1)S(1)} %get-tuple-element.37), channel_id=1, source_target_pairs={{0,1},{1,2},{2,3},{3,4},{4,5},{5,6},{6,7},{7,0},{8,9},{9,10},{10,1... | collective-permute-start | bytes 614408 | tf_op jit(solution)/shard_map/ppermute | solution.py:32
  13.9 20.0 %collective-permute-start.5 = (bf16[2,200,256]{2,1,0:T(8,128)(2,1)S(1)}, bf16[2,200,256]{2,1,0:T(8,128)(2,1)S(1)}, u32[]{:S(2)}, u32[]{:S(2)}) collective-permute-start(bf16[2,200,256]{2,1,0:T(8,128)(2,1)S(1)} %get-tuple-element.40), channel_id=1, source_target_pairs={{0,7},{1,0},{2,1},{3,2},{4,3},{5,4},{6,5},{7,6},{8,15},{9,8},{10,9... | collective-permute-start | bytes 614408 | tf_op jit(solution)/shard_map/ppermute | solution.py:32
  25.2 34.4 %collective-permute-start.7 = (bf16[2,200,256]{2,1,0:T(8,128)(2,1)S(1)}, bf16[2,200,256]{2,1,0:T(8,128)(2,1)S(1)}, u32[]{:S(2)}, u32[]{:S(2)}) collective-permute-start(bf16[2,200,256]{2,1,0:T(8,128)(2,1)S(1)} %get-tuple-element.43), channel_id=1, source_target_pairs={{0,4},{1,5},{2,6},{3,7},{4,0},{5,1},{6,2},{7,3},{8,12},{9,13},{10,... | collective-permute-start | bytes 614408 | tf_op jit(solution)/shard_map/ppermute | solution.py:32
  29.3 59.9 %collective-permute-start.1 = (bf16[256,1024]{1,0:T(8,128)(2,1)}, bf16[256,1024]{1,0:T(8,128)(2,1)}, u32[]{:S(2)}, u32[]{:S(2)}) collective-permute-start(bf16[256,1024]{1,0:T(8,128)(2,1)} %collective-permute-done), channel_id=1, source_target_pairs={{40,256},{137,257},{202,258},{59,259},{236,260},{189,261},{30,262}... | collective-permute-start | bytes 1572872 | tf_op jit(solution)/shard_map/ppermute | solution.py:236
  31.1 30.4 %collective-permute-start.9 = (bf16[2,200,256]{2,1,0:T(8,128)(2,1)S(1)}, bf16[2,200,256]{2,1,0:T(8,128)(2,1)S(1)}, u32[]{:S(2)}, u32[]{:S(2)}) collective-permute-start(bf16[2,200,256]{2,1,0:T(8,128)(2,1)S(1)} %get-tuple-element.46), channel_id=1, source_target_pairs={{0,2},{1,3},{2,4},{3,5},{4,6},{5,7},{6,0},{7,1},{8,10},{9,11},{10,... | collective-permute-start | bytes 614408 | tf_op jit(solution)/shard_map/ppermute | solution.py:32
  33.9 60.7 %collective-permute-start.4 = (bf16[2,200,256]{2,1,0:T(8,128)(2,1)S(1)}, bf16[2,200,256]{2,1,0:T(8,128)(2,1)S(1)}, u32[]{:S(2)}, u32[]{:S(2)}) collective-permute-start(bf16[2,200,256]{2,1,0:T(8,128)(2,1)S(1)} %get-tuple-element.38), channel_id=1, source_target_pairs={{0,6},{1,7},{2,0},{3,1},{4,2},{5,3},{6,4},{7,5},{8,14},{9,15},{10,... | collective-permute-start | bytes 614408 | tf_op jit(solution)/shard_map/ppermute | solution.py:32
  59.6 35.0 %collective-permute-start.6 = (bf16[2,200,256]{2,1,0:T(8,128)(2,1)S(1)}, bf16[2,200,256]{2,1,0:T(8,128)(2,1)S(1)}, u32[]{:S(2)}, u32[]{:S(2)}) collective-permute-start(bf16[2,200,256]{2,1,0:T(8,128)(2,1)S(1)} %get-tuple-element.41), channel_id=1, source_target_pairs={{0,3},{1,4},{2,5},{3,6},{4,7},{5,0},{6,1},{7,2},{8,11},{9,12},{10,... | collective-permute-start | bytes 614408 | tf_op jit(solution)/shard_map/ppermute | solution.py:32
  61.5 33.1 %collective-permute-start.8 = (bf16[2,200,256]{2,1,0:T(8,128)(2,1)S(1)}, bf16[2,200,256]{2,1,0:T(8,128)(2,1)S(1)}, u32[]{:S(2)}, u32[]{:S(2)}) collective-permute-start(bf16[2,200,256]{2,1,0:T(8,128)(2,1)S(1)} %get-tuple-element.44), channel_id=1, source_target_pairs={{0,5},{1,6},{2,7},{3,0},{4,1},{5,2},{6,3},{7,4},{8,13},{9,14},{10,... | collective-permute-start | bytes 614408 | tf_op jit(solution)/shard_map/ppermute | solution.py:32
  90.3 4.3 %copy-start.3 = (bf16[128,1024]{1,0:T(8,128)(2,1)S(1)}, bf16[128,1024]{1,0:T(8,128)(2,1)}, u32[]{:S(2)}) copy-start(bf16[128,1024]{1,0:T(8,128)(2,1)} %refs_3_.3) | copy-start | bytes 786436
  97.8 5.6 %collective-permute-start.11 = (f32[8,1024]{1,0:T(8,128)S(1)}, f32[8,1024]{1,0:T(8,128)S(1)}, u32[]{:S(2)}, u32[]{:S(2)}) collective-permute-start(f32[8,1024]{1,0:T(8,128)S(1)} %get-tuple-element.75), channel_id=1, source_target_pairs={{0,8},{8,16},{16,24},{24,32},{32,40},{40,48},{48,56},{56,64},{64,7... | collective-permute-start | bytes 98312 | tf_op jit(solution)/shard_map/ppermute | solution.py:32
  99.7 5.2 %collective-permute-start.10 = (f32[8,1024]{1,0:T(8,128)S(1)}, f32[8,1024]{1,0:T(8,128)S(1)}, u32[]{:S(2)}, u32[]{:S(2)}) collective-permute-start(f32[8,1024]{1,0:T(8,128)S(1)} %get-tuple-element.76), channel_id=1, source_target_pairs={{0,504},{8,0},{16,8},{24,16},{32,24},{40,32},{48,40},{56,48},{64,5... | collective-permute-start | bytes 98312 | tf_op jit(solution)/shard_map/ppermute | solution.py:32
  115.8 17.9 %collective-permute-start.12 = (bf16[256,1024]{1,0:T(8,128)(2,1)}, bf16[256,1024]{1,0:T(8,128)(2,1)}, u32[]{:S(2)}, u32[]{:S(2)}) collective-permute-start(bf16[256,1024]{1,0:T(8,128)(2,1)} %constant_dynamic-update-slice_fusion), channel_id=1, source_target_pairs={{0,40},{1,137},{2,202},{3,59},{4,236},{5,189},{6,30},{7,79},{256,2... | collective-permute-start | bytes 1572872 | tf_op jit(solution)/shard_map/ppermute | solution.py:236
  117.3 72.8 %collective-permute-start.14 = (bf16[256,1024]{1,0:T(8,128)(2,1)}, bf16[256,1024]{1,0:T(8,128)(2,1)}, u32[]{:S(2)}, u32[]{:S(2)}) collective-permute-start(bf16[256,1024]{1,0:T(8,128)(2,1)} %constant_dynamic-update-slice_fusion), channel_id=1, source_target_pairs={{8,0},{16,8},{24,16},{32,24},{40,32},{48,40},{56,48},{64,56},{72,6... | collective-permute-start | bytes 1572872 | tf_op jit(solution)/shard_map/ppermute | solution.py:226
  133.8 56.3 %collective-permute-start.13 = (bf16[256,1024]{1,0:T(8,128)(2,1)}, bf16[256,1024]{1,0:T(8,128)(2,1)}, u32[]{:S(2)}, u32[]{:S(2)}) collective-permute-start(bf16[256,1024]{1,0:T(8,128)(2,1)} %collective-permute-done.12), channel_id=1, source_target_pairs={{40,504},{137,505},{202,506},{59,507},{236,508},{189,509},{30,510}... | collective-permute-start | bytes 1572872 | tf_op jit(solution)/shard_map/ppermute | solution.py:236
  135.2 13.6 %collective-permute-start.15 = (bf16[2,200,256]{2,1,0:T(8,128)(2,1)S(1)}, bf16[2,200,256]{2,1,0:T(8,128)(2,1)S(1)}, u32[]{:S(2)}, u32[]{:S(2)}) collective-permute-start(bf16[2,200,256]{2,1,0:T(8,128)(2,1)S(1)} %get-tuple-element.56), channel_id=1, source_target_pairs={{0,6},{1,7},{2,0},{3,1},{4,2},{5,3},{6,4},{7,5},{8,14},{9,15},{10,... | collective-permute-start | bytes 614408 | tf_op jit(solution)/shard_map/ppermute | solution.py:32
  138.0 16.1 %collective-permute-start.16 = (bf16[2,200,256]{2,1,0:T(8,128)(2,1)}, bf16[2,200,256]{2,1,0:T(8,128)(2,1)S(1)}, u32[]{:S(2)}, u32[]{:S(2)}) collective-permute-start(bf16[2,200,256]{2,1,0:T(8,128)(2,1)} %get-tuple-element.58), channel_id=1, source_target_pairs={{0,7},{1,0},{2,1},{3,2},{4,3},{5,4},{6,5},{7,6},{8,15},{9,8},{10,9... | collective-permute-start | bytes 614408 | tf_op jit(solution)/shard_map/ppermute | solution.py:32
  146.9 13.5 %collective-permute-start.17 = (bf16[2,200,256]{2,1,0:T(8,128)(2,1)}, bf16[2,200,256]{2,1,0:T(8,128)(2,1)S(1)}, u32[]{:S(2)}, u32[]{:S(2)}) collective-permute-start(bf16[2,200,256]{2,1,0:T(8,128)(2,1)} %get-tuple-element.60), channel_id=1, source_target_pairs={{0,1},{1,2},{2,3},{3,4},{4,5},{5,6},{6,7},{7,0},{8,9},{9,10},{10,1... | collective-permute-start | bytes 614408 | tf_op jit(solution)/shard_map/ppermute | solution.py:32
  148.9 39.3 %collective-permute-start.19 = (bf16[2,200,256]{2,1,0:T(8,128)(2,1)S(1)}, bf16[2,200,256]{2,1,0:T(8,128)(2,1)S(1)}, u32[]{:S(2)}, u32[]{:S(2)}) collective-permute-start(bf16[2,200,256]{2,1,0:T(8,128)(2,1)S(1)} %get-tuple-element.62), channel_id=1, source_target_pairs={{0,4},{1,5},{2,6},{3,7},{4,0},{5,1},{6,2},{7,3},{8,12},{9,13},{10,... | collective-permute-start | bytes 614408 | tf_op jit(solution)/shard_map/ppermute | solution.py:32
  154.1 37.1 %collective-permute-start.21 = (bf16[2,200,256]{2,1,0:T(8,128)(2,1)S(1)}, bf16[2,200,256]{2,1,0:T(8,128)(2,1)S(1)}, u32[]{:S(2)}, u32[]{:S(2)}) collective-permute-start(bf16[2,200,256]{2,1,0:T(8,128)(2,1)S(1)} %get-tuple-element.66), channel_id=1, source_target_pairs={{0,2},{1,3},{2,4},{3,5},{4,6},{5,7},{6,0},{7,1},{8,10},{9,11},{10,... | collective-permute-start | bytes 614408 | tf_op jit(solution)/shard_map/ppermute | solution.py:32
  160.4 31.2 %collective-permute-start.18 = (bf16[2,200,256]{2,1,0:T(8,128)(2,1)S(1)}, bf16[2,200,256]{2,1,0:T(8,128)(2,1)S(1)}, u32[]{:S(2)}, u32[]{:S(2)}) collective-permute-start(bf16[2,200,256]{2,1,0:T(8,128)(2,1)S(1)} %get-tuple-element.61), channel_id=1, source_target_pairs={{0,5},{1,6},{2,7},{3,0},{4,1},{5,2},{6,3},{7,4},{8,13},{9,14},{10,... | collective-permute-start | bytes 614408 | tf_op jit(solution)/shard_map/ppermute | solution.py:32
  188.2 29.2 %collective-permute-start.20 = (bf16[2,200,256]{2,1,0:T(8,128)(2,1)S(1)}, bf16[2,200,256]{2,1,0:T(8,128)(2,1)S(1)}, u32[]{:S(2)}, u32[]{:S(2)}) collective-permute-start(bf16[2,200,256]{2,1,0:T(8,128)(2,1)S(1)} %get-tuple-element.64), channel_id=1, source_target_pairs={{0,3},{1,4},{2,5},{3,6},{4,7},{5,0},{6,1},{7,2},{8,11},{9,12},{10,... | collective-permute-start | bytes 614408 | tf_op jit(solution)/shard_map/ppermute | solution.py:32

commit v5 on v4

--- a/solution.py
+++ b/solution.py
@@ -15,7 +15,7 @@
 LOG2E = 1.4426950408889634
 SCALE = HEAD ** (-0.5)
 SCALE2 = SCALE * LOG2E
-WINDOW = 4
+WINDOW = 5
 
 NT = (((1,), (1,)), ((), ()))
 TN = (((0,), (0,)), ((), ()))

time: 220 us -> 214 us (0.973); the launches traced: 219 us -> 211 us
  waiting for transfers between devices: 73.3 us -> 64.1 us
    ppermute x16, waiting for transfers between devices: 73.2 us -> 64.1 us  [shift(): return lax.ppermute(value, axis, pairs)]
    ppermute x16, starting transfers between devices: 88.5 us -> 93.2 us  [shift(): return lax.ppermute(value, axis, pairs)]
    ppermute x2, starting transfers between devices: 21 us -> 17 us  [within(): return lax.ppermute(value, 'dp', inside)]
where the time goes in v5:
time: 214 us; the launch traced here: 211 us
  starting transfers between devices  116 us (54%)
  waiting for transfers between devices  64.1 us (30%)
  Pallas kernels  19.4 us (9%)
  local copies, waits for them, and re-layouts  5.83 us (3%)
  other arithmetic  3.98 us (2%)
    ppermute x16, starting transfers between devices, shift(): return lax.ppermute(value, axis, pairs)  93.2 us
    ppermute x16, waiting for transfers between devices, shift(): return lax.ppermute(value, axis, pairs)  64.1 us
    pallas_call x5, Pallas kernels, call(): pl.pallas_call(kernel, out_shape=[jax.ShapeDtypeStruct(*o) for o in outs]...  19.4 us
    ppermute x2, starting transfers between devices, within(): return lax.ppermute(value, 'dp', inside)  17 us
    ppermute x4, starting transfers between devices, send(): lax.ppermute(part, ('dp', 'tensor'), [(d * n + t, e * n + t) for d, e, t...  5.97 us
  transfers between devices with their start and end apart: 22, of which 6 were waited for; matrix products, arithmetic and copies ran while one was open for 3% of the time, Pallas kernels for 2%

profile of v5, /device:TPU:1, one launch (start us, length us, event | category | flops | bytes accessed | tf_op | source)
XLA Modules:
  0.0 210.6 jit_solution(1018908970777071504)
XLA Ops:
  0.6 0.0 copy-start
  0.6 0.9 copy-done
  1.6 0.9 copy-done.2
  2.5 1.4 copy-done.4
  4.0 0.3 split.1
  4.2 0.0 copy-start.1
  4.2 1.6 collective-permute-start
  5.8 4.5 %collective-permute-start.2 = (bf16[256,1024]{1,0:T(8,128)(2,1)S(1)}, bf16[256,1024]{1,0:T(8,128)(2,1)}, u32[]{:S(2)}, u32[]{:S(2)}) collective-permute-start(bf16[256,1024]{1,0:T(8,128)(2,1)S(1)} %get-tuple-element.33), channel_id=1, source_target_pairs={{0,8},{8,16},{16,24},{24,32},{32,40},{40,48},{48,56},{56,64},{64,7... | collective-permute-start | bytes 1572872 | tf_op jit(solution)/shard_map/ppermute | solution.py:226
  10.3 3.5 %collective-permute-start.3 = (bf16[2,200,256]{2,1,0:T(8,128)(2,1)S(1)}, bf16[2,200,256]{2,1,0:T(8,128)(2,1)S(1)}, u32[]{:S(2)}, u32[]{:S(2)}) collective-permute-start(bf16[2,200,256]{2,1,0:T(8,128)(2,1)S(1)} %get-tuple-element.35), channel_id=1, source_target_pairs={{0,1},{1,2},{2,3},{3,4},{4,5},{5,6},{6,7},{7,0},{8,9},{9,10},{10,1... | collective-permute-start | bytes 614408 | tf_op jit(solution)/shard_map/ppermute | solution.py:32
  13.9 11.3 %collective-permute-start.5 = (bf16[2,200,256]{2,1,0:T(8,128)(2,1)S(1)}, bf16[2,200,256]{2,1,0:T(8,128)(2,1)S(1)}, u32[]{:S(2)}, u32[]{:S(2)}) collective-permute-start(bf16[2,200,256]{2,1,0:T(8,128)(2,1)S(1)} %get-tuple-element.38), channel_id=1, source_target_pairs={{0,7},{1,0},{2,1},{3,2},{4,3},{5,4},{6,5},{7,6},{8,15},{9,8},{10,9... | collective-permute-start | bytes 614408 | tf_op jit(solution)/shard_map/ppermute | solution.py:32
  25.2 1.9 collective-permute-start.7
  27.1 0.6 fusion.5
  27.7 0.2 dynamic-slice_reduce_fusion
  28.0 1.3 iota_compare_fusion
  29.3 0.0 collective-permute-done
  29.3 1.5 collective-permute-start.1
  30.7 0.2 fusion.1
  30.9 0.2 fusion.3
  31.1 0.1 copy.11
  31.2 0.1 copy.12
  31.3 0.1 pad_add_fusion.refs_0_
  31.4 0.0 collective-permute-done.3.refs_4_.refs_8_
  31.4 2.5 %collective-permute-start.8 = (bf16[2,200,256]{2,1,0:T(8,128)(2,1)S(1)}, bf16[2,200,256]{2,1,0:T(8,128)(2,1)S(1)}, u32[]{:S(2)}, u32[]{:S(2)}) collective-permute-start(bf16[2,200,256]{2,1,0:T(8,128)(2,1)S(1)} %get-tuple-element.43), channel_id=1, source_target_pairs={{0,2},{1,3},{2,4},{3,5},{4,6},{5,7},{6,0},{7,1},{8,10},{9,11},{10,... | collective-permute-start | bytes 614408 | tf_op jit(solution)/shard_map/ppermute | solution.py:32
  33.9 0.0 collective-permute-done.5.refs_5_.refs_9_
  33.9 8.5 %collective-permute-start.9 = (bf16[2,200,256]{2,1,0:T(8,128)(2,1)S(1)}, bf16[2,200,256]{2,1,0:T(8,128)(2,1)S(1)}, u32[]{:S(2)}, u32[]{:S(2)}) collective-permute-start(bf16[2,200,256]{2,1,0:T(8,128)(2,1)S(1)} %get-tuple-element.44), channel_id=1, source_target_pairs={{0,6},{1,7},{2,0},{3,1},{4,2},{5,3},{6,4},{7,5},{8,14},{9,15},{10,... | collective-permute-start | bytes 614408 | tf_op jit(solution)/shard_map/ppermute | solution.py:32
  42.4 17.1 %collective-permute-done.7.refs_6_.refs_10_ = bf16[2,200,256]{2,1,0:T(8,128)(2,1)S(1)} collective-permute-done((bf16[2,200,256]{2,1,0:T(8,128)(2,1)S(1)}, bf16[2,200,256]{2,1,0:T(8,128)(2,1)S(1)}, u32[]{:S(2)}, u32[]{:S(2)}) %collective-permute-start.7) | collective-permute-done | bytes 204832 | tf_op jit(solution)/shard_map/ppermute | solution.py:32
  59.6 1.9 collective-permute-start.4
  61.5 0.0 collective-permute-done.2
  61.5 8.2 %collective-permute-start.6 = (bf16[2,200,256]{2,1,0:T(8,128)(2,1)S(1)}, bf16[2,200,256]{2,1,0:T(8,128)(2,1)S(1)}, u32[]{:S(2)}, u32[]{:S(2)}) collective-permute-start(bf16[2,200,256]{2,1,0:T(8,128)(2,1)S(1)} %get-tuple-element.39), channel_id=1, source_target_pairs={{0,5},{1,6},{2,7},{3,0},{4,1},{5,2},{6,3},{7,4},{8,13},{9,14},{10,... | collective-permute-start | bytes 614408 | tf_op jit(solution)/shard_map/ppermute | solution.py:32
  69.7 0.0 collective-permute-done.1
  69.7 1.1 broadcast_select_fusion.1
  70.8 0.0 copy-start.3
  70.8 0.0 collective-permute-done.8.refs_7_.refs_11_
  70.9 0.0 collective-permute-done.9.refs_8_.refs_12_
  70.9 4.9 %attend.2 = (f32[2,128,1024]{2,1,0:T(8,128)S(1)}, f32[2,8,1024]{2,1,0:T(8,128)S(1)}) custom-call(s32[2,2]{1,0:T(2,128)S(1)} %pad_add_fusion.refs_0_, bf16[128,1024]{1,0:T(8,128)(2,1)S(1)} %copy-done.1, bf16[128,1024]{1,0:T(8,128)(2,1)S(1)} %get-tuple-element.70.refs_2_, bf16[2,200,256]{2,1,0:T(8,128)(2,1)S(1)} %get-tuple-element.42.refs_3_.refs_15_, ...), custom_call_target="tpu_custom_call" | custom-call | bytes 1048576 | tf_op jit(solution)/shard_map/attend/pallas_call | solution.py:205
  75.8 10.4 %collective-permute-done.4.refs_5_.refs_13_ = bf16[2,200,256]{2,1,0:T(8,128)(2,1)S(1)} collective-permute-done((bf16[2,200,256]{2,1,0:T(8,128)(2,1)S(1)}, bf16[2,200,256]{2,1,0:T(8,128)(2,1)S(1)}, u32[]{:S(2)}, u32[]{:S(2)}) %collective-permute-start.4) | collective-permute-done | bytes 204832 | tf_op jit(solution)/shard_map/ppermute | solution.py:32
  86.1 0.0 collective-permute-done.6.refs_6_.refs_14_
  86.1 2.5 %attend.3 = (f32[128,1024]{1,0:T(8,128)S(1)}, bf16[128,1024]{1,0:T(8,128)(2,1)S(1)}, f32[2,8,1024]{2,1,0:T(8,128)S(1)}) custom-call(s32[2,2]{1,0:T(2,128)S(1)} %pad_add_fusion.refs_0_, bf16[128,1024]{1,0:T(8,128)(2,1)S(1)} %copy-done.1, bf16[128,1024]{1,0:T(8,128)(2,1)S(1)} %get-tuple-element.70.refs_2_, bf16[128,1024]{1,0:T(8,128)(2,1)S(1)} %copy-done.3, ...), custom_call_target="tpu_custom_call" | custom-call | bytes 1048576 | tf_op jit(solution)/shard_map/attend/pallas_call | solution.py:205
  88.6 5.4 %collective-permute-start.11 = (f32[8,1024]{1,0:T(8,128)S(1)}, f32[8,1024]{1,0:T(8,128)S(1)}, u32[]{:S(2)}, u32[]{:S(2)}) collective-permute-start(f32[8,1024]{1,0:T(8,128)S(1)} %get-tuple-element.71), channel_id=1, source_target_pairs={{0,8},{8,16},{16,24},{24,32},{32,40},{40,48},{48,56},{56,64},{64,7... | collective-permute-start | bytes 98312 | tf_op jit(solution)/shard_map/ppermute | solution.py:32
  94.0 2.1 collective-permute-start.10
  96.1 0.7 constant_dynamic-update-slice_fusion.1
  96.8 0.0 collective-permute-done.11.refs_7_
  96.8 2.4 %collective-permute-done.10.refs_6_.far = f32[8,1024]{1,0:T(8,128)S(1)} collective-permute-done((f32[8,1024]{1,0:T(8,128)S(1)}, f32[8,1024]{1,0:T(8,128)S(1)}, u32[]{:S(2)}, u32[]{:S(2)}) %collective-permute-start.10) | collective-permute-done | bytes 32800 | tf_op jit(solution)/shard_map/ppermute | solution.py:32
  99.2 10.2 %backward.1 = (f32[128,1024]{1,0:T(8,128)S(1)}, bf16[128,1024]{1,0:T(8,128)(2,1)S(1)}, bf16[2,200,256]{2,1,0:T(8,128)(2,1)}, bf16[2,200,256]{2,1,0:T(8,128)(2,1)...) custom-call(s32[2,2]{1,0:T(2,128)S(1)} %pad_add_fusion.refs_0_, ...), custom_call_target="tpu_custom_call" | custom-call | bytes 1048576 | tf_op jit(solution)/shard_map/backward/pallas_call | solution.py:205
  109.4 0.7 constant_dynamic-update-slice_fusion
  110.1 1.4 collective-permute-start.12
  111.6 12.5 %collective-permute-start.14 = (bf16[256,1024]{1,0:T(8,128)(2,1)}, bf16[256,1024]{1,0:T(8,128)(2,1)}, u32[]{:S(2)}, u32[]{:S(2)}) collective-permute-start(bf16[256,1024]{1,0:T(8,128)(2,1)} %constant_dynamic-update-slice_fusion), channel_id=1, source_target_pairs={{8,0},{16,8},{24,16},{32,24},{40,32},{48,40},{56,48},{64,56},{72,6... | collective-permute-start | bytes 1572872 | tf_op jit(solution)/shard_map/ppermute | solution.py:226
  124.1 0.0 collective-permute-done.12
  124.1 1.5 collective-permute-start.13
  125.6 9.7 %collective-permute-start.15 = (bf16[2,200,256]{2,1,0:T(8,128)(2,1)}, bf16[2,200,256]{2,1,0:T(8,128)(2,1)S(1)}, u32[]{:S(2)}, u32[]{:S(2)}) collective-permute-start(bf16[2,200,256]{2,1,0:T(8,128)(2,1)} %get-tuple-element.53), channel_id=1, source_target_pairs={{0,4},{1,5},{2,6},{3,7},{4,0},{5,1},{6,2},{7,3},{8,12},{9,13},{10,... | collective-permute-start | bytes 614408 | tf_op jit(solution)/shard_map/ppermute | solution.py:32
  135.3 7.4 %collective-permute-start.16 = (bf16[2,200,256]{2,1,0:T(8,128)(2,1)}, bf16[2,200,256]{2,1,0:T(8,128)(2,1)S(1)}, u32[]{:S(2)}, u32[]{:S(2)}) collective-permute-start(bf16[2,200,256]{2,1,0:T(8,128)(2,1)} %get-tuple-element.55), channel_id=1, source_target_pairs={{0,7},{1,0},{2,1},{3,2},{4,3},{5,4},{6,5},{7,6},{8,15},{9,8},{10,9... | collective-permute-start | bytes 614408 | tf_op jit(solution)/shard_map/ppermute | solution.py:32
  142.8 1.9 collective-permute-start.19
  144.7 0.0 collective-permute-done.15.refs_4_
  144.7 18.6 %collective-permute-start.17 = (bf16[2,200,256]{2,1,0:T(8,128)(2,1)S(1)}, bf16[2,200,256]{2,1,0:T(8,128)(2,1)S(1)}, u32[]{:S(2)}, u32[]{:S(2)}) collective-permute-start(bf16[2,200,256]{2,1,0:T(8,128)(2,1)S(1)} %get-tuple-element.56), channel_id=1, source_target_pairs={{0,6},{1,7},{2,0},{3,1},{4,2},{5,3},{6,4},{7,5},{8,14},{9,15},{10,... | collective-permute-start | bytes 614408 | tf_op jit(solution)/shard_map/ppermute | solution.py:32
  163.3 0.0 collective-permute-done.16.refs_1_
  163.3 1.9 collective-permute-start.21
  165.2 6.5 %collective-permute-start.18 = (bf16[2,200,256]{2,1,0:T(8,128)(2,1)S(1)}, bf16[2,200,256]{2,1,0:T(8,128)(2,1)S(1)}, u32[]{:S(2)}, u32[]{:S(2)}) collective-permute-start(bf16[2,200,256]{2,1,0:T(8,128)(2,1)S(1)} %get-tuple-element.58), channel_id=1, source_target_pairs={{0,5},{1,6},{2,7},{3,0},{4,1},{5,2},{6,3},{7,4},{8,13},{9,14},{10,... | collective-permute-start | bytes 614408 | tf_op jit(solution)/shard_map/ppermute | solution.py:32
  171.7 1.9 collective-permute-start.20
  173.6 0.0 collective-permute-done.13
  173.6 1.1 broadcast_select_fusion.both
  174.8 2.3 %collective-permute-done.21.refs_6_ = bf16[2,200,256]{2,1,0:T(8,128)(2,1)S(1)} collective-permute-done((bf16[2,200,256]{2,1,0:T(8,128)(2,1)S(1)}, bf16[2,200,256]{2,1,0:T(8,128)(2,1)S(1)}, u32[]{:S(2)}, u32[]{:S(2)}) %collective-permute-start.21) | collective-permute-done | bytes 204832 | tf_op jit(solution)/shard_map/ppermute | solution.py:32
  177.1 16.5 %collective-permute-done.18.refs_3_ = bf16[2,200,256]{2,1,0:T(8,128)(2,1)S(1)} collective-permute-done((bf16[2,200,256]{2,1,0:T(8,128)(2,1)S(1)}, bf16[2,200,256]{2,1,0:T(8,128)(2,1)S(1)}, u32[]{:S(2)}, u32[]{:S(2)}) %collective-permute-start.18) | collective-permute-done | bytes 204832 | tf_op jit(solution)/shard_map/ppermute | solution.py:32
  193.6 15.3 %collective-permute-done.20.refs_5_ = bf16[2,200,256]{2,1,0:T(8,128)(2,1)S(1)} collective-permute-done((bf16[2,200,256]{2,1,0:T(8,128)(2,1)S(1)}, bf16[2,200,256]{2,1,0:T(8,128)(2,1)S(1)}, u32[]{:S(2)}, u32[]{:S(2)}) %collective-permute-start.20) | collective-permute-done | bytes 204832 | tf_op jit(solution)/shard_map/ppermute | solution.py:32
  208.9 1.6 finish.1
  (17 shorter events, 0.1 us)
Async XLA Ops:
  0.6 1.0 copy-start
  1.6 0.9 copy-start.2
  2.5 1.4 copy-start.4
  4.0 23.2 %copy-start.7 = (s32[64]{0:T(128)S(1)}, s32[64]{0:T(128)}, u32[]{:S(2)}) copy-start(s32[64]{0:T(128)} %param.10) | copy-start | bytes 772
  4.0 23.8 %copy-start.5 = (s32[64,4]{0,1:T(4,128)S(1)}, s32[64,4]{0,1:T(4,128)}, u32[]{:S(2)}) copy-start(s32[64,4]{0,1:T(4,128)} %param.11) | copy-start | bytes 3076
  4.0 23.8 %copy-start.6 = (s32[64,4]{0,1:T(4,128)S(1)}, s32[64,4]{0,1:T(4,128)}, u32[]{:S(2)}) copy-start(s32[64,4]{0,1:T(4,128)} %param.9) | copy-start | bytes 3076
  4.2 66.6 %copy-start.1 = (bf16[128,1024]{1,0:T(8,128)(2,1)S(1)}, bf16[128,1024]{1,0:T(8,128)(2,1)}, u32[]{:S(2)}) copy-start(bf16[128,1024]{1,0:T(8,128)(2,1)} %refs_1_.5) | copy-start | bytes 786436
  4.2 25.0 %collective-permute-start = (bf16[256,1024]{1,0:T(8,128)(2,1)S(1)}, bf16[256,1024]{1,0:T(8,128)(2,1)}, u32[]{:S(2)}, u32[]{:S(2)}) collective-permute-start(bf16[256,1024]{1,0:T(8,128)(2,1)S(1)} %get-tuple-element.33), channel_id=1, source_target_pairs={{248,40},{249,137},{250,202},{251,59},{252,236},{253,189},{254,30}... | collective-permute-start | bytes 1572872 | tf_op jit(solution)/shard_map/ppermute | solution.py:236
  5.8 55.6 %collective-permute-start.2 = (bf16[256,1024]{1,0:T(8,128)(2,1)S(1)}, bf16[256,1024]{1,0:T(8,128)(2,1)}, u32[]{:S(2)}, u32[]{:S(2)}) collective-permute-start(bf16[256,1024]{1,0:T(8,128)(2,1)S(1)} %get-tuple-element.33), channel_id=1, source_target_pairs={{0,8},{8,16},{16,24},{24,32},{32,40},{40,48},{48,56},{56,64},{64,7... | collective-permute-start | bytes 1572872 | tf_op jit(solution)/shard_map/ppermute | solution.py:226
  10.3 21.1 %collective-permute-start.3 = (bf16[2,200,256]{2,1,0:T(8,128)(2,1)S(1)}, bf16[2,200,256]{2,1,0:T(8,128)(2,1)S(1)}, u32[]{:S(2)}, u32[]{:S(2)}) collective-permute-start(bf16[2,200,256]{2,1,0:T(8,128)(2,1)S(1)} %get-tuple-element.35), channel_id=1, source_target_pairs={{0,1},{1,2},{2,3},{3,4},{4,5},{5,6},{6,7},{7,0},{8,9},{9,10},{10,1... | collective-permute-start | bytes 614408 | tf_op jit(solution)/shard_map/ppermute | solution.py:32
  13.9 20.0 %collective-permute-start.5 = (bf16[2,200,256]{2,1,0:T(8,128)(2,1)S(1)}, bf16[2,200,256]{2,1,0:T(8,128)(2,1)S(1)}, u32[]{:S(2)}, u32[]{:S(2)}) collective-permute-start(bf16[2,200,256]{2,1,0:T(8,128)(2,1)S(1)} %get-tuple-element.38), channel_id=1, source_target_pairs={{0,7},{1,0},{2,1},{3,2},{4,3},{5,4},{6,5},{7,6},{8,15},{9,8},{10,9... | collective-permute-start | bytes 614408 | tf_op jit(solution)/shard_map/ppermute | solution.py:32
  25.2 34.4 %collective-permute-start.7 = (bf16[2,200,256]{2,1,0:T(8,128)(2,1)S(1)}, bf16[2,200,256]{2,1,0:T(8,128)(2,1)S(1)}, u32[]{:S(2)}, u32[]{:S(2)}) collective-permute-start(bf16[2,200,256]{2,1,0:T(8,128)(2,1)S(1)} %get-tuple-element.41), channel_id=1, source_target_pairs={{0,4},{1,5},{2,6},{3,7},{4,0},{5,1},{6,2},{7,3},{8,12},{9,13},{10,... | collective-permute-start | bytes 614408 | tf_op jit(solution)/shard_map/ppermute | solution.py:32
  29.3 40.4 %collective-permute-start.1 = (bf16[256,1024]{1,0:T(8,128)(2,1)}, bf16[256,1024]{1,0:T(8,128)(2,1)}, u32[]{:S(2)}, u32[]{:S(2)}) collective-permute-start(bf16[256,1024]{1,0:T(8,128)(2,1)} %collective-permute-done), channel_id=1, source_target_pairs={{40,256},{137,257},{202,258},{59,259},{236,260},{189,261},{30,262}... | collective-permute-start | bytes 1572872 | tf_op jit(solution)/shard_map/ppermute | solution.py:236
  31.4 39.4 %collective-permute-start.8 = (bf16[2,200,256]{2,1,0:T(8,128)(2,1)S(1)}, bf16[2,200,256]{2,1,0:T(8,128)(2,1)S(1)}, u32[]{:S(2)}, u32[]{:S(2)}) collective-permute-start(bf16[2,200,256]{2,1,0:T(8,128)(2,1)S(1)} %get-tuple-element.43), channel_id=1, source_target_pairs={{0,2},{1,3},{2,4},{3,5},{4,6},{5,7},{6,0},{7,1},{8,10},{9,11},{10,... | collective-permute-start | bytes 614408 | tf_op jit(solution)/shard_map/ppermute | solution.py:32
  33.9 37.0 %collective-permute-start.9 = (bf16[2,200,256]{2,1,0:T(8,128)(2,1)S(1)}, bf16[2,200,256]{2,1,0:T(8,128)(2,1)S(1)}, u32[]{:S(2)}, u32[]{:S(2)}) collective-permute-start(bf16[2,200,256]{2,1,0:T(8,128)(2,1)S(1)} %get-tuple-element.44), channel_id=1, source_target_pairs={{0,6},{1,7},{2,0},{3,1},{4,2},{5,3},{6,4},{7,5},{8,14},{9,15},{10,... | collective-permute-start | bytes 614408 | tf_op jit(solution)/shard_map/ppermute | solution.py:32
  59.6 26.6 %collective-permute-start.4 = (bf16[2,200,256]{2,1,0:T(8,128)(2,1)S(1)}, bf16[2,200,256]{2,1,0:T(8,128)(2,1)S(1)}, u32[]{:S(2)}, u32[]{:S(2)}) collective-permute-start(bf16[2,200,256]{2,1,0:T(8,128)(2,1)S(1)} %get-tuple-element.36), channel_id=1, source_target_pairs={{0,3},{1,4},{2,5},{3,6},{4,7},{5,0},{6,1},{7,2},{8,11},{9,12},{10,... | collective-permute-start | bytes 614408 | tf_op jit(solution)/shard_map/ppermute | solution.py:32
  61.5 24.6 %collective-permute-start.6 = (bf16[2,200,256]{2,1,0:T(8,128)(2,1)S(1)}, bf16[2,200,256]{2,1,0:T(8,128)(2,1)S(1)}, u32[]{:S(2)}, u32[]{:S(2)}) collective-permute-start(bf16[2,200,256]{2,1,0:T(8,128)(2,1)S(1)} %get-tuple-element.39), channel_id=1, source_target_pairs={{0,5},{1,6},{2,7},{3,0},{4,1},{5,2},{6,3},{7,4},{8,13},{9,14},{10,... | collective-permute-start | bytes 614408 | tf_op jit(solution)/shard_map/ppermute | solution.py:32
  70.8 15.3 %copy-start.3 = (bf16[128,1024]{1,0:T(8,128)(2,1)S(1)}, bf16[128,1024]{1,0:T(8,128)(2,1)}, u32[]{:S(2)}) copy-start(bf16[128,1024]{1,0:T(8,128)(2,1)} %refs_3_.3) | copy-start | bytes 786436
  88.6 8.2 %collective-permute-start.11 = (f32[8,1024]{1,0:T(8,128)S(1)}, f32[8,1024]{1,0:T(8,128)S(1)}, u32[]{:S(2)}, u32[]{:S(2)}) collective-permute-start(f32[8,1024]{1,0:T(8,128)S(1)} %get-tuple-element.71), channel_id=1, source_target_pairs={{0,8},{8,16},{16,24},{24,32},{32,40},{40,48},{48,56},{56,64},{64,7... | collective-permute-start | bytes 98312 | tf_op jit(solution)/shard_map/ppermute | solution.py:32
  94.0 5.2 %collective-permute-start.10 = (f32[8,1024]{1,0:T(8,128)S(1)}, f32[8,1024]{1,0:T(8,128)S(1)}, u32[]{:S(2)}, u32[]{:S(2)}) collective-permute-start(f32[8,1024]{1,0:T(8,128)S(1)} %get-tuple-element.72), channel_id=1, source_target_pairs={{0,504},{8,0},{16,8},{24,16},{32,24},{40,32},{48,40},{56,48},{64,5... | collective-permute-start | bytes 98312 | tf_op jit(solution)/shard_map/ppermute | solution.py:32
  110.1 14.0 %collective-permute-start.12 = (bf16[256,1024]{1,0:T(8,128)(2,1)}, bf16[256,1024]{1,0:T(8,128)(2,1)}, u32[]{:S(2)}, u32[]{:S(2)}) collective-permute-start(bf16[256,1024]{1,0:T(8,128)(2,1)} %constant_dynamic-update-slice_fusion), channel_id=1, source_target_pairs={{0,40},{1,137},{2,202},{3,59},{4,236},{5,189},{6,30},{7,79},{256,2... | collective-permute-start | bytes 1572872 | tf_op jit(solution)/shard_map/ppermute | solution.py:236
  111.6 60.1 %collective-permute-start.14 = (bf16[256,1024]{1,0:T(8,128)(2,1)}, bf16[256,1024]{1,0:T(8,128)(2,1)}, u32[]{:S(2)}, u32[]{:S(2)}) collective-permute-start(bf16[256,1024]{1,0:T(8,128)(2,1)} %constant_dynamic-update-slice_fusion), channel_id=1, source_target_pairs={{8,0},{16,8},{24,16},{32,24},{40,32},{48,40},{56,48},{64,56},{72,6... | collective-permute-start | bytes 1572872 | tf_op jit(solution)/shard_map/ppermute | solution.py:226
  124.1 49.5 %collective-permute-start.13 = (bf16[256,1024]{1,0:T(8,128)(2,1)}, bf16[256,1024]{1,0:T(8,128)(2,1)}, u32[]{:S(2)}, u32[]{:S(2)}) collective-permute-start(bf16[256,1024]{1,0:T(8,128)(2,1)} %collective-permute-done.12), channel_id=1, source_target_pairs={{40,504},{137,505},{202,506},{59,507},{236,508},{189,509},{30,510}... | collective-permute-start | bytes 1572872 | tf_op jit(solution)/shard_map/ppermute | solution.py:236
  125.6 19.1 %collective-permute-start.15 = (bf16[2,200,256]{2,1,0:T(8,128)(2,1)}, bf16[2,200,256]{2,1,0:T(8,128)(2,1)S(1)}, u32[]{:S(2)}, u32[]{:S(2)}) collective-permute-start(bf16[2,200,256]{2,1,0:T(8,128)(2,1)} %get-tuple-element.53), channel_id=1, source_target_pairs={{0,4},{1,5},{2,6},{3,7},{4,0},{5,1},{6,2},{7,3},{8,12},{9,13},{10,... | collective-permute-start | bytes 614408 | tf_op jit(solution)/shard_map/ppermute | solution.py:32
  135.3 27.9 %collective-permute-start.16 = (bf16[2,200,256]{2,1,0:T(8,128)(2,1)}, bf16[2,200,256]{2,1,0:T(8,128)(2,1)S(1)}, u32[]{:S(2)}, u32[]{:S(2)}) collective-permute-start(bf16[2,200,256]{2,1,0:T(8,128)(2,1)} %get-tuple-element.55), channel_id=1, source_target_pairs={{0,7},{1,0},{2,1},{3,2},{4,3},{5,4},{6,5},{7,6},{8,15},{9,8},{10,9... | collective-permute-start | bytes 614408 | tf_op jit(solution)/shard_map/ppermute | solution.py:32
  142.8 22.5 %collective-permute-start.19 = (bf16[2,200,256]{2,1,0:T(8,128)(2,1)S(1)}, bf16[2,200,256]{2,1,0:T(8,128)(2,1)S(1)}, u32[]{:S(2)}, u32[]{:S(2)}) collective-permute-start(bf16[2,200,256]{2,1,0:T(8,128)(2,1)S(1)} %get-tuple-element.60), channel_id=1, source_target_pairs={{0,1},{1,2},{2,3},{3,4},{4,5},{5,6},{6,7},{7,0},{8,9},{9,10},{10,1... | collective-permute-start | bytes 614408 | tf_op jit(solution)/shard_map/ppermute | solution.py:32
  144.7 30.1 %collective-permute-start.17 = (bf16[2,200,256]{2,1,0:T(8,128)(2,1)S(1)}, bf16[2,200,256]{2,1,0:T(8,128)(2,1)S(1)}, u32[]{:S(2)}, u32[]{:S(2)}) collective-permute-start(bf16[2,200,256]{2,1,0:T(8,128)(2,1)S(1)} %get-tuple-element.56), channel_id=1, source_target_pairs={{0,6},{1,7},{2,0},{3,1},{4,2},{5,3},{6,4},{7,5},{8,14},{9,15},{10,... | collective-permute-start | bytes 614408 | tf_op jit(solution)/shard_map/ppermute | solution.py:32
  163.3 13.8 %collective-permute-start.21 = (bf16[2,200,256]{2,1,0:T(8,128)(2,1)S(1)}, bf16[2,200,256]{2,1,0:T(8,128)(2,1)S(1)}, u32[]{:S(2)}, u32[]{:S(2)}) collective-permute-start(bf16[2,200,256]{2,1,0:T(8,128)(2,1)S(1)} %get-tuple-element.62), channel_id=1, source_target_pairs={{0,2},{1,3},{2,4},{3,5},{4,6},{5,7},{6,0},{7,1},{8,10},{9,11},{10,... | collective-permute-start | bytes 614408 | tf_op jit(solution)/shard_map/ppermute | solution.py:32
  165.2 28.4 %collective-permute-start.18 = (bf16[2,200,256]{2,1,0:T(8,128)(2,1)S(1)}, bf16[2,200,256]{2,1,0:T(8,128)(2,1)S(1)}, u32[]{:S(2)}, u32[]{:S(2)}) collective-permute-start(bf16[2,200,256]{2,1,0:T(8,128)(2,1)S(1)} %get-tuple-element.58), channel_id=1, source_target_pairs={{0,5},{1,6},{2,7},{3,0},{4,1},{5,2},{6,3},{7,4},{8,13},{9,14},{10,... | collective-permute-start | bytes 614408 | tf_op jit(solution)/shard_map/ppermute | solution.py:32
  171.7 37.2 %collective-permute-start.20 = (bf16[2,200,256]{2,1,0:T(8,128)(2,1)S(1)}, bf16[2,200,256]{2,1,0:T(8,128)(2,1)S(1)}, u32[]{:S(2)}, u32[]{:S(2)}) collective-permute-start(bf16[2,200,256]{2,1,0:T(8,128)(2,1)S(1)} %get-tuple-element.61), channel_id=1, source_target_pairs={{0,3},{1,4},{2,5},{3,6},{4,7},{5,0},{6,1},{7,2},{8,11},{9,12},{10,... | collective-permute-start | bytes 614408 | tf_op jit(solution)/shard_map/ppermute | solution.py:32

commit v6 on v5

--- a/solution.py
+++ b/solution.py
@@ -268,7 +268,7 @@
         functools.partial(split_kernel, "tensor"), "split", [((2 * tok, cols), bf16)] + [piece_shape] * n,
         (queries, output_gradient, key_value_store),
     )
-    order = [1, n - 1, n // 2] + [k for d in range(2, n // 2) for k in (d, n - d)] + [0]
+    order = [1, n - 1, 2, n - 2, n // 2] + [k for d in range(3, n // 2) for k in (d, n - d)] + [0]
     kv, both = exchange(sends, order, 1, both, 1)
     q_back, g_back = both[:tok], both[tok:]
 

time: 214 us -> 224 us (1.047)
  the two profiles are of different devices: /device:TPU:1 before, /device:TPU:32 now
where the time goes in v6:
time: 224 us; the launch traced here: 223 us
  starting transfers between devices  142 us (63%)
  waiting for transfers between devices  50.7 us (23%)
  Pallas kernels  19.4 us (9%)
  local copies, waits for them, and re-layouts  5.83 us (3%)
  other arithmetic  3.98 us (2%)
    ppermute x16, starting transfers between devices, shift(): return lax.ppermute(value, axis, pairs)  132 us
    ppermute x16, waiting for transfers between devices, shift(): return lax.ppermute(value, axis, pairs)  45.8 us
    pallas_call x5, Pallas kernels, call(): pl.pallas_call(kernel, out_shape=[jax.ShapeDtypeStruct(*o) for o in outs]...  19.4 us
    ppermute x4, starting transfers between devices, send(): lax.ppermute(part, ('dp', 'tensor'), [(d * n + t, e * n + t) for d, e, t...  6.42 us
    ppermute x4, waiting for transfers between devices, send(): lax.ppermute(part, ('dp', 'tensor'), [(d * n + t, e * n + t) for d, e, t...  4.93 us
  transfers between devices with their start and end apart: 22, of which 5 were waited for; matrix products, arithmetic and copies ran while one was open for 3% of the time, Pallas kernels for 2%

profile of v6, /device:TPU:32, one launch (start us, length us, event | category | flops | bytes accessed | tf_op | source)
XLA Modules:
  0.0 223.5 jit_solution(6215348704882578710)
XLA Ops:
  0.6 0.0 copy-start
  0.6 0.9 copy-done
  1.6 0.9 copy-done.2
  2.5 1.4 copy-done.4
  4.0 0.3 split.1
  4.2 0.0 copy-start.1
  4.2 1.6 collective-permute-start
  5.8 2.5 %collective-permute-start.2 = (bf16[256,1024]{1,0:T(8,128)(2,1)S(1)}, bf16[256,1024]{1,0:T(8,128)(2,1)}, u32[]{:S(2)}, u32[]{:S(2)}) collective-permute-start(bf16[256,1024]{1,0:T(8,128)(2,1)S(1)} %get-tuple-element.33), channel_id=1, source_target_pairs={{0,8},{8,16},{16,24},{24,32},{32,40},{40,48},{48,56},{56,64},{64,7... | collective-permute-start | bytes 1572872 | tf_op jit(solution)/shard_map/ppermute | solution.py:226
  8.4 3.8 %collective-permute-start.3 = (bf16[2,200,256]{2,1,0:T(8,128)(2,1)S(1)}, bf16[2,200,256]{2,1,0:T(8,128)(2,1)S(1)}, u32[]{:S(2)}, u32[]{:S(2)}) collective-permute-start(bf16[2,200,256]{2,1,0:T(8,128)(2,1)S(1)} %get-tuple-element.35), channel_id=1, source_target_pairs={{0,1},{1,2},{2,3},{3,4},{4,5},{5,6},{6,7},{7,0},{8,9},{9,10},{10,1... | collective-permute-start | bytes 614408 | tf_op jit(solution)/shard_map/ppermute | solution.py:32
  12.2 5.0 %collective-permute-start.5 = (bf16[2,200,256]{2,1,0:T(8,128)(2,1)S(1)}, bf16[2,200,256]{2,1,0:T(8,128)(2,1)S(1)}, u32[]{:S(2)}, u32[]{:S(2)}) collective-permute-start(bf16[2,200,256]{2,1,0:T(8,128)(2,1)S(1)} %get-tuple-element.38), channel_id=1, source_target_pairs={{0,7},{1,0},{2,1},{3,2},{4,3},{5,4},{6,5},{7,6},{8,15},{9,8},{10,9... | collective-permute-start | bytes 614408 | tf_op jit(solution)/shard_map/ppermute | solution.py:32
  17.3 3.3 %collective-permute-start.7 = (bf16[2,200,256]{2,1,0:T(8,128)(2,1)S(1)}, bf16[2,200,256]{2,1,0:T(8,128)(2,1)S(1)}, u32[]{:S(2)}, u32[]{:S(2)}) collective-permute-start(bf16[2,200,256]{2,1,0:T(8,128)(2,1)S(1)} %get-tuple-element.41), channel_id=1, source_target_pairs={{0,2},{1,3},{2,4},{3,5},{4,6},{5,7},{6,0},{7,1},{8,10},{9,11},{10,... | collective-permute-start | bytes 614408 | tf_op jit(solution)/shard_map/ppermute | solution.py:32
  20.6 0.6 fusion.5
  21.2 0.2 dynamic-slice_reduce_fusion
  21.4 1.3 iota_compare_fusion
  22.7 0.0 collective-permute-done
  22.7 1.3 collective-permute-start.1
  24.0 0.2 fusion.1
  24.2 0.2 fusion.3
  24.4 0.1 copy.11
  24.5 0.1 copy.12
  24.6 0.1 pad_add_fusion.refs_0_
  24.7 0.0 collective-permute-done.3.refs_4_.refs_8_
  24.7 8.3 %collective-permute-start.8 = (bf16[2,200,256]{2,1,0:T(8,128)(2,1)S(1)}, bf16[2,200,256]{2,1,0:T(8,128)(2,1)S(1)}, u32[]{:S(2)}, u32[]{:S(2)}) collective-permute-start(bf16[2,200,256]{2,1,0:T(8,128)(2,1)S(1)} %get-tuple-element.43), channel_id=1, source_target_pairs={{0,6},{1,7},{2,0},{3,1},{4,2},{5,3},{6,4},{7,5},{8,14},{9,15},{10,... | collective-permute-start | bytes 614408 | tf_op jit(solution)/shard_map/ppermute | solution.py:32
  33.0 0.0 collective-permute-done.5.refs_5_.refs_9_
  33.0 2.5 %collective-permute-start.9 = (bf16[2,200,256]{2,1,0:T(8,128)(2,1)S(1)}, bf16[2,200,256]{2,1,0:T(8,128)(2,1)S(1)}, u32[]{:S(2)}, u32[]{:S(2)}) collective-permute-start(bf16[2,200,256]{2,1,0:T(8,128)(2,1)S(1)} %get-tuple-element.44), channel_id=1, source_target_pairs={{0,4},{1,5},{2,6},{3,7},{4,0},{5,1},{6,2},{7,3},{8,12},{9,13},{10,... | collective-permute-start | bytes 614408 | tf_op jit(solution)/shard_map/ppermute | solution.py:32
  35.5 0.0 collective-permute-done.7.refs_6_.refs_10_
  35.5 14.4 %collective-permute-start.4 = (bf16[2,200,256]{2,1,0:T(8,128)(2,1)S(1)}, bf16[2,200,256]{2,1,0:T(8,128)(2,1)S(1)}, u32[]{:S(2)}, u32[]{:S(2)}) collective-permute-start(bf16[2,200,256]{2,1,0:T(8,128)(2,1)S(1)} %get-tuple-element.36), channel_id=1, source_target_pairs={{0,3},{1,4},{2,5},{3,6},{4,7},{5,0},{6,1},{7,2},{8,11},{9,12},{10,... | collective-permute-start | bytes 614408 | tf_op jit(solution)/shard_map/ppermute | solution.py:32
  49.9 0.0 collective-permute-done.2
  49.9 2.3 %collective-permute-start.6 = (bf16[2,200,256]{2,1,0:T(8,128)(2,1)S(1)}, bf16[2,200,256]{2,1,0:T(8,128)(2,1)S(1)}, u32[]{:S(2)}, u32[]{:S(2)}) collective-permute-start(bf16[2,200,256]{2,1,0:T(8,128)(2,1)S(1)} %get-tuple-element.39), channel_id=1, source_target_pairs={{0,5},{1,6},{2,7},{3,0},{4,1},{5,2},{6,3},{7,4},{8,13},{9,14},{10,... | collective-permute-start | bytes 614408 | tf_op jit(solution)/shard_map/ppermute | solution.py:32
  52.2 0.0 collective-permute-done.1
  52.2 1.1 broadcast_select_fusion.1
  53.4 0.0 copy-start.3
  53.4 0.0 collective-permute-done.8.refs_7_.refs_11_
  53.4 21.4 %collective-permute-done.9.refs_8_.refs_12_ = bf16[2,200,256]{2,1,0:T(8,128)(2,1)S(1)} collective-permute-done((bf16[2,200,256]{2,1,0:T(8,128)(2,1)S(1)}, bf16[2,200,256]{2,1,0:T(8,128)(2,1)S(1)}, u32[]{:S(2)}, u32[]{:S(2)}) %collective-permute-start.9) | collective-permute-done | bytes 204832 | tf_op jit(solution)/shard_map/ppermute | solution.py:32
  74.9 4.9 %attend.2 = (f32[2,128,1024]{2,1,0:T(8,128)S(1)}, f32[2,8,1024]{2,1,0:T(8,128)S(1)}) custom-call(s32[2,2]{1,0:T(2,128)S(1)} %pad_add_fusion.refs_0_, bf16[128,1024]{1,0:T(8,128)(2,1)S(1)} %copy-done.1, bf16[128,1024]{1,0:T(8,128)(2,1)S(1)} %get-tuple-element.70.refs_2_, bf16[2,200,256]{2,1,0:T(8,128)(2,1)S(1)} %get-tuple-element.42.refs_3_.refs_15_, ...), custom_call_target="tpu_custom_call" | custom-call | bytes 1048576 | tf_op jit(solution)/shard_map/attend/pallas_call | solution.py:205
  79.7 0.0 collective-permute-done.4.refs_5_.refs_13_
  79.7 12.5 %collective-permute-done.6.refs_6_.refs_14_ = bf16[2,200,256]{2,1,0:T(8,128)(2,1)S(1)} collective-permute-done((bf16[2,200,256]{2,1,0:T(8,128)(2,1)S(1)}, bf16[2,200,256]{2,1,0:T(8,128)(2,1)S(1)}, u32[]{:S(2)}, u32[]{:S(2)}) %collective-permute-start.6) | collective-permute-done | bytes 204832 | tf_op jit(solution)/shard_map/ppermute | solution.py:32
  92.3 2.5 %attend.3 = (f32[128,1024]{1,0:T(8,128)S(1)}, bf16[128,1024]{1,0:T(8,128)(2,1)S(1)}, f32[2,8,1024]{2,1,0:T(8,128)S(1)}) custom-call(s32[2,2]{1,0:T(2,128)S(1)} %pad_add_fusion.refs_0_, bf16[128,1024]{1,0:T(8,128)(2,1)S(1)} %copy-done.1, bf16[128,1024]{1,0:T(8,128)(2,1)S(1)} %get-tuple-element.70.refs_2_, bf16[128,1024]{1,0:T(8,128)(2,1)S(1)} %copy-done.3, ...), custom_call_target="tpu_custom_call" | custom-call | bytes 1048576 | tf_op jit(solution)/shard_map/attend/pallas_call | solution.py:205
  94.8 2.0 collective-permute-start.11
  96.7 16.7 %collective-permute-start.10 = (f32[8,1024]{1,0:T(8,128)S(1)}, f32[8,1024]{1,0:T(8,128)S(1)}, u32[]{:S(2)}, u32[]{:S(2)}) collective-permute-start(f32[8,1024]{1,0:T(8,128)S(1)} %get-tuple-element.72), channel_id=1, source_target_pairs={{0,504},{8,0},{16,8},{24,16},{32,24},{40,32},{48,40},{56,48},{64,5... | collective-permute-start | bytes 98312 | tf_op jit(solution)/shard_map/ppermute | solution.py:32
  113.5 0.7 constant_dynamic-update-slice_fusion.1
  114.2 0.0 collective-permute-done.11.refs_7_
  114.2 0.7 collective-permute-done.10.refs_6_.far
  114.9 10.2 %backward.1 = (f32[128,1024]{1,0:T(8,128)S(1)}, bf16[128,1024]{1,0:T(8,128)(2,1)S(1)}, bf16[2,200,256]{2,1,0:T(8,128)(2,1)}, bf16[2,200,256]{2,1,0:T(8,128)(2,1)...) custom-call(s32[2,2]{1,0:T(2,128)S(1)} %pad_add_fusion.refs_0_, ...), custom_call_target="tpu_custom_call" | custom-call | bytes 1048576 | tf_op jit(solution)/shard_map/backward/pallas_call | solution.py:205
  125.0 0.7 constant_dynamic-update-slice_fusion
  125.8 2.1 collective-permute-start.12
  127.8 1.3 collective-permute-start.14
  129.1 4.9 %collective-permute-done.12 = bf16[256,1024]{1,0:T(8,128)(2,1)} collective-permute-done((bf16[256,1024]{1,0:T(8,128)(2,1)}, bf16[256,1024]{1,0:T(8,128)(2,1)}, u32[]{:S(2)}, u32[]{:S(2)}) %collective-permute-start.12) | collective-permute-done | bytes 524320 | tf_op jit(solution)/shard_map/ppermute | solution.py:236
  134.0 1.5 collective-permute-start.13
  135.5 6.5 %collective-permute-start.15 = (bf16[2,200,256]{2,1,0:T(8,128)(2,1)}, bf16[2,200,256]{2,1,0:T(8,128)(2,1)S(1)}, u32[]{:S(2)}, u32[]{:S(2)}) collective-permute-start(bf16[2,200,256]{2,1,0:T(8,128)(2,1)} %get-tuple-element.53), channel_id=1, source_target_pairs={{0,6},{1,7},{2,0},{3,1},{4,2},{5,3},{6,4},{7,5},{8,14},{9,15},{10,... | collective-permute-start | bytes 614408 | tf_op jit(solution)/shard_map/ppermute | solution.py:32
  142.0 1.9 collective-permute-start.16
  143.9 6.1 %collective-permute-start.19 = (bf16[2,200,256]{2,1,0:T(8,128)(2,1)S(1)}, bf16[2,200,256]{2,1,0:T(8,128)(2,1)S(1)}, u32[]{:S(2)}, u32[]{:S(2)}) collective-permute-start(bf16[2,200,256]{2,1,0:T(8,128)(2,1)S(1)} %get-tuple-element.60), channel_id=1, source_target_pairs={{0,1},{1,2},{2,3},{3,4},{4,5},{5,6},{6,7},{7,0},{8,9},{9,10},{10,1... | collective-permute-start | bytes 614408 | tf_op jit(solution)/shard_map/ppermute | solution.py:32
  150.0 0.0 collective-permute-done.15.refs_2_
  150.0 6.9 %collective-permute-start.18 = (bf16[2,200,256]{2,1,0:T(8,128)(2,1)S(1)}, bf16[2,200,256]{2,1,0:T(8,128)(2,1)S(1)}, u32[]{:S(2)}, u32[]{:S(2)}) collective-permute-start(bf16[2,200,256]{2,1,0:T(8,128)(2,1)S(1)} %get-tuple-element.58), channel_id=1, source_target_pairs={{0,4},{1,5},{2,6},{3,7},{4,0},{5,1},{6,2},{7,3},{8,12},{9,13},{10,... | collective-permute-start | bytes 614408 | tf_op jit(solution)/shard_map/ppermute | solution.py:32
  157.0 0.0 collective-permute-done.16.refs_1_
  157.0 43.7 %collective-permute-start.21 = (bf16[2,200,256]{2,1,0:T(8,128)(2,1)S(1)}, bf16[2,200,256]{2,1,0:T(8,128)(2,1)S(1)}, u32[]{:S(2)}, u32[]{:S(2)}) collective-permute-start(bf16[2,200,256]{2,1,0:T(8,128)(2,1)S(1)} %get-tuple-element.62), channel_id=1, source_target_pairs={{0,2},{1,3},{2,4},{3,5},{4,6},{5,7},{6,0},{7,1},{8,10},{9,11},{10,... | collective-permute-start | bytes 614408 | tf_op jit(solution)/shard_map/ppermute | solution.py:32
  200.7 1.9 collective-permute-start.17
  202.6 6.9 %collective-permute-start.20 = (bf16[2,200,256]{2,1,0:T(8,128)(2,1)S(1)}, bf16[2,200,256]{2,1,0:T(8,128)(2,1)S(1)}, u32[]{:S(2)}, u32[]{:S(2)}) collective-permute-start(bf16[2,200,256]{2,1,0:T(8,128)(2,1)S(1)} %get-tuple-element.61), channel_id=1, source_target_pairs={{0,3},{1,4},{2,5},{3,6},{4,7},{5,0},{6,1},{7,2},{8,11},{9,12},{10,... | collective-permute-start | bytes 614408 | tf_op jit(solution)/shard_map/ppermute | solution.py:32
  209.6 0.0 collective-permute-done.13
  209.6 1.1 broadcast_select_fusion.both
  210.7 0.0 collective-permute-done.21.refs_6_
  210.7 11.1 %collective-permute-done.17.refs_3_ = bf16[2,200,256]{2,1,0:T(8,128)(2,1)S(1)} collective-permute-done((bf16[2,200,256]{2,1,0:T(8,128)(2,1)S(1)}, bf16[2,200,256]{2,1,0:T(8,128)(2,1)S(1)}, u32[]{:S(2)}, u32[]{:S(2)}) %collective-permute-start.17) | collective-permute-done | bytes 204832 | tf_op jit(solution)/shard_map/ppermute | solution.py:32
  221.8 0.0 collective-permute-done.20.refs_5_
  221.8 1.6 finish.1
  (17 shorter events, 0.1 us)
Async XLA Ops:
  0.6 1.0 copy-start
  1.6 0.9 copy-start.2
  2.5 1.4 copy-start.4
  4.0 16.6 %copy-start.7 = (s32[64]{0:T(128)S(1)}, s32[64]{0:T(128)}, u32[]{:S(2)}) copy-start(s32[64]{0:T(128)} %param.10) | copy-start | bytes 772
  4.0 17.2 %copy-start.5 = (s32[64,4]{0,1:T(4,128)S(1)}, s32[64,4]{0,1:T(4,128)}, u32[]{:S(2)}) copy-start(s32[64,4]{0,1:T(4,128)} %param.11) | copy-start | bytes 3076
  4.0 17.2 %copy-start.6 = (s32[64,4]{0,1:T(4,128)S(1)}, s32[64,4]{0,1:T(4,128)}, u32[]{:S(2)}) copy-start(s32[64,4]{0,1:T(4,128)} %param.9) | copy-start | bytes 3076
  4.2 70.6 %copy-start.1 = (bf16[128,1024]{1,0:T(8,128)(2,1)S(1)}, bf16[128,1024]{1,0:T(8,128)(2,1)}, u32[]{:S(2)}) copy-start(bf16[128,1024]{1,0:T(8,128)(2,1)} %refs_1_.5) | copy-start | bytes 786436
  4.2 18.5 %collective-permute-start = (bf16[256,1024]{1,0:T(8,128)(2,1)S(1)}, bf16[256,1024]{1,0:T(8,128)(2,1)}, u32[]{:S(2)}, u32[]{:S(2)}) collective-permute-start(bf16[256,1024]{1,0:T(8,128)(2,1)S(1)} %get-tuple-element.33), channel_id=1, source_target_pairs={{248,40},{249,137},{250,202},{251,59},{252,236},{253,189},{254,30}... | collective-permute-start | bytes 1572872 | tf_op jit(solution)/shard_map/ppermute | solution.py:236
  5.8 44.1 %collective-permute-start.2 = (bf16[256,1024]{1,0:T(8,128)(2,1)S(1)}, bf16[256,1024]{1,0:T(8,128)(2,1)}, u32[]{:S(2)}, u32[]{:S(2)}) collective-permute-start(bf16[256,1024]{1,0:T(8,128)(2,1)S(1)} %get-tuple-element.33), channel_id=1, source_target_pairs={{0,8},{8,16},{16,24},{24,32},{32,40},{40,48},{48,56},{56,64},{64,7... | collective-permute-start | bytes 1572872 | tf_op jit(solution)/shard_map/ppermute | solution.py:226
  8.4 16.3 %collective-permute-start.3 = (bf16[2,200,256]{2,1,0:T(8,128)(2,1)S(1)}, bf16[2,200,256]{2,1,0:T(8,128)(2,1)S(1)}, u32[]{:S(2)}, u32[]{:S(2)}) collective-permute-start(bf16[2,200,256]{2,1,0:T(8,128)(2,1)S(1)} %get-tuple-element.35), channel_id=1, source_target_pairs={{0,1},{1,2},{2,3},{3,4},{4,5},{5,6},{6,7},{7,0},{8,9},{9,10},{10,1... | collective-permute-start | bytes 614408 | tf_op jit(solution)/shard_map/ppermute | solution.py:32
  12.2 20.8 %collective-permute-start.5 = (bf16[2,200,256]{2,1,0:T(8,128)(2,1)S(1)}, bf16[2,200,256]{2,1,0:T(8,128)(2,1)S(1)}, u32[]{:S(2)}, u32[]{:S(2)}) collective-permute-start(bf16[2,200,256]{2,1,0:T(8,128)(2,1)S(1)} %get-tuple-element.38), channel_id=1, source_target_pairs={{0,7},{1,0},{2,1},{3,2},{4,3},{5,4},{6,5},{7,6},{8,15},{9,8},{10,9... | collective-permute-start | bytes 614408 | tf_op jit(solution)/shard_map/ppermute | solution.py:32
  17.3 18.2 %collective-permute-start.7 = (bf16[2,200,256]{2,1,0:T(8,128)(2,1)S(1)}, bf16[2,200,256]{2,1,0:T(8,128)(2,1)S(1)}, u32[]{:S(2)}, u32[]{:S(2)}) collective-permute-start(bf16[2,200,256]{2,1,0:T(8,128)(2,1)S(1)} %get-tuple-element.41), channel_id=1, source_target_pairs={{0,2},{1,3},{2,4},{3,5},{4,6},{5,7},{6,0},{7,1},{8,10},{9,11},{10,... | collective-permute-start | bytes 614408 | tf_op jit(solution)/shard_map/ppermute | solution.py:32
  22.7 29.5 %collective-permute-start.1 = (bf16[256,1024]{1,0:T(8,128)(2,1)}, bf16[256,1024]{1,0:T(8,128)(2,1)}, u32[]{:S(2)}, u32[]{:S(2)}) collective-permute-start(bf16[256,1024]{1,0:T(8,128)(2,1)} %collective-permute-done), channel_id=1, source_target_pairs={{40,256},{137,257},{202,258},{59,259},{236,260},{189,261},{30,262}... | collective-permute-start | bytes 1572872 | tf_op jit(solution)/shard_map/ppermute | solution.py:236
  24.7 28.7 %collective-permute-start.8 = (bf16[2,200,256]{2,1,0:T(8,128)(2,1)S(1)}, bf16[2,200,256]{2,1,0:T(8,128)(2,1)S(1)}, u32[]{:S(2)}, u32[]{:S(2)}) collective-permute-start(bf16[2,200,256]{2,1,0:T(8,128)(2,1)S(1)} %get-tuple-element.43), channel_id=1, source_target_pairs={{0,6},{1,7},{2,0},{3,1},{4,2},{5,3},{6,4},{7,5},{8,14},{9,15},{10,... | collective-permute-start | bytes 614408 | tf_op jit(solution)/shard_map/ppermute | solution.py:32
  33.0 41.9 %collective-permute-start.9 = (bf16[2,200,256]{2,1,0:T(8,128)(2,1)S(1)}, bf16[2,200,256]{2,1,0:T(8,128)(2,1)S(1)}, u32[]{:S(2)}, u32[]{:S(2)}) collective-permute-start(bf16[2,200,256]{2,1,0:T(8,128)(2,1)S(1)} %get-tuple-element.44), channel_id=1, source_target_pairs={{0,4},{1,5},{2,6},{3,7},{4,0},{5,1},{6,2},{7,3},{8,12},{9,13},{10,... | collective-permute-start | bytes 614408 | tf_op jit(solution)/shard_map/ppermute | solution.py:32
  35.5 44.2 %collective-permute-start.4 = (bf16[2,200,256]{2,1,0:T(8,128)(2,1)S(1)}, bf16[2,200,256]{2,1,0:T(8,128)(2,1)S(1)}, u32[]{:S(2)}, u32[]{:S(2)}) collective-permute-start(bf16[2,200,256]{2,1,0:T(8,128)(2,1)S(1)} %get-tuple-element.36), channel_id=1, source_target_pairs={{0,3},{1,4},{2,5},{3,6},{4,7},{5,0},{6,1},{7,2},{8,11},{9,12},{10,... | collective-permute-start | bytes 614408 | tf_op jit(solution)/shard_map/ppermute | solution.py:32
  49.9 42.4 %collective-permute-start.6 = (bf16[2,200,256]{2,1,0:T(8,128)(2,1)S(1)}, bf16[2,200,256]{2,1,0:T(8,128)(2,1)S(1)}, u32[]{:S(2)}, u32[]{:S(2)}) collective-permute-start(bf16[2,200,256]{2,1,0:T(8,128)(2,1)S(1)} %get-tuple-element.39), channel_id=1, source_target_pairs={{0,5},{1,6},{2,7},{3,0},{4,1},{5,2},{6,3},{7,4},{8,13},{9,14},{10,... | collective-permute-start | bytes 614408 | tf_op jit(solution)/shard_map/ppermute | solution.py:32
  53.4 38.9 %copy-start.3 = (bf16[128,1024]{1,0:T(8,128)(2,1)S(1)}, bf16[128,1024]{1,0:T(8,128)(2,1)}, u32[]{:S(2)}) copy-start(bf16[128,1024]{1,0:T(8,128)(2,1)} %refs_3_.3) | copy-start | bytes 786436
  94.8 19.4 %collective-permute-start.11 = (f32[8,1024]{1,0:T(8,128)S(1)}, f32[8,1024]{1,0:T(8,128)S(1)}, u32[]{:S(2)}, u32[]{:S(2)}) collective-permute-start(f32[8,1024]{1,0:T(8,128)S(1)} %get-tuple-element.71), channel_id=1, source_target_pairs={{0,8},{8,16},{16,24},{24,32},{32,40},{40,48},{48,56},{56,64},{64,7... | collective-permute-start | bytes 98312 | tf_op jit(solution)/shard_map/ppermute | solution.py:32
  96.7 18.1 %collective-permute-start.10 = (f32[8,1024]{1,0:T(8,128)S(1)}, f32[8,1024]{1,0:T(8,128)S(1)}, u32[]{:S(2)}, u32[]{:S(2)}) collective-permute-start(f32[8,1024]{1,0:T(8,128)S(1)} %get-tuple-element.72), channel_id=1, source_target_pairs={{0,504},{8,0},{16,8},{24,16},{32,24},{40,32},{48,40},{56,48},{64,5... | collective-permute-start | bytes 98312 | tf_op jit(solution)/shard_map/ppermute | solution.py:32
  125.8 8.3 %collective-permute-start.12 = (bf16[256,1024]{1,0:T(8,128)(2,1)}, bf16[256,1024]{1,0:T(8,128)(2,1)}, u32[]{:S(2)}, u32[]{:S(2)}) collective-permute-start(bf16[256,1024]{1,0:T(8,128)(2,1)} %constant_dynamic-update-slice_fusion), channel_id=1, source_target_pairs={{0,40},{1,137},{2,202},{3,59},{4,236},{5,189},{6,30},{7,79},{256,2... | collective-permute-start | bytes 1572872 | tf_op jit(solution)/shard_map/ppermute | solution.py:236
  127.8 74.8 %collective-permute-start.14 = (bf16[256,1024]{1,0:T(8,128)(2,1)}, bf16[256,1024]{1,0:T(8,128)(2,1)}, u32[]{:S(2)}, u32[]{:S(2)}) collective-permute-start(bf16[256,1024]{1,0:T(8,128)(2,1)} %constant_dynamic-update-slice_fusion), channel_id=1, source_target_pairs={{8,0},{16,8},{24,16},{32,24},{40,32},{48,40},{56,48},{64,56},{72,6... | collective-permute-start | bytes 1572872 | tf_op jit(solution)/shard_map/ppermute | solution.py:226
  134.0 75.5 %collective-permute-start.13 = (bf16[256,1024]{1,0:T(8,128)(2,1)}, bf16[256,1024]{1,0:T(8,128)(2,1)}, u32[]{:S(2)}, u32[]{:S(2)}) collective-permute-start(bf16[256,1024]{1,0:T(8,128)(2,1)} %collective-permute-done.12), channel_id=1, source_target_pairs={{40,504},{137,505},{202,506},{59,507},{236,508},{189,509},{30,510}... | collective-permute-start | bytes 1572872 | tf_op jit(solution)/shard_map/ppermute | solution.py:236
  135.5 14.5 %collective-permute-start.15 = (bf16[2,200,256]{2,1,0:T(8,128)(2,1)}, bf16[2,200,256]{2,1,0:T(8,128)(2,1)S(1)}, u32[]{:S(2)}, u32[]{:S(2)}) collective-permute-start(bf16[2,200,256]{2,1,0:T(8,128)(2,1)} %get-tuple-element.53), channel_id=1, source_target_pairs={{0,6},{1,7},{2,0},{3,1},{4,2},{5,3},{6,4},{7,5},{8,14},{9,15},{10,... | collective-permute-start | bytes 614408 | tf_op jit(solution)/shard_map/ppermute | solution.py:32
  142.0 15.0 %collective-permute-start.16 = (bf16[2,200,256]{2,1,0:T(8,128)(2,1)}, bf16[2,200,256]{2,1,0:T(8,128)(2,1)S(1)}, u32[]{:S(2)}, u32[]{:S(2)}) collective-permute-start(bf16[2,200,256]{2,1,0:T(8,128)(2,1)} %get-tuple-element.55), channel_id=1, source_target_pairs={{0,7},{1,0},{2,1},{3,2},{4,3},{5,4},{6,5},{7,6},{8,15},{9,8},{10,9... | collective-permute-start | bytes 614408 | tf_op jit(solution)/shard_map/ppermute | solution.py:32
  143.9 56.8 %collective-permute-start.19 = (bf16[2,200,256]{2,1,0:T(8,128)(2,1)S(1)}, bf16[2,200,256]{2,1,0:T(8,128)(2,1)S(1)}, u32[]{:S(2)}, u32[]{:S(2)}) collective-permute-start(bf16[2,200,256]{2,1,0:T(8,128)(2,1)S(1)} %get-tuple-element.60), channel_id=1, source_target_pairs={{0,1},{1,2},{2,3},{3,4},{4,5},{5,6},{6,7},{7,0},{8,9},{9,10},{10,1... | collective-permute-start | bytes 614408 | tf_op jit(solution)/shard_map/ppermute | solution.py:32
  150.0 60.7 %collective-permute-start.18 = (bf16[2,200,256]{2,1,0:T(8,128)(2,1)S(1)}, bf16[2,200,256]{2,1,0:T(8,128)(2,1)S(1)}, u32[]{:S(2)}, u32[]{:S(2)}) collective-permute-start(bf16[2,200,256]{2,1,0:T(8,128)(2,1)S(1)} %get-tuple-element.58), channel_id=1, source_target_pairs={{0,4},{1,5},{2,6},{3,7},{4,0},{5,1},{6,2},{7,3},{8,12},{9,13},{10,... | collective-permute-start | bytes 614408 | tf_op jit(solution)/shard_map/ppermute | solution.py:32
  157.0 53.7 %collective-permute-start.21 = (bf16[2,200,256]{2,1,0:T(8,128)(2,1)S(1)}, bf16[2,200,256]{2,1,0:T(8,128)(2,1)S(1)}, u32[]{:S(2)}, u32[]{:S(2)}) collective-permute-start(bf16[2,200,256]{2,1,0:T(8,128)(2,1)S(1)} %get-tuple-element.62), channel_id=1, source_target_pairs={{0,2},{1,3},{2,4},{3,5},{4,6},{5,7},{6,0},{7,1},{8,10},{9,11},{10,... | collective-permute-start | bytes 614408 | tf_op jit(solution)/shard_map/ppermute | solution.py:32
  200.7 21.1 %collective-permute-start.17 = (bf16[2,200,256]{2,1,0:T(8,128)(2,1)S(1)}, bf16[2,200,256]{2,1,0:T(8,128)(2,1)S(1)}, u32[]{:S(2)}, u32[]{:S(2)}) collective-permute-start(bf16[2,200,256]{2,1,0:T(8,128)(2,1)S(1)} %get-tuple-element.57), channel_id=1, source_target_pairs={{0,5},{1,6},{2,7},{3,0},{4,1},{5,2},{6,3},{7,4},{8,13},{9,14},{10,... | collective-permute-start | bytes 614408 | tf_op jit(solution)/shard_map/ppermute | solution.py:32
  202.6 19.2 %collective-permute-start.20 = (bf16[2,200,256]{2,1,0:T(8,128)(2,1)S(1)}, bf16[2,200,256]{2,1,0:T(8,128)(2,1)S(1)}, u32[]{:S(2)}, u32[]{:S(2)}) collective-permute-start(bf16[2,200,256]{2,1,0:T(8,128)(2,1)S(1)} %get-tuple-element.61), channel_id=1, source_target_pairs={{0,3},{1,4},{2,5},{3,6},{4,7},{5,0},{6,1},{7,2},{8,11},{9,12},{10,... | collective-permute-start | bytes 614408 | tf_op jit(solution)/shard_map/ppermute | solution.py:32
